TPU v7x, 32 devices: a whole 2x2x4 slice. The times are simulated.
32 devices in a mesh: space: 16 (over z, y, x), mp: 2 (over core).
Axes of the slice: x: 2, y: 2, z: 4, core: 2. Of those that a mesh axis runs over, the one named last changes fastest.
Arguments:
- points: bfloat16 [32768, 512], P('space'), may hold values from -40 to 40
- curve_rank: int32 [32768], P('space'), may hold values from 0 to 32767, as said below
- patch_counts: int32 [16, 4], P('space'), may hold values from 1 to 1024, 2048 in all within a row
- norm_gain_attn: float32 [512], replicated, may hold values from 0.1 to 1.9
- w_qkv: bfloat16 [3, 512, 512], P(None, None, 'mp'), may hold values from -1.5 to 1.5
- w_out: bfloat16 [512, 512], P('mp'), may hold values from -0.75 to 0.75
- norm_gain_mlp: float32 [512], replicated, may hold values from 0.1 to 1.9
- w_fc1: bfloat16 [512, 2048], P(None, 'mp'), may hold values from -0.25 to 0.25
- w_fc2: bfloat16 [2048, 512], P('mp'), may hold values from -0.1875 to 0.1875
Outputs:
- layer_out: bfloat16 [32768, 512], P('space')
Inputs may be any that keep to these rules, and one draw needn't show every extreme that they name: curve_rank is a permutation; the points of shard a take exactly the positions b * 2048 + a * 128 + m for every owner b and every m below 128. `patch_counts`: each row sums to 2048.
All inputs are finite; a program needn't handle non-finite values.
Results may differ from a plain program's by a relative error of at most 0.0075.
Values may be sent and summed in bfloat16 or wider, within the bound.
No kernel may reach another device: no remote copies, remote signals or barrier semaphores. Data moves between devices by JAX's collectives and lax.ppermute only.
A program may use at most 128 MiB of HBM per device.

v0:
```python
import functools
import math

import jax
import jax.numpy as jnp
from jax import lax
from jax.experimental import pallas as pl
from jax.experimental.pallas import tpu as pltpu
from jax.sharding import PartitionSpec as P

HDIM = 64
LANES = 128
ROWS = 256
EPSILON = 1e-06
FAR = 1e30
SEND_BYTES = 58 * 1024 * 1024
VMEM_BYTES = 30 * 1024 * 1024

f32 = jnp.float32
bf16 = jnp.bfloat16


def normalise(values, gain_row):
    average = jnp.mean(values, axis=-1, keepdims=True)
    centred = values - average
    second = jnp.mean(centred * centred, axis=-1, keepdims=True)
    return (centred * lax.rsqrt(second + EPSILON) * gain_row).astype(bf16)


def dot(left, right):
    return jnp.dot(left, right, preferred_element_type=f32)


def split_rank(rank, length):
    if length & (length - 1) == 0:
        return rank >> (length.bit_length() - 1), rank & (length - 1)
    return rank // length, rank % length


def slots(rank, length, shards):
    cell = length // shards
    owner, within = split_rank(rank, length)
    return owner * cell + within - lax.axis_index("space") * cell


def send_kernel(shards, rank_hbm, gain_hbm, points_hbm, out_ref, rank_ref, gain_ref, points_ref, half_ref, small, large):
    length, features = points_ref.shape
    half = features // 2
    core = lax.axis_index("mp")
    blocks = length // ROWS
    rows_of = [slice(i * ROWS, (i + 1) * ROWS) for i in range(blocks)]
    gain_copy = pltpu.make_async_copy(gain_hbm, gain_ref, small.at[0])
    rank_copy = pltpu.make_async_copy(rank_hbm, rank_ref, small.at[1])
    copies = [
        pltpu.make_async_copy(points_hbm.at[rows], points_ref.at[rows], large.at[i])
        for i, rows in enumerate(rows_of)
    ]
    gain_copy.start()
    for copy in copies:
        copy.start()
    rank_copy.start()
    gain_copy.wait()
    for copy, rows in zip(copies, rows_of):
        copy.wait()
        normed = normalise(points_ref[rows, :].astype(f32), gain_ref[...])
        half_ref[rows, :] = jnp.where(core == 0, normed[:, :half], normed[:, half:])
    rank_copy.wait()
    slot = slots(rank_ref[...], length, shards)

    def order_block(i, carry):
        start = pl.multiple_of(i * ROWS, ROWS)
        place = lax.broadcasted_iota(jnp.int32, (ROWS, length), 0) + start
        pick = (place == slot).astype(f32).astype(bf16)
        out_ref[pl.ds(start, ROWS), :] = dot(pick, half_ref[...]).astype(bf16)
        return carry

    lax.fori_loop(0, blocks, order_block, 0)


def order_for_owners(points, rank_row, gain_row, shards):
    length, features = points.shape
    anywhere = pl.BlockSpec(memory_space=pl.ANY)
    return pl.pallas_call(
        functools.partial(send_kernel, shards),
        out_shape=jax.ShapeDtypeStruct((length, features // 2), bf16),
        in_specs=[anywhere] * 3,
        out_specs=pl.BlockSpec(memory_space=pltpu.VMEM),
        scratch_shapes=[
            pltpu.VMEM((1, length), jnp.int32),
            pltpu.VMEM((1, features), f32),
            pltpu.VMEM((length, features), bf16),
            pltpu.VMEM((length, features // 2), bf16),
            pltpu.SemaphoreType.DMA((2,)),
            pltpu.SemaphoreType.DMA((length // ROWS,)),
        ],
        compiler_params=pltpu.CompilerParams(vmem_limit_bytes=SEND_BYTES),
        cost_estimate=pl.CostEstimate(
            flops=length * length * features, bytes_accessed=4 * length * features, transcendentals=0
        ),
    )(rank_row, gain_row, points)


def attend_kernel(pair, counts_ref, own_ref, other_ref, weight_ref, out_ref, w_ref, q_ref, k_ref, v_ref):
    length, half = own_ref.shape
    tiles = counts_ref.shape[1]
    core = lax.axis_index("mp")
    own_rows = pl.ds(pl.multiple_of(core * half, half), half)
    other_rows = pl.ds(pl.multiple_of((1 - core) * half, half), half)
    scale = math.log2(math.e) / math.sqrt(HDIM)

    starts = [jnp.int32(0)]
    for t in range(tiles):
        starts.append(starts[-1] + counts_ref[0, t])
    lane = lax.broadcasted_iota(jnp.int32, (1, LANES), 1)
    first = jnp.full((1, LANES), length, jnp.int32)
    last = jnp.zeros((1, LANES), jnp.int32)
    for t in range(tiles):
        first = jnp.where(lane == HDIM + t, starts[t], first)
        last = jnp.where(lane == HDIM + t, starts[t + 1], last)
    flags = jnp.logical_and(lane >= HDIM, lane < HDIM + tiles)
    low_lanes = lane < HDIM

    for j in range(3):
        both = weight_ref[j, :, pair * LANES : (pair + 1) * LANES].astype(f32)
        w_ref[j, :, :LANES] = jnp.where(low_lanes, both, 0.0).astype(bf16)
        odd = jnp.where(low_lanes, pltpu.roll(both, HDIM, 1), 0.0) if j < 2 else jnp.where(low_lanes, 0.0, both)
        w_ref[j, :, LANES:] = odd.astype(bf16)

    def project(i, carry):
        rows = pl.ds(pl.multiple_of(i * ROWS, ROWS), ROWS)
        mine, theirs = own_ref[rows, :], other_ref[rows, :]
        place = lax.broadcasted_iota(jnp.int32, (ROWS, LANES), 0) + i * ROWS
        inside = jnp.logical_and(place >= first, place < last)
        q_flag = jnp.where(inside, 1.0, 0.0)
        k_flag = jnp.where(jnp.logical_and(flags, jnp.logical_not(inside)), -FAR, 0.0)
        spread = [
            dot(mine, w_ref[j, own_rows, :]) + dot(theirs, w_ref[j, other_rows, :]) for j in range(3)
        ]
        for h in range(2):
            cols = slice(h * LANES, (h + 1) * LANES)
            q_ref[h, rows, :] = (spread[0][:, cols] * scale + q_flag).astype(bf16)
            k_ref[h, rows, :] = (spread[1][:, cols] + k_flag).astype(bf16)
            ones = jnp.logical_not(low_lanes) if h == 0 else low_lanes
            v_ref[h, rows, :] = (spread[2][:, cols] + jnp.where(ones, 1.0, 0.0)).astype(bf16)
        return carry

    lax.fori_loop(0, length // ROWS, project, 0)

    def raise_scores(scores):
        return jnp.exp2(scores - jnp.max(scores, axis=1, keepdims=True)).astype(bf16)

    def query_block(i, carry):
        begin = i * ROWS
        rows = pl.ds(pl.multiple_of(begin, ROWS), ROWS)
        low, high = jnp.int32(0), jnp.int32(length)
        for t in range(tiles):
            low = jnp.where(starts[t] <= begin, starts[t], low)
            end = starts[tiles - t]
            high = jnp.where(end >= begin + ROWS, end, high)
        low = (low // 16) * 16
        blocks = (high - low + ROWS - 1) // ROWS
        for n in range(1, length // ROWS + 1):

            @pl.when(blocks == n)
            def _(n=n):
                start = jnp.minimum(low, length - n * ROWS)
                keys = pl.ds(pl.multiple_of(start, 16), n * ROWS)
                scores = [
                    lax.dot_general(
                        q_ref[h, rows, :],
                        k_ref[h, keys, :],
                        (((1,), (1,)), ((), ())),
                        preferred_element_type=f32,
                    )
                    for h in range(2)
                ]
                even = dot(raise_scores(scores[0]), v_ref[0, keys, :])
                odd = dot(raise_scores(scores[1]), v_ref[1, keys, :])
                total = pltpu.roll(jnp.where(low_lanes, odd, even), HDIM, 1)
                out_ref[rows, :] = (jnp.where(low_lanes, even, odd) / total).astype(bf16)

        return carry

    lax.fori_loop(0, length // ROWS, query_block, 0)


def attend(pair, counts, own, other, w_qkv):
    length, half = own.shape
    features = w_qkv.shape[1]
    whole = pl.BlockSpec(memory_space=pltpu.VMEM)
    return pl.pallas_call(
        functools.partial(attend_kernel, pair),
        out_shape=jax.ShapeDtypeStruct((length, LANES), bf16),
        in_specs=[pl.BlockSpec(memory_space=pltpu.SMEM), whole, whole, whole],
        out_specs=whole,
        scratch_shapes=[pltpu.VMEM((3, features, 2 * LANES), bf16)] + [pltpu.VMEM((2, length, LANES), bf16)] * 3,
        compiler_params=pltpu.CompilerParams(vmem_limit_bytes=VMEM_BYTES),
        cost_estimate=pl.CostEstimate(
            flops=32 * length * length * HDIM, bytes_accessed=8 * length * half, transcendentals=2 * length * length
        ),
    )(counts, own, other, w_qkv)


def finish_kernel(
    shards,
    rank_ref,
    gain_ref,
    points_ref,
    own_a_ref,
    own_b_ref,
    other_a_ref,
    other_b_ref,
    out_own_ref,
    out_other_ref,
    fc1_own_ref,
    fc1_other_ref,
    fc2_own_ref,
    fc2_other_ref,
    done_ref,
    whole_ref,
    context_ref,
    sems,
):
    length = points_ref.shape[0]
    half_rows = done_ref.shape[0]
    base = lax.axis_index("mp") * half_rows
    half = out_own_ref.shape[0]
    for k, ref in enumerate((own_a_ref, own_b_ref, other_a_ref, other_b_ref)):
        context_ref[:, k * LANES : (k + 1) * LANES] = ref[...]

    def away(i):
        here = pl.multiple_of(i * ROWS, ROWS)
        there = pl.multiple_of(base + i * ROWS, ROWS)
        return pltpu.make_async_copy(
            done_ref.at[pl.ds(here, ROWS)], whole_ref.at[pl.ds(there, ROWS)], sems.at[i]
        )

    def block(i, carry):
        start = pl.multiple_of(base + i * ROWS, ROWS)
        rank = rank_ref[:, pl.ds(start, ROWS)]
        slot = slots(rank, length, shards)
        slot = jnp.transpose(jnp.broadcast_to(slot, (LANES, ROWS)))
        place = lax.broadcasted_iota(jnp.int32, (ROWS, LANES), 1)
        pick = jnp.concatenate(
            [
                (slot == place + k * LANES).astype(f32).astype(bf16)
                for k in range(length // LANES)
            ],
            axis=1,
        )
        context = dot(pick, context_ref[...]).astype(bf16)
        attn_out = dot(context[:, :half], out_own_ref[...]) + dot(context[:, half:], out_other_ref[...])
        middle = points_ref[pl.ds(start, ROWS), :].astype(f32) + attn_out.astype(bf16).astype(f32)
        middle = middle.astype(bf16).astype(f32)
        normed = normalise(middle, gain_ref[...])
        total = middle
        for fc1_ref, fc2_ref in ((fc1_own_ref, fc2_own_ref), (fc1_other_ref, fc2_other_ref)):
            hidden = jax.nn.gelu(dot(normed, fc1_ref[...]), approximate=True).astype(bf16)
            total = total + dot(hidden, fc2_ref[...])
        done_ref[pl.ds(pl.multiple_of(i * ROWS, ROWS), ROWS), :] = total.astype(bf16)
        away(i).start()
        return carry

    lax.fori_loop(0, half_rows // ROWS, block, 0)
    for i in range(half_rows // ROWS):
        away(i).wait()


def finish(shards, rank_row, gain_row, points, *arrays):
    length, features = points.shape
    half_rows = length // 2
    return pl.pallas_call(
        functools.partial(finish_kernel, shards),
        out_shape=(
            jax.ShapeDtypeStruct((half_rows, features), bf16),
            jax.ShapeDtypeStruct((length, features), bf16),
        ),
        out_specs=(pl.BlockSpec(memory_space=pltpu.VMEM), pl.BlockSpec(memory_space=pl.ANY)),
        scratch_shapes=[
            pltpu.VMEM((length, features), bf16),
            pltpu.SemaphoreType.DMA((half_rows // ROWS,)),
        ],
        compiler_params=pltpu.CompilerParams(vmem_limit_bytes=VMEM_BYTES),
        cost_estimate=pl.CostEstimate(
            flops=2 * half_rows * features * (length + 9 * features),
            bytes_accessed=16 * length * features,
            transcendentals=half_rows * 4 * features,
        ),
    )(rank_row, gain_row, points, *arrays)


def join_kernel(whole_in_ref, other_ref, whole_ref, sem):
    del whole_in_ref
    half_rows = other_ref.shape[0]
    start = pl.multiple_of((1 - lax.axis_index("mp")) * half_rows, half_rows)
    copy = pltpu.make_async_copy(other_ref, whole_ref.at[pl.ds(start, half_rows)], sem)
    copy.start()
    copy.wait()


def join(whole, other):
    anywhere = pl.BlockSpec(memory_space=pl.ANY)
    return pl.pallas_call(
        join_kernel,
        out_shape=jax.ShapeDtypeStruct(whole.shape, whole.dtype),
        in_specs=[anywhere, pl.BlockSpec(memory_space=pltpu.VMEM)],
        out_specs=anywhere,
        scratch_shapes=[pltpu.SemaphoreType.DMA],
        input_output_aliases={0: 0},
    )(whole, other)


def across(values):
    return lax.ppermute(values, "mp", [(0, 1), (1, 0)])


def exchange(rows, shards):
    length, columns = rows.shape
    cells = rows.reshape(shards, length // shards, columns)
    return lax.all_to_all(cells, "space", split_axis=0, concat_axis=0, tiled=True).reshape(length, columns)


def body(points, curve_rank, patch_counts, norm_gain_attn, w_qkv, w_out, norm_gain_mlp, w_fc1, w_fc2):
    shards = lax.axis_size("space")
    length, features = points.shape
    rank_row = curve_rank.reshape(1, length)
    send = order_for_owners(points, rank_row, norm_gain_attn.reshape(1, features), shards)
    own = exchange(send, shards)
    other_fc1, other_fc2, other_out = across(w_fc1), across(w_fc2), across(w_out)
    other = across(own)
    returned = [exchange(attend(pair, patch_counts, own, other, w_qkv), shards) for pair in range(w_qkv.shape[2] // LANES)]
    crossed = [across(rows) for rows in returned]
    done, whole = finish(
        shards,
        rank_row,
        norm_gain_mlp.reshape(1, features),
        points,
        *returned,
        *crossed,
        w_out,
        other_out,
        w_fc1,
        other_fc1,
        w_fc2,
        other_fc2,
    )
    return join(whole, across(done))


def solution(mesh):
    placed = (
        P("space", None),
        P("space"),
        P("space", None),
        P(),
        P(None, None, "mp"),
        P("mp", None),
        P(),
        P(None, "mp"),
        P("mp", None),
    )
    return jax.shard_map(
        body, mesh=mesh, in_specs=placed, out_specs=P("space", None), check_vma=False
    )
```

profile of v0, /device:TPU:0, one launch (start us, length us, event | category | flops | bytes accessed | tf_op | source)
XLA Modules:
  0.0 122.9 jit_solution(13377281952373540255)
XLA Ops:
  0.0 7.7 %shard_map.91 = bf16[2048,256]{1,0:T(8,128)(2,1)} custom-call(s32[1,2048]{1,0:T(1,128)} %bitcast.16, f32[1,512]{1,0:T(1,128)} %bitcast.20, bf16[2048,512]{1,0:T(8,128)(2,1)} %points_ref.1), custom_call_target="tpu_custom_call" | custom-call | flops 2147483648 | bytes 4194304 | tf_op jit(solution)/shard_map/pallas_call | solution.py:83
  7.8 0.0 copy-start.5
  7.8 34.8 %all_to_all.15 = bf16[16,128,256]{2,1,0:T(8,128)(2,1)S(1)} all-to-all(bf16[16,128,256]{2,1,0:T(8,128)(2,1)} %bitcast.19), channel_id=1, replica_groups=mesh['space'=16,'mp'=2] {'space'}, dimensions={0} | all-to-all | bytes 2097152 | tf_op jit(solution)/shard_map/all_to_all | solution.py:320
  42.6 2.7 %collective-permute-done.other_ref = bf16[2048,256]{1,0:T(8,128)(2,1)S(1)} collective-permute-done((bf16[2048,256]{1,0:T(8,128)(2,1)S(1)}, bf16[2048,256]{1,0:T(8,128)(2,1)S(1)}, u32[]{:S(2)}, u32[]{:S(2)}) %collective-permute-start) | collective-permute-done | bytes 1048608 | tf_op jit(solution)/shard_map/ppermute | solution.py:314
  45.3 12.5 %shard_map.92 = bf16[2048,128]{1,0:T(8,128)(2,1)} custom-call(s32[1,4]{1,0:T(1,128)S(1)} %copy-done.10, bf16[2048,256]{1,0:T(8,128)(2,1)S(1)} %bitcast.10, bf16[2048,256]{1,0:T(8,128)(2,1)S(1)} %collective-permute-done.other_ref, bf16[3,512,256]{2,1,0:T(8,128)(2,1)S(1)} %copy-done.5), custom_call_target="tpu_custom_call" | custom-call | flops 8589934592 | bytes 4194304 | tf_op jit(solution)/shard_map/pallas_call | solution.py:191
  57.8 4.5 %all-to-all-start.1 = ((bf16[16,128,128]{2,1,0:T(8,128)(2,1)}), bf16[16,128,128]{2,1,0:T(8,128)(2,1)S(1)}, u32[]{:S(2)}, u32[]{:S(2)}) async-start(bf16[16,128,128]{2,1,0:T(8,128)(2,1)} %bitcast.5), calls=%async_computation.1 | async-start | bytes 1048576 | tf_op jit(solution)/shard_map/all_to_all | solution.py:320
  62.2 1.2 copy-done.4
  63.5 1.1 copy-done.6
  64.6 12.5 %shard_map.93 = bf16[2048,128]{1,0:T(8,128)(2,1)} custom-call(s32[1,4]{1,0:T(1,128)S(1)} %copy-done.10, bf16[2048,256]{1,0:T(8,128)(2,1)S(1)} %bitcast.11, bf16[2048,256]{1,0:T(8,128)(2,1)S(1)} %copy-done.4, bf16[3,512,256]{2,1,0:T(8,128)(2,1)S(1)} %copy-done.6), custom_call_target="tpu_custom_call" | custom-call | flops 8589934592 | bytes 4194304 | tf_op jit(solution)/shard_map/pallas_call | solution.py:191
  77.1 0.5 all-to-all-done.1
  77.6 6.0 %all-to-all-start.2 = ((bf16[16,128,128]{2,1,0:T(8,128)(2,1)}), bf16[16,128,128]{2,1,0:T(8,128)(2,1)S(1)}, u32[]{:S(2)}, u32[]{:S(2)}) async-start(bf16[16,128,128]{2,1,0:T(8,128)(2,1)} %bitcast.7), calls=%async_computation.2 | async-start | bytes 1048576 | tf_op jit(solution)/shard_map/all_to_all | solution.py:320
  83.7 0.1 collective-permute-start.4
  83.7 0.5 collective-permute-start.5
  84.2 0.1 collective-permute-start.1
  84.3 14.2 %all-to-all-done.2 = bf16[16,128,128]{2,1,0:T(8,128)(2,1)S(1)} async-done(((bf16[16,128,128]{2,1,0:T(8,128)(2,1)}), bf16[16,128,128]{2,1,0:T(8,128)(2,1)S(1)}, u32[]{:S(2)}, u32[]{:S(2)}) %all-to-all-start.2) | async-done | bytes 524320 | tf_op jit(solution)/shard_map/all_to_all | solution.py:320
  98.5 0.5 collective-permute-start.3
  99.0 1.8 %collective-permute-done.3.out_other_ref = bf16[256,512]{1,0:T(8,128)(2,1)S(1)} collective-permute-done((bf16[256,512]{1,0:T(8,128)(2,1)S(1)}, bf16[256,512]{1,0:T(8,128)(2,1)S(1)}, u32[]{:S(2)}, u32[]{:S(2)}) %collective-permute-start.3) | collective-permute-done | bytes 262176 | tf_op jit(solution)/shard_map/ppermute | solution.py:314
  100.9 1.6 %copy-done = bf16[2048,512]{1,0:T(8,128)(2,1)S(1)} copy-done((bf16[2048,512]{1,0:T(8,128)(2,1)S(1)}, bf16[2048,512]{1,0:T(8,128)(2,1)}, u32[]{:S(2)}) %copy-start) | copy-done | bytes 2097176
  102.4 1.2 copy-done.2
  103.7 13.1 %shard_map.94 = (bf16[1024,512]{1,0:T(8,128)(2,1)S(1)}, bf16[2048,512]{1,0:T(8,128)(2,1)}) custom-call(s32[1,2048]{1,0:T(1,128)S(1)} %bitcast.17, f32[1,512]{1,0:T(1,128)S(1)} %bitcast.18, bf16[2048,512]{1,0:T(8,128)(2,1)S(1)} %copy-done, bf16[2048,128]{1,0:T(8,128)(2,1)S(1)} %bitcast.13, bf16[2048,128]{1,0:T(8,128)(2,1)S(1)} %bitcast.15, ...), custom_call_target="tpu_custom_call" | custom-call | flops 6979321856 | bytes 16777216 | tf_op jit(solution)/shard_map/pallas_call | solution.py:272
  116.8 0.2 collective-permute-start.6
  117.0 2.5 %collective-permute-done.6.other_ref = bf16[1024,512]{1,0:T(8,128)(2,1)S(1)} collective-permute-done((bf16[1024,512]{1,0:T(8,128)(2,1)S(1)}, bf16[1024,512]{1,0:T(8,128)(2,1)S(1)}, u32[]{:S(2)}, u32[]{:S(2)}) %collective-permute-start.6) | collective-permute-done | bytes 1048608 | tf_op jit(solution)/shard_map/ppermute | solution.py:314
  119.5 1.0 copy-done.11
  120.5 2.2 %shard_map.95 = bf16[2048,512]{1,0:T(8,128)(2,1)} custom-call(bf16[2048,512]{1,0:T(8,128)(2,1)} %get-tuple-element.7.whole_in_ref, bf16[1024,512]{1,0:T(8,128)(2,1)} %copy-done.11), custom_call_target="tpu_custom_call", output_to_operand_aliasing={{}: (0, {})} | custom-call | tf_op jit(solution)/shard_map/pallas_call | solution.py:303
  (24 shorter events, 0.1 us)
Async XLA Ops:
  7.8 37.5 %copy-start.5 = (bf16[3,512,256]{2,1,0:T(8,128)(2,1)S(1)}, bf16[3,512,256]{2,1,0:T(8,128)(2,1)}, u32[]{:S(2)}) copy-start(bf16[3,512,256]{2,1,0:T(8,128)(2,1)} %weight_ref.3) | copy-start | bytes 2359300
  7.8 37.5 %copy-start.10 = (s32[1,4]{1,0:T(1,128)S(1)}, s32[1,4]{1,0:T(1,128)}, u32[]{:S(2)}) copy-start(s32[1,4]{1,0:T(1,128)} %counts_ref.3) | copy-start | bytes 52
  42.6 2.7 %collective-permute-start = (bf16[2048,256]{1,0:T(8,128)(2,1)S(1)}, bf16[2048,256]{1,0:T(8,128)(2,1)S(1)}, u32[]{:S(2)}, u32[]{:S(2)}) collective-permute-start(bf16[2048,256]{1,0:T(8,128)(2,1)S(1)} %bitcast.9), channel_id=1, source_target_pairs={{0,1},{1,0},{2,3},{3,2},{4,5},{5,4},{6,7},{7,6},{8,9},{9,8},{10,11... | collective-permute-start | bytes 3145736 | tf_op jit(solution)/shard_map/ppermute | solution.py:314
  45.3 12.5 %copy-start.3 = (bf16[2048,256]{1,0:T(8,128)(2,1)}, bf16[2048,256]{1,0:T(8,128)(2,1)S(1)}, u32[]{:S(2)}) copy-start(bf16[2048,256]{1,0:T(8,128)(2,1)S(1)} %collective-permute-done.other_ref) | copy-start | bytes 3145732
  57.8 19.9 %all-to-all-start.1 = ((bf16[16,128,128]{2,1,0:T(8,128)(2,1)}), bf16[16,128,128]{2,1,0:T(8,128)(2,1)S(1)}, u32[]{:S(2)}, u32[]{:S(2)}) async-start(bf16[16,128,128]{2,1,0:T(8,128)(2,1)} %bitcast.5), calls=%async_computation.1 | async-start | bytes 1048576 | tf_op jit(solution)/shard_map/all_to_all | solution.py:320
  62.2 1.2 copy-start.4
  63.5 1.1 copy-start.6
  64.6 19.1 %copy-start.1 = (bf16[512,1024]{1,0:T(8,128)(2,1)S(1)}, bf16[512,1024]{1,0:T(8,128)(2,1)}, u32[]{:S(2)}) copy-start(bf16[512,1024]{1,0:T(8,128)(2,1)} %fc1_own_ref.1) | copy-start | bytes 3145732
  64.6 33.9 %copy-start.7 = (bf16[256,512]{1,0:T(8,128)(2,1)S(1)}, bf16[256,512]{1,0:T(8,128)(2,1)}, u32[]{:S(2)}) copy-start(bf16[256,512]{1,0:T(8,128)(2,1)} %out_own_ref.1) | copy-start | bytes 786436
  64.6 36.2 %copy-start.8 = (s32[2048]{0:T(1024)S(1)}, s32[2048]{0:T(1024)}, u32[]{:S(2)}) copy-start(s32[2048]{0:T(1024)} %param.10) | copy-start | bytes 24580
  64.6 36.2 %copy-start.9 = (f32[512]{0:T(512)S(1)}, f32[512]{0:T(512)}, u32[]{:S(2)}) copy-start(f32[512]{0:T(512)} %param.15) | copy-start | bytes 6148
  77.6 20.9 %all-to-all-start.2 = ((bf16[16,128,128]{2,1,0:T(8,128)(2,1)}), bf16[16,128,128]{2,1,0:T(8,128)(2,1)S(1)}, u32[]{:S(2)}, u32[]{:S(2)}) async-start(bf16[16,128,128]{2,1,0:T(8,128)(2,1)} %bitcast.7), calls=%async_computation.2 | async-start | bytes 1048576 | tf_op jit(solution)/shard_map/all_to_all | solution.py:320
  83.7 17.2 %collective-permute-start.4 = (bf16[512,1024]{1,0:T(8,128)(2,1)S(1)}, bf16[512,1024]{1,0:T(8,128)(2,1)S(1)}, u32[]{:S(2)}, u32[]{:S(2)}) collective-permute-start(bf16[512,1024]{1,0:T(8,128)(2,1)S(1)} %copy-done.1), channel_id=1, source_target_pairs={{0,1},{1,0},{2,3},{3,2},{4,5},{5,4},{6,7},{7,6},{8,9},{9,8},{10,11... | collective-permute-start | bytes 3145736 | tf_op jit(solution)/shard_map/ppermute | solution.py:314
  83.7 17.1 %collective-permute-start.5 = (bf16[1024,512]{1,0:T(8,128)(2,1)}, bf16[1024,512]{1,0:T(8,128)(2,1)}, u32[]{:S(2)}, u32[]{:S(2)}) collective-permute-start(bf16[1024,512]{1,0:T(8,128)(2,1)} %fc2_own_ref.1), channel_id=1, source_target_pairs={{0,1},{1,0},{2,3},{3,2},{4,5},{5,4},{6,7},{7,6},{8,9},{9,8},{10,11... | collective-permute-start | bytes 3145736 | tf_op jit(solution)/shard_map/ppermute | solution.py:314
  84.2 16.6 %collective-permute-start.1 = (bf16[2048,128]{1,0:T(8,128)(2,1)S(1)}, bf16[2048,128]{1,0:T(8,128)(2,1)}, u32[]{:S(2)}, u32[]{:S(2)}) collective-permute-start(bf16[2048,128]{1,0:T(8,128)(2,1)S(1)} %bitcast.12), channel_id=1, source_target_pairs={{0,1},{1,0},{2,3},{3,2},{4,5},{5,4},{6,7},{7,6},{8,9},{9,8},{10,11... | collective-permute-start | bytes 1572872 | tf_op jit(solution)/shard_map/ppermute | solution.py:314
  98.5 2.3 %collective-permute-start.2 = (bf16[2048,128]{1,0:T(8,128)(2,1)S(1)}, bf16[2048,128]{1,0:T(8,128)(2,1)S(1)}, u32[]{:S(2)}, u32[]{:S(2)}) collective-permute-start(bf16[2048,128]{1,0:T(8,128)(2,1)S(1)} %bitcast.14), channel_id=1, source_target_pairs={{0,1},{1,0},{2,3},{3,2},{4,5},{5,4},{6,7},{7,6},{8,9},{9,8},{10,11... | collective-permute-start | bytes 1572872 | tf_op jit(solution)/shard_map/ppermute | solution.py:314
  98.5 2.3 %collective-permute-start.3 = (bf16[256,512]{1,0:T(8,128)(2,1)S(1)}, bf16[256,512]{1,0:T(8,128)(2,1)S(1)}, u32[]{:S(2)}, u32[]{:S(2)}) collective-permute-start(bf16[256,512]{1,0:T(8,128)(2,1)S(1)} %copy-done.7), channel_id=1, source_target_pairs={{0,1},{1,0},{2,3},{3,2},{4,5},{5,4},{6,7},{7,6},{8,9},{9,8},{10,11... | collective-permute-start | bytes 786440 | tf_op jit(solution)/shard_map/ppermute | solution.py:314
  100.9 1.6 %copy-start = (bf16[2048,512]{1,0:T(8,128)(2,1)S(1)}, bf16[2048,512]{1,0:T(8,128)(2,1)}, u32[]{:S(2)}) copy-start(bf16[2048,512]{1,0:T(8,128)(2,1)} %points_ref.1) | copy-start | bytes 6291460
  102.4 1.2 copy-start.2
  116.8 2.7 %collective-permute-start.6 = (bf16[1024,512]{1,0:T(8,128)(2,1)S(1)}, bf16[1024,512]{1,0:T(8,128)(2,1)S(1)}, u32[]{:S(2)}, u32[]{:S(2)}) collective-permute-start(bf16[1024,512]{1,0:T(8,128)(2,1)S(1)} %get-tuple-element.8), channel_id=1, source_target_pairs={{0,1},{1,0},{2,3},{3,2},{4,5},{5,4},{6,7},{7,6},{8,9},{9,8},{10,11... | collective-permute-start | bytes 3145736 | tf_op jit(solution)/shard_map/ppermute | solution.py:314
  119.5 1.0 copy-start.11
where the time goes:
time: 124 us; the launch traced here: 123 us
  Pallas kernels  48.1 us (39%)
  blocking collectives  34.8 us (28%)
  waiting for transfers between devices  21.7 us (18%)
  starting transfers between devices  11.8 us (10%)
  local copies, waits for them, and re-layouts  6.19 us (5%)
    all_to_all x1, blocking collectives, exchange(): lax.all_to_all(cells, 'space', split_axis=0, concat_axis=0, tiled=True)  34.8 us
    pallas_call x2, Pallas kernels, attend(): pl.pallas_call(functools.partial(attend_kernel, pair), out_shape=jax.Shap...  25 us
    all_to_all x2, waiting for transfers between devices, exchange(): lax.all_to_all(cells, 'space', split_axis=0, concat_axis=0, tiled=True)  14.7 us
    pallas_call x1, Pallas kernels, finish(): pl.pallas_call(functools.partial(finish_kernel, shards), out_shape=(jax.S...  13.1 us
    all_to_all x2, starting transfers between devices, exchange(): lax.all_to_all(cells, 'space', split_axis=0, concat_axis=0, tiled=True)  10.5 us
    pallas_call x1, Pallas kernels, order_for_owners(): pl.pallas_call(functools.partial(send_kernel, shards), out_shape=jax.Shap...  7.74 us
    ppermute x7, waiting for transfers between devices, across(): return lax.ppermute(values, 'mp', [(0, 1), (1, 0)])  6.98 us
    unnamed x24, local copies, waits for them, and re-layouts  6.19 us
  transfers between devices with their start and end apart: 9, of which 5 were waited for; matrix products, arithmetic and copies ran while one was open for 0% of the time, Pallas kernels for 10%

commit v1 on v0

v1 whole, which is shorter than its diff:
```python
import functools
import math

import jax
import jax.numpy as jnp
from jax import lax
from jax.experimental import pallas as pl
from jax.experimental.pallas import tpu as pltpu
from jax.sharding import PartitionSpec as P

HDIM = 64
LANES = 128
ROWS = 256
EPSILON = 1e-06
FAR = 1e30
VMEM_BYTES = 58 * 1024 * 1024

f32 = jnp.float32
bf16 = jnp.bfloat16

ANYWHERE = pl.BlockSpec(memory_space=pl.ANY)
SCALARS = pl.BlockSpec(memory_space=pltpu.SMEM)


def normalise(values, gain_row):
    average = jnp.mean(values, axis=-1, keepdims=True)
    centred = values - average
    second = jnp.mean(centred * centred, axis=-1, keepdims=True)
    return (centred * lax.rsqrt(second + EPSILON) * gain_row).astype(bf16)


def dot(left, right):
    return jnp.dot(left, right, preferred_element_type=f32)


def split(number, size):
    if size & (size - 1) == 0:
        return number >> (size.bit_length() - 1), number & (size - 1)
    return number // size, number % size


def owner_slots(rank, length, shards):
    owner, within = split(rank, length)
    return owner, within - lax.axis_index("space") * (length // shards)


def equal(left, right):
    return (left == right).astype(f32).astype(bf16)


def blocks_of(length, rows=ROWS):
    return [slice(i * rows, (i + 1) * rows) for i in range(length // rows)]


def params():
    return pltpu.CompilerParams(vmem_limit_bytes=VMEM_BYTES)


def part_slots(rank, length, shards, parts):
    owner, within = owner_slots(rank, length, shards)
    part_cell = length // shards // parts
    part, row = split(within, part_cell)
    return part * (length // parts) + owner * part_cell + row


def pick_rows(first_row, slot, source_ref, out_ref):
    def order_block(i, carry):
        start = pl.multiple_of(i * ROWS, ROWS)
        place = lax.broadcasted_iota(jnp.int32, (ROWS, slot.shape[1]), 0) + (start + first_row)
        out_ref[pl.ds(start, ROWS), :] = dot(equal(place, slot), source_ref[...]).astype(bf16)
        return carry

    lax.fori_loop(0, out_ref.shape[0] // ROWS, order_block, 0)


def first_send_kernel(
    shards, parts, rank_hbm, gain_hbm, points_hbm, out_ref, normed_hbm, rank_ref, gain_ref, points_ref, half_ref, small, large, away
):
    length, features = points_ref.shape
    half = features // 2
    core = lax.axis_index("mp")
    gain_copy = pltpu.make_async_copy(gain_hbm, gain_ref, small.at[0])
    rank_copy = pltpu.make_async_copy(rank_hbm, rank_ref, small.at[1])
    rows_of = blocks_of(length)
    copies = [
        pltpu.make_async_copy(points_hbm.at[rows], points_ref.at[rows], large.at[i])
        for i, rows in enumerate(rows_of)
    ]
    gain_copy.start()
    for copy in copies:
        copy.start()
    rank_copy.start()
    gain_copy.wait()
    for copy, rows in zip(copies, rows_of):
        copy.wait()
        normed = normalise(points_ref[rows, :].astype(f32), gain_ref[...])
        half_ref[rows, :] = jnp.where(core == 0, normed[:, :half], normed[:, half:])
    keep = pltpu.make_async_copy(half_ref, normed_hbm, away)
    keep.start()
    rank_copy.wait()
    pick_rows(0, part_slots(rank_ref[...], length, shards, parts), half_ref, out_ref)
    keep.wait()


def first_send(shards, parts, rank_row, gain_row, points):
    length, features = points.shape
    return pl.pallas_call(
        functools.partial(first_send_kernel, shards, parts),
        out_shape=(
            jax.ShapeDtypeStruct((length // parts, features // 2), bf16),
            jax.ShapeDtypeStruct((length, features // 2), bf16),
        ),
        in_specs=[ANYWHERE] * 3,
        out_specs=(pl.BlockSpec(memory_space=pltpu.VMEM), ANYWHERE),
        scratch_shapes=[
            pltpu.VMEM((1, length), jnp.int32),
            pltpu.VMEM((1, features), f32),
            pltpu.VMEM((length, features), bf16),
            pltpu.VMEM((length, features // 2), bf16),
            pltpu.SemaphoreType.DMA((2,)),
            pltpu.SemaphoreType.DMA((length // ROWS,)),
            pltpu.SemaphoreType.DMA,
        ],
        compiler_params=params(),
        cost_estimate=pl.CostEstimate(
            flops=length * length * features // parts, bytes_accessed=4 * length * features, transcendentals=0
        ),
    )(rank_row, gain_row, points)


def next_send_kernel(shards, parts, part, rank_hbm, normed_hbm, out_ref, rank_ref, half_ref, sems):
    length = half_ref.shape[0]
    copies = [
        pltpu.make_async_copy(rank_hbm, rank_ref, sems.at[0]),
        pltpu.make_async_copy(normed_hbm, half_ref, sems.at[1]),
    ]
    for copy in copies:
        copy.start()
    for copy in copies:
        copy.wait()
    pick_rows(part * out_ref.shape[0], part_slots(rank_ref[...], length, shards, parts), half_ref, out_ref)


def next_send(shards, parts, part, rank_row, normed):
    length, half = normed.shape
    return pl.pallas_call(
        functools.partial(next_send_kernel, shards, parts, part),
        out_shape=jax.ShapeDtypeStruct((length // parts, half), bf16),
        in_specs=[ANYWHERE] * 2,
        out_specs=pl.BlockSpec(memory_space=pltpu.VMEM),
        scratch_shapes=[
            pltpu.VMEM((1, length), jnp.int32),
            pltpu.VMEM((length, half), bf16),
            pltpu.SemaphoreType.DMA((2,)),
        ],
        compiler_params=params(),
        cost_estimate=pl.CostEstimate(
            flops=2 * length * length * half // parts, bytes_accessed=4 * length * half, transcendentals=0
        ),
    )(rank_row, normed)


def attend_kernel(pair, parts, counts_ref, *refs):
    arrived = refs[: 2 * parts]
    weight_hbm, out_hbm, x_ref, raw_ref, w_ref, q_ref, k_ref, v_ref, out_ref, x_sems, w_sems, out_sems = refs[2 * parts :]
    length, features = q_ref.shape[1], w_ref.shape[0]
    half = features // 2
    tiles = counts_ref.shape[1]
    core = lax.axis_index("mp")
    scale = math.log2(math.e) / math.sqrt(HDIM)
    pair_columns = slice(pair * LANES, (pair + 1) * LANES)

    w_copies = [
        pltpu.make_async_copy(
            weight_hbm.at[:, pl.ds(pl.multiple_of(at * half, half), half), pair_columns],
            raw_ref.at[:, k * half : (k + 1) * half],
            w_sems.at[k],
        )
        for k, at in enumerate((core, 1 - core))
    ]
    part_cell = arrived[0].shape[1]
    x_copies = [
        pltpu.make_async_copy(
            arrived[k * parts + part],
            x_ref.at[:, part * part_cell : (part + 1) * part_cell, k * half : (k + 1) * half],
            x_sems.at[k * parts + part],
        )
        for k in range(2)
        for part in range(parts)
    ]
    for copy in w_copies + x_copies:
        copy.start()

    starts = [jnp.int32(0)]
    for t in range(tiles):
        starts.append(starts[-1] + counts_ref[0, t])
    lane = lax.broadcasted_iota(jnp.int32, (1, LANES), 1)
    first = jnp.full((1, LANES), length, jnp.int32)
    last = jnp.zeros((1, LANES), jnp.int32)
    for t in range(tiles):
        first = jnp.where(lane == HDIM + t, starts[t], first)
        last = jnp.where(lane == HDIM + t, starts[t + 1], last)
    flags = jnp.logical_and(lane >= HDIM, lane < HDIM + tiles)
    low_lanes = lane < HDIM

    for copy in w_copies:
        copy.wait()
    for j in range(3):
        both = raw_ref[j].astype(f32)
        at = 2 * j * LANES
        w_ref[:, at : at + LANES] = jnp.where(low_lanes, both, 0.0).astype(bf16)
        odd = jnp.where(low_lanes, pltpu.roll(both, HDIM, 1), 0.0) if j < 2 else jnp.where(low_lanes, 0.0, both)
        w_ref[:, at + LANES : at + 2 * LANES] = odd.astype(bf16)
    for copy in x_copies:
        copy.wait()

    cell = x_ref.shape[1]
    cells = ROWS // cell

    def project(i, carry):
        rows = pl.ds(pl.multiple_of(i * ROWS, ROWS), ROWS)
        block = x_ref[pl.ds(i * cells, cells)].reshape(ROWS, features)
        place = lax.broadcasted_iota(jnp.int32, (ROWS, LANES), 0) + i * ROWS
        inside = jnp.logical_and(place >= first, place < last)
        q_flag = jnp.where(inside, 1.0, 0.0)
        k_flag = jnp.where(jnp.logical_and(flags, jnp.logical_not(inside)), -FAR, 0.0)
        spread = dot(block, w_ref[...])
        for h in range(2):
            q, k, v = (spread[:, (2 * j + h) * LANES : (2 * j + h + 1) * LANES] for j in range(3))
            q_ref[h, rows, :] = (q * scale + q_flag).astype(bf16)
            k_ref[h, rows, :] = (k + k_flag).astype(bf16)
            ones = jnp.logical_not(low_lanes) if h == 0 else low_lanes
            v_ref[h, rows, :] = (v + jnp.where(ones, 1.0, 0.0)).astype(bf16)
        return carry

    lax.fori_loop(0, length // ROWS, project, 0)

    def raise_scores(scores):
        return jnp.exp2(scores - jnp.max(scores, axis=1, keepdims=True)).astype(bf16)

    def send_out(i):
        rows = pl.ds(pl.multiple_of(i * ROWS, ROWS), ROWS)
        return pltpu.make_async_copy(out_ref.at[rows], out_hbm.at[rows], out_sems.at[i])

    def query_block(i, carry):
        begin = i * ROWS
        rows = pl.ds(pl.multiple_of(begin, ROWS), ROWS)
        low, high = jnp.int32(0), jnp.int32(length)
        for t in range(tiles):
            low = jnp.where(starts[t] <= begin, starts[t], low)
            end = starts[tiles - t]
            high = jnp.where(end >= begin + ROWS, end, high)
        low = (low // 16) * 16
        blocks = (high - low + ROWS - 1) // ROWS
        for n in range(1, length // ROWS + 1):

            @pl.when(blocks == n)
            def _(n=n):
                start = jnp.minimum(low, length - n * ROWS)
                keys = pl.ds(pl.multiple_of(start, 16), n * ROWS)
                scores = [
                    lax.dot_general(
                        q_ref[h, rows, :],
                        k_ref[h, keys, :],
                        (((1,), (1,)), ((), ())),
                        preferred_element_type=f32,
                    )
                    for h in range(2)
                ]
                even = dot(raise_scores(scores[0]), v_ref[0, keys, :])
                odd = dot(raise_scores(scores[1]), v_ref[1, keys, :])
                total = pltpu.roll(jnp.where(low_lanes, odd, even), HDIM, 1)
                out_ref[rows, :] = (jnp.where(low_lanes, even, odd) / total).astype(bf16)

        send_out(i).start()
        return carry

    lax.fori_loop(0, length // ROWS, query_block, 0)
    for i in range(length // ROWS):
        send_out(i).wait()


def attend(pair, counts, arrived, w_qkv):
    parts = len(arrived) // 2
    shards, part_cell, half = arrived[0].shape
    cell = part_cell * parts
    length = shards * cell
    features = 2 * half
    return pl.pallas_call(
        functools.partial(attend_kernel, pair, parts),
        out_shape=jax.ShapeDtypeStruct((length, LANES), bf16),
        in_specs=[SCALARS] + [ANYWHERE] * (2 * parts + 1),
        out_specs=ANYWHERE,
        scratch_shapes=[
            pltpu.VMEM((shards, cell, features), bf16),
            pltpu.VMEM((3, features, LANES), bf16),
            pltpu.VMEM((features, 6 * LANES), bf16),
            pltpu.VMEM((2, length, LANES), bf16),
            pltpu.VMEM((2, length, LANES), bf16),
            pltpu.VMEM((2, length, LANES), bf16),
            pltpu.VMEM((length, LANES), bf16),
            pltpu.SemaphoreType.DMA((2 * parts,)),
            pltpu.SemaphoreType.DMA((2,)),
            pltpu.SemaphoreType.DMA((length // ROWS,)),
        ],
        compiler_params=params(),
        cost_estimate=pl.CostEstimate(
            flops=32 * length * length * HDIM, bytes_accessed=8 * length * half, transcendentals=2 * length * length
        ),
    )(counts, *arrived, w_qkv)


def unorder(rank_ref, start, length, shards, context_ref):
    owner, within = owner_slots(rank_ref[:, pl.ds(start, ROWS)], length, shards)
    slot = owner * (length // shards) + within
    slot = jnp.transpose(jnp.broadcast_to(slot, (LANES, ROWS)))
    place = lax.broadcasted_iota(jnp.int32, (ROWS, LANES), 1)
    pick = jnp.concatenate([equal(slot, place + k * LANES) for k in range(length // LANES)], axis=1)
    return dot(pick, context_ref[...]).astype(bf16)


def unorder_kernel(shards, rank_hbm, own_hbm, other_hbm, out_ref, rank_ref, context_ref, sems):
    length = context_ref.shape[0]
    half_rows = out_ref.shape[0]
    base = lax.axis_index("mp") * half_rows
    copies = [
        pltpu.make_async_copy(rank_hbm, rank_ref, sems.at[0]),
        pltpu.make_async_copy(own_hbm, context_ref.at[:, :LANES], sems.at[1]),
        pltpu.make_async_copy(other_hbm, context_ref.at[:, LANES:], sems.at[2]),
    ]
    for copy in copies:
        copy.start()
    for copy in copies:
        copy.wait()

    def block(i, carry):
        start = pl.multiple_of(base + i * ROWS, ROWS)
        out_ref[pl.ds(pl.multiple_of(i * ROWS, ROWS), ROWS), :] = unorder(
            rank_ref, start, length, shards, context_ref
        )
        return carry

    lax.fori_loop(0, half_rows // ROWS, block, 0)


def unorder_pair(shards, rank_row, own, other):
    length = own.shape[0]
    half_rows = length // 2
    return pl.pallas_call(
        functools.partial(unorder_kernel, shards),
        out_shape=jax.ShapeDtypeStruct((half_rows, 2 * LANES), bf16),
        in_specs=[ANYWHERE] * 3,
        out_specs=pl.BlockSpec(memory_space=pltpu.VMEM),
        scratch_shapes=[
            pltpu.VMEM((1, length), jnp.int32),
            pltpu.VMEM((length, 2 * LANES), bf16),
            pltpu.SemaphoreType.DMA((3,)),
        ],
        compiler_params=params(),
        cost_estimate=pl.CostEstimate(
            flops=4 * half_rows * length * LANES, bytes_accessed=8 * length * LANES, transcendentals=0
        ),
    )(rank_row, own, other)


def finish_kernel(
    shards,
    rank_hbm,
    gain_hbm,
    points_hbm,
    first_hbm,
    own_hbm,
    other_hbm,
    out_own_hbm,
    out_other_hbm,
    fc1_own_hbm,
    fc1_other_hbm,
    fc2_own_hbm,
    fc2_other_hbm,
    done_ref,
    whole_hbm,
    rank_ref,
    gain_ref,
    points_ref,
    first_ref,
    context_ref,
    out_ref,
    fc1_ref,
    fc2_ref,
    in_sems,
    sems,
):
    length = context_ref.shape[0]
    half_rows = done_ref.shape[0]
    base = pl.multiple_of(lax.axis_index("mp") * half_rows, half_rows)
    half = out_own_hbm.shape[0]
    hidden_half = fc2_own_hbm.shape[0]
    pairs = [
        (rank_hbm, rank_ref),
        (own_hbm, context_ref.at[:, :LANES]),
        (other_hbm, context_ref.at[:, LANES:]),
        (gain_hbm, gain_ref),
        (first_hbm, first_ref),
        (out_own_hbm, out_ref.at[:half]),
        (out_other_hbm, out_ref.at[half:]),
        (points_hbm.at[pl.ds(base, half_rows)], points_ref),
        (fc1_own_hbm, fc1_ref.at[0]),
        (fc2_own_hbm, fc2_ref.at[0]),
        (fc1_other_hbm, fc1_ref.at[1]),
        (fc2_other_hbm, fc2_ref.at[1]),
    ]
    copies = [pltpu.make_async_copy(*pair, in_sems.at[k]) for k, pair in enumerate(pairs)]
    for copy in copies:
        copy.start()

    def away(i):
        here = pl.multiple_of(i * ROWS, ROWS)
        there = pl.multiple_of(base + i * ROWS, ROWS)
        return pltpu.make_async_copy(
            done_ref.at[pl.ds(here, ROWS)], whole_hbm.at[pl.ds(there, ROWS)], sems.at[i]
        )

    def block(i, late):
        here = pl.ds(pl.multiple_of(i * ROWS, ROWS), ROWS)
        start = pl.multiple_of(base + i * ROWS, ROWS)
        second = unorder(rank_ref, start, length, shards, context_ref)
        for copy in late[:5]:
            copy.wait()
        pick = first_ref[here, :]
        context = jnp.concatenate([pick[:, :LANES], second[:, :LANES], pick[:, LANES:], second[:, LANES:]], axis=1)
        attn_out = dot(context, out_ref[...]).astype(bf16).astype(f32)
        middle = (points_ref[here, :].astype(f32) + attn_out).astype(bf16).astype(f32)
        normed = normalise(middle, gain_ref[...])
        for copy in late[5:]:
            copy.wait()
        total = middle
        for k in range(2):
            hidden = jax.nn.gelu(dot(normed, fc1_ref[k]), approximate=True).astype(bf16)
            total = total + dot(hidden, fc2_ref[k])
        done_ref[here, :] = total.astype(bf16)
        away(i).start()

    for copy in copies[:3]:
        copy.wait()
    block(0, copies[3:])

    def rest(i, carry):
        block(i, ())
        return carry

    lax.fori_loop(1, half_rows // ROWS, rest, 0)
    for i in range(half_rows // ROWS):
        away(i).wait()


def finish(shards, rank_row, gain_row, points, first, own, other, w_out, other_out, *mlp):
    length, features = points.shape
    half_rows = length // 2
    hidden_half = mlp[2].shape[0]
    return pl.pallas_call(
        functools.partial(finish_kernel, shards),
        out_shape=(
            jax.ShapeDtypeStruct((half_rows, features), bf16),
            jax.ShapeDtypeStruct((length, features), bf16),
        ),
        in_specs=[ANYWHERE] * 12,
        out_specs=(pl.BlockSpec(memory_space=pltpu.VMEM), ANYWHERE),
        scratch_shapes=[
            pltpu.VMEM((1, length), jnp.int32),
            pltpu.VMEM((1, features), f32),
            pltpu.VMEM((half_rows, features), bf16),
            pltpu.VMEM((half_rows, 2 * LANES), bf16),
            pltpu.VMEM((length, 2 * LANES), bf16),
            pltpu.VMEM((features, features), bf16),
            pltpu.VMEM((2, features, hidden_half), bf16),
            pltpu.VMEM((2, hidden_half, features), bf16),
            pltpu.SemaphoreType.DMA((12,)),
            pltpu.SemaphoreType.DMA((half_rows // ROWS,)),
        ],
        compiler_params=params(),
        cost_estimate=pl.CostEstimate(
            flops=2 * half_rows * features * (length + 9 * features),
            bytes_accessed=16 * length * features,
            transcendentals=half_rows * 4 * features,
        ),
    )(rank_row, gain_row, points, first, own, other, w_out, other_out, *mlp)


def across(values):
    return lax.ppermute(values, "mp", [(0, 1), (1, 0)])


def exchange(rows, shards):
    length, columns = rows.shape
    cells = rows.reshape(shards, length // shards, columns)
    return lax.all_to_all(cells, "space", split_axis=0, concat_axis=0, tiled=True)


def body(points, curve_rank, patch_counts, norm_gain_attn, w_qkv, w_out, norm_gain_mlp, w_fc1, w_fc2):
    shards = lax.axis_size("space")
    length, features = points.shape
    parts = 2 if (length // shards) % 32 == 0 else 1
    rank_row = curve_rank.reshape(1, length)
    send, normed = first_send(shards, parts, rank_row, norm_gain_attn.reshape(1, features), points)
    own = [exchange(send, shards)]
    for part in range(1, parts):
        own.append(exchange(next_send(shards, parts, part, rank_row, normed), shards))
    mlp = w_fc1, across(w_fc1), w_fc2, across(w_fc2)
    other_out = across(w_out)
    other = [across(rows) for rows in own]
    returned = [
        exchange(attend(pair, patch_counts, own + other, w_qkv), shards).reshape(length, LANES) for pair in range(2)
    ]
    crossed = [across(rows) for rows in returned]
    first = unorder_pair(shards, rank_row, returned[0], crossed[0])
    done, whole = finish(
        shards,
        rank_row,
        norm_gain_mlp.reshape(1, features),
        points,
        first,
        returned[1],
        crossed[1],
        w_out,
        other_out,
        *mlp,
    )
    start = (1 - lax.axis_index("mp")) * (length // 2)
    return lax.dynamic_update_slice(whole, across(done), (start, 0))


def solution(mesh):
    placed = (
        P("space", None),
        P("space"),
        P("space", None),
        P(),
        P(None, None, "mp"),
        P("mp", None),
        P(),
        P(None, "mp"),
        P("mp", None),
    )
    return jax.shard_map(
        body, mesh=mesh, in_specs=placed, out_specs=P("space", None), check_vma=False
    )
```

time: 124 us -> 133 us (1.073)
  waiting for transfers between devices: 21.7 us -> 34.4 us
  blocking collectives: 34.8 us -> 23.5 us
  Pallas kernels: 48.1 us -> 56.3 us
  starting transfers between devices: 11.8 us -> 15.4 us
  local copies, waits for them, and re-layouts: 6.19 us -> 2.69 us
    all_to_all x2 -> x3, waiting for transfers between devices: 14.7 us -> 29.7 us  [exchange(): lax.all_to_all(cells, 'space', split_axis=0, concat_axis=0, tiled=True)]
    all_to_all x1, blocking collectives: 34.8 us -> 23.5 us  [exchange(): lax.all_to_all(cells, 'space', split_axis=0, concat_axis=0, tiled=True)]
    pallas_call x4 -> x5, Pallas kernels: 34.9 us -> 41.8 us  [the longest x2 28.2 us: attend(): pl.pallas_call(functools.partial(attend_kernel, pair, parts), out_shape=j...]
    unnamed x24 -> x22, local copies, waits for them, and re-layouts: 6.19 us -> 1.66 us
    all_to_all x2 -> x3, starting transfers between devices: 10.5 us -> 14 us  [exchange(): lax.all_to_all(cells, 'space', split_axis=0, concat_axis=0, tiled=True)]
    ppermute x7 -> x8, waiting for transfers between devices: 6.98 us -> 4.72 us  [across(): return lax.ppermute(values, 'mp', [(0, 1), (1, 0)])]
    pallas_call x1, Pallas kernels: 13.1 us -> 14.5 us  [finish(): pl.pallas_call(functools.partial(finish_kernel, shards), out_shape=(jax.S...]
  transfers between devices with their start and end apart: 9 -> 11, of which waited for: 5 -> 5; matrix products, arithmetic and copies ran while one was open for 0% -> 0% of each run, Pallas kernels for 10% -> 14%
where the time goes in v1:
time: 133 us; the launch traced here: 132 us
  Pallas kernels  56.3 us (42%)
  waiting for transfers between devices  34.4 us (26%)
  blocking collectives  23.5 us (18%)
  starting transfers between devices  15.4 us (12%)
  local copies, waits for them, and re-layouts  2.69 us (2%)
    all_to_all x3, waiting for transfers between devices, exchange(): lax.all_to_all(cells, 'space', split_axis=0, concat_axis=0, tiled=True)  29.7 us
    pallas_call x2, Pallas kernels, attend(): pl.pallas_call(functools.partial(attend_kernel, pair, parts), out_shape=j...  28.2 us
    all_to_all x1, blocking collectives, exchange(): lax.all_to_all(cells, 'space', split_axis=0, concat_axis=0, tiled=True)  23.5 us
    pallas_call x1, Pallas kernels, finish(): pl.pallas_call(functools.partial(finish_kernel, shards), out_shape=(jax.S...  14.5 us
    all_to_all x3, starting transfers between devices, exchange(): lax.all_to_all(cells, 'space', split_axis=0, concat_axis=0, tiled=True)  14 us
    pallas_call x1, Pallas kernels, first_send(): pl.pallas_call(functools.partial(first_send_kernel, shards, parts), out_s...  5.83 us
    ppermute x8, waiting for transfers between devices, across(): return lax.ppermute(values, 'mp', [(0, 1), (1, 0)])  4.72 us
    pallas_call x1, Pallas kernels, unorder_pair(): pl.pallas_call(functools.partial(unorder_kernel, shards), out_shape=jax.S...  3.99 us
  transfers between devices with their start and end apart: 11, of which 5 were waited for; matrix products, arithmetic and copies ran while one was open for 0% of the time, Pallas kernels for 14%

profile of v1, /device:TPU:0, one launch (start us, length us, event | category | flops | bytes accessed | tf_op | source)
XLA Modules:
  0.0 132.5 jit_solution(193015762038299941)
XLA Ops:
  0.0 5.8 %shard_map.91 = (bf16[1024,256]{1,0:T(8,128)(2,1)}, bf16[2048,256]{1,0:T(8,128)(2,1)}) custom-call(s32[1,2048]{1,0:T(1,128)} %bitcast.16, f32[1,512]{1,0:T(1,128)} %bitcast.20, bf16[2048,512]{1,0:T(8,128)(2,1)} %points_hbm.3), custom_call_target="tpu_custom_call" | custom-call | flops 1073741824 | bytes 4194304 | tf_op jit(solution)/shard_map/pallas_call | solution.py:107
  5.8 3.8 %shard_map.92 = bf16[1024,256]{1,0:T(8,128)(2,1)} custom-call(s32[1,2048]{1,0:T(1,128)} %bitcast.17, bf16[2048,256]{1,0:T(8,128)(2,1)} %get-tuple-element.10.normed_hbm), custom_call_target="tpu_custom_call" | custom-call | flops 1073741824 | bytes 2097152 | tf_op jit(solution)/shard_map/pallas_call | solution.py:146
  9.7 23.5 %all_to_all.20.refs_1_ = bf16[16,64,256]{2,1,0:T(8,128)(2,1)S(1)} all-to-all(bf16[16,64,256]{2,1,0:T(8,128)(2,1)} %bitcast.15), channel_id=1, replica_groups=mesh['space'=16,'mp'=2] {'space'}, dimensions={0} | all-to-all | bytes 1048576 | tf_op jit(solution)/shard_map/all_to_all | solution.py:496
  33.1 3.9 %all-to-all-start = ((bf16[16,64,256]{2,1,0:T(8,128)(2,1)}), bf16[16,64,256]{2,1,0:T(8,128)(2,1)S(1)}, u32[]{:S(2)}, u32[]{:S(2)}) async-start(bf16[16,64,256]{2,1,0:T(8,128)(2,1)} %bitcast.3), calls=%async_computation | async-start | bytes 1048576 | tf_op jit(solution)/shard_map/all_to_all | solution.py:496
  37.1 14.3 %all-to-all-done.refs_0_ = bf16[16,64,256]{2,1,0:T(8,128)(2,1)S(1)} async-done(((bf16[16,64,256]{2,1,0:T(8,128)(2,1)}), bf16[16,64,256]{2,1,0:T(8,128)(2,1)S(1)}, u32[]{:S(2)}, u32[]{:S(2)}) %all-to-all-start) | async-done | bytes 524320 | tf_op jit(solution)/shard_map/all_to_all | solution.py:496
  51.5 1.9 %collective-permute-done.refs_2_ = bf16[16,64,256]{2,1,0:T(8,128)(2,1)S(1)} collective-permute-done((bf16[16,64,256]{2,1,0:T(8,128)(2,1)S(1)}, bf16[16,64,256]{2,1,0:T(8,128)(2,1)S(1)}, u32[]{:S(2)}, u32[]{:S(2)}) %collective-permute-start) | collective-permute-done | bytes 524320 | tf_op jit(solution)/shard_map/ppermute | solution.py:490
  53.4 0.8 copy-done.8
  54.2 14.0 %shard_map.93 = bf16[2048,128]{1,0:T(8,128)(2,1)} custom-call(s32[1,4]{1,0:T(1,128)} %counts_ref.3, bf16[16,64,256]{2,1,0:T(8,128)(2,1)} %copy-done.3, bf16[16,64,256]{2,1,0:T(8,128)(2,1)} %copy-done.2, bf16[16,64,256]{2,1,0:T(8,128)(2,1)} %copy-done.8, bf16[16,64,256]{2,1,0:T(8,128)(2,1)} %copy-done.7, bf16[3,512,256]{2,1,0:T(8,128)(2,1)} %refs_4_.3), custom_call_target="tpu_custom_call" | custom-call | flops 8589934592 | bytes 4194304 | tf_op jit(solution)/shard_map/pallas_call | solution.py:289
  68.2 4.1 %all-to-all-start.2 = ((bf16[16,128,128]{2,1,0:T(8,128)(2,1)}), bf16[16,128,128]{2,1,0:T(8,128)(2,1)S(1)}, u32[]{:S(2)}, u32[]{:S(2)}) async-start(bf16[16,128,128]{2,1,0:T(8,128)(2,1)} %bitcast.14), calls=%async_computation.2 | async-start | bytes 1048576 | tf_op jit(solution)/shard_map/all_to_all | solution.py:496
  72.4 14.2 %shard_map.95 = bf16[2048,128]{1,0:T(8,128)(2,1)} custom-call(s32[1,4]{1,0:T(1,128)} %counts_ref.3, bf16[16,64,256]{2,1,0:T(8,128)(2,1)} %copy-done.3, bf16[16,64,256]{2,1,0:T(8,128)(2,1)} %copy-done.2, bf16[16,64,256]{2,1,0:T(8,128)(2,1)} %copy-done.8, bf16[16,64,256]{2,1,0:T(8,128)(2,1)} %copy-done.7, bf16[3,512,256]{2,1,0:T(8,128)(2,1)} %refs_4_.3), custom_call_target="tpu_custom_call" | custom-call | flops 8589934592 | bytes 4194304 | tf_op jit(solution)/shard_map/pallas_call | solution.py:289
  86.5 1.2 all-to-all-done.2
  87.7 6.0 %all-to-all-start.3 = ((bf16[16,128,128]{2,1,0:T(8,128)(2,1)}), bf16[16,128,128]{2,1,0:T(8,128)(2,1)S(1)}, u32[]{:S(2)}, u32[]{:S(2)}) async-start(bf16[16,128,128]{2,1,0:T(8,128)(2,1)} %bitcast.13), calls=%async_computation.3 | async-start | bytes 1048576 | tf_op jit(solution)/shard_map/all_to_all | solution.py:496
  93.8 0.1 collective-permute-start.5
  93.8 0.5 collective-permute-start.6
  94.3 0.1 collective-permute-start.2
  94.4 14.2 %all-to-all-done.3 = bf16[16,128,128]{2,1,0:T(8,128)(2,1)S(1)} async-done(((bf16[16,128,128]{2,1,0:T(8,128)(2,1)}), bf16[16,128,128]{2,1,0:T(8,128)(2,1)S(1)}, u32[]{:S(2)}, u32[]{:S(2)}) %all-to-all-start.3) | async-done | bytes 524320 | tf_op jit(solution)/shard_map/all_to_all | solution.py:496
  108.6 0.5 collective-permute-start.4
  109.1 4.0 %shard_map.94.first_hbm = bf16[1024,256]{1,0:T(8,128)(2,1)} custom-call(s32[1,2048]{1,0:T(1,128)} %bitcast.18, bf16[2048,128]{1,0:T(8,128)(2,1)} %bitcast.12, bf16[2048,128]{1,0:T(8,128)(2,1)} %collective-permute-done.2.other_hbm), custom_call_target="tpu_custom_call" | custom-call | flops 1073741824 | bytes 2097152 | tf_op jit(solution)/shard_map/pallas_call | solution.py:349
  113.2 0.6 copy-done.10
  113.8 0.2 copy-done.6
  114.0 14.5 %shard_map.96 = (bf16[1024,512]{1,0:T(8,128)(2,1)}, bf16[2048,512]{1,0:T(8,128)(2,1)}) custom-call(s32[1,2048]{1,0:T(1,128)} %bitcast.19, f32[1,512]{1,0:T(1,128)} %bitcast.21, bf16[2048,512]{1,0:T(8,128)(2,1)} %points_hbm.3, bf16[1024,256]{1,0:T(8,128)(2,1)} %shard_map.94.first_hbm, bf16[2048,128]{1,0:T(8,128)(2,1)} %bitcast.10, ...), custom_call_target="tpu_custom_call" | custom-call | flops 6979321856 | bytes 16777216 | tf_op jit(solution)/shard_map/pallas_call | solution.py:460
  128.5 0.1 collective-permute-start.7
  128.6 2.8 %collective-permute-done.7 = bf16[1024,512]{1,0:T(8,128)(2,1)S(1)} collective-permute-done((bf16[1024,512]{1,0:T(8,128)(2,1)}, bf16[1024,512]{1,0:T(8,128)(2,1)S(1)}, u32[]{:S(2)}, u32[]{:S(2)}) %collective-permute-start.7) | collective-permute-done | bytes 1048608 | tf_op jit(solution)/shard_map/ppermute | solution.py:490
  131.4 1.0 constant_dynamic-update-slice_fusion
  (28 shorter events, 0.1 us)
Async XLA Ops:
  33.1 20.2 %copy-start.2 = (bf16[16,64,256]{2,1,0:T(8,128)(2,1)}, bf16[16,64,256]{2,1,0:T(8,128)(2,1)S(1)}, u32[]{:S(2)}) copy-start(bf16[16,64,256]{2,1,0:T(8,128)(2,1)S(1)} %all_to_all.20.refs_1_) | copy-start | bytes 1572868
  33.1 18.3 %all-to-all-start = ((bf16[16,64,256]{2,1,0:T(8,128)(2,1)}), bf16[16,64,256]{2,1,0:T(8,128)(2,1)S(1)}, u32[]{:S(2)}, u32[]{:S(2)}) async-start(bf16[16,64,256]{2,1,0:T(8,128)(2,1)} %bitcast.3), calls=%async_computation | async-start | bytes 1048576 | tf_op jit(solution)/shard_map/all_to_all | solution.py:496
  37.0 14.4 %collective-permute-start.1 = (bf16[16,64,256]{2,1,0:T(8,128)(2,1)S(1)}, bf16[16,64,256]{2,1,0:T(8,128)(2,1)S(1)}, u32[]{:S(2)}, u32[]{:S(2)}) collective-permute-start(bf16[16,64,256]{2,1,0:T(8,128)(2,1)S(1)} %all_to_all.20.refs_1_), channel_id=1, source_target_pairs={{0,1},{1,0},{2,3},{3,2},{4,5},{5,4},{6,7},{7,6},{8,9},{9,8},{10,11... | collective-permute-start | bytes 1572872 | tf_op jit(solution)/shard_map/ppermute | solution.py:490
  51.5 1.9 %copy-start.3 = (bf16[16,64,256]{2,1,0:T(8,128)(2,1)}, bf16[16,64,256]{2,1,0:T(8,128)(2,1)S(1)}, u32[]{:S(2)}) copy-start(bf16[16,64,256]{2,1,0:T(8,128)(2,1)S(1)} %all-to-all-done.refs_0_) | copy-start | bytes 1572868
  51.5 1.9 %collective-permute-start = (bf16[16,64,256]{2,1,0:T(8,128)(2,1)S(1)}, bf16[16,64,256]{2,1,0:T(8,128)(2,1)S(1)}, u32[]{:S(2)}, u32[]{:S(2)}) collective-permute-start(bf16[16,64,256]{2,1,0:T(8,128)(2,1)S(1)} %all-to-all-done.refs_0_), channel_id=1, source_target_pairs={{0,1},{1,0},{2,3},{3,2},{4,5},{5,4},{6,7},{7,6},{8,9},{9,8},{10,11... | collective-permute-start | bytes 1572872 | tf_op jit(solution)/shard_map/ppermute | solution.py:490
  51.5 1.9 %copy-start.7 = (bf16[16,64,256]{2,1,0:T(8,128)(2,1)}, bf16[16,64,256]{2,1,0:T(8,128)(2,1)S(1)}, u32[]{:S(2)}) copy-start(bf16[16,64,256]{2,1,0:T(8,128)(2,1)S(1)} %collective-permute-done.1.refs_3_) | copy-start | bytes 1572868
  53.4 0.8 copy-start.8
  68.2 19.5 %all-to-all-start.2 = ((bf16[16,128,128]{2,1,0:T(8,128)(2,1)}), bf16[16,128,128]{2,1,0:T(8,128)(2,1)S(1)}, u32[]{:S(2)}, u32[]{:S(2)}) async-start(bf16[16,128,128]{2,1,0:T(8,128)(2,1)} %bitcast.14), calls=%async_computation.2 | async-start | bytes 1048576 | tf_op jit(solution)/shard_map/all_to_all | solution.py:496
  72.3 21.4 %copy-start.4 = (bf16[512,1024]{1,0:T(8,128)(2,1)S(1)}, bf16[512,1024]{1,0:T(8,128)(2,1)}, u32[]{:S(2)}) copy-start(bf16[512,1024]{1,0:T(8,128)(2,1)} %fc1_own_hbm.1) | copy-start | bytes 3145732
  72.3 21.5 %copy-start.5 = (bf16[1024,512]{1,0:T(8,128)(2,1)S(1)}, bf16[1024,512]{1,0:T(8,128)(2,1)}, u32[]{:S(2)}) copy-start(bf16[1024,512]{1,0:T(8,128)(2,1)} %fc2_own_hbm.1) | copy-start | bytes 3145732
  72.4 36.3 %copy-start.9 = (bf16[256,512]{1,0:T(8,128)(2,1)S(1)}, bf16[256,512]{1,0:T(8,128)(2,1)}, u32[]{:S(2)}) copy-start(bf16[256,512]{1,0:T(8,128)(2,1)} %out_own_hbm.1) | copy-start | bytes 786436
  87.7 21.4 %copy-start.1 = (bf16[16,128,128]{2,1,0:T(8,128)(2,1)}, bf16[16,128,128]{2,1,0:T(8,128)(2,1)S(1)}, u32[]{:S(2)}) copy-start(bf16[16,128,128]{2,1,0:T(8,128)(2,1)S(1)} %all-to-all-done.2) | copy-start | bytes 1572868
  87.7 20.9 %all-to-all-start.3 = ((bf16[16,128,128]{2,1,0:T(8,128)(2,1)}), bf16[16,128,128]{2,1,0:T(8,128)(2,1)S(1)}, u32[]{:S(2)}, u32[]{:S(2)}) async-start(bf16[16,128,128]{2,1,0:T(8,128)(2,1)} %bitcast.13), calls=%async_computation.3 | async-start | bytes 1048576 | tf_op jit(solution)/shard_map/all_to_all | solution.py:496
  93.8 19.4 %collective-permute-start.5 = (bf16[512,1024]{1,0:T(8,128)(2,1)S(1)}, bf16[512,1024]{1,0:T(8,128)(2,1)}, u32[]{:S(2)}, u32[]{:S(2)}) collective-permute-start(bf16[512,1024]{1,0:T(8,128)(2,1)S(1)} %copy-done.4), channel_id=1, source_target_pairs={{0,1},{1,0},{2,3},{3,2},{4,5},{5,4},{6,7},{7,6},{8,9},{9,8},{10,11... | collective-permute-start | bytes 3145736 | tf_op jit(solution)/shard_map/ppermute | solution.py:490
  93.8 19.3 %collective-permute-start.6 = (bf16[1024,512]{1,0:T(8,128)(2,1)S(1)}, bf16[1024,512]{1,0:T(8,128)(2,1)}, u32[]{:S(2)}, u32[]{:S(2)}) collective-permute-start(bf16[1024,512]{1,0:T(8,128)(2,1)S(1)} %copy-done.5), channel_id=1, source_target_pairs={{0,1},{1,0},{2,3},{3,2},{4,5},{5,4},{6,7},{7,6},{8,9},{9,8},{10,11... | collective-permute-start | bytes 3145736 | tf_op jit(solution)/shard_map/ppermute | solution.py:490
  94.3 14.8 %collective-permute-start.2 = (bf16[2048,128]{1,0:T(8,128)(2,1)S(1)}, bf16[2048,128]{1,0:T(8,128)(2,1)}, u32[]{:S(2)}, u32[]{:S(2)}) collective-permute-start(bf16[2048,128]{1,0:T(8,128)(2,1)S(1)} %bitcast.11), channel_id=1, source_target_pairs={{0,1},{1,0},{2,3},{3,2},{4,5},{5,4},{6,7},{7,6},{8,9},{9,8},{10,11... | collective-permute-start | bytes 1572872 | tf_op jit(solution)/shard_map/ppermute | solution.py:490
  108.6 4.6 %copy-start = (bf16[16,128,128]{2,1,0:T(8,128)(2,1)}, bf16[16,128,128]{2,1,0:T(8,128)(2,1)S(1)}, u32[]{:S(2)}) copy-start(bf16[16,128,128]{2,1,0:T(8,128)(2,1)S(1)} %all-to-all-done.3) | copy-start | bytes 1572868
  108.6 4.6 %collective-permute-start.3 = (bf16[2048,128]{1,0:T(8,128)(2,1)S(1)}, bf16[2048,128]{1,0:T(8,128)(2,1)S(1)}, u32[]{:S(2)}, u32[]{:S(2)}) collective-permute-start(bf16[2048,128]{1,0:T(8,128)(2,1)S(1)} %bitcast.9), channel_id=1, source_target_pairs={{0,1},{1,0},{2,3},{3,2},{4,5},{5,4},{6,7},{7,6},{8,9},{9,8},{10,11... | collective-permute-start | bytes 1572872 | tf_op jit(solution)/shard_map/ppermute | solution.py:490
  108.6 4.5 %collective-permute-start.4 = (bf16[256,512]{1,0:T(8,128)(2,1)S(1)}, bf16[256,512]{1,0:T(8,128)(2,1)S(1)}, u32[]{:S(2)}, u32[]{:S(2)}) collective-permute-start(bf16[256,512]{1,0:T(8,128)(2,1)S(1)} %copy-done.9), channel_id=1, source_target_pairs={{0,1},{1,0},{2,3},{3,2},{4,5},{5,4},{6,7},{7,6},{8,9},{9,8},{10,11... | collective-permute-start | bytes 786440 | tf_op jit(solution)/shard_map/ppermute | solution.py:490
  113.1 0.7 copy-start.10
  113.2 0.8 copy-start.6
  128.5 2.9 %collective-permute-start.7 = (bf16[1024,512]{1,0:T(8,128)(2,1)}, bf16[1024,512]{1,0:T(8,128)(2,1)S(1)}, u32[]{:S(2)}, u32[]{:S(2)}) collective-permute-start(bf16[1024,512]{1,0:T(8,128)(2,1)} %get-tuple-element.12), channel_id=1, source_target_pairs={{0,1},{1,0},{2,3},{3,2},{4,5},{5,4},{6,7},{7,6},{8,9},{9,8},{10,11... | collective-permute-start | bytes 3145736 | tf_op jit(solution)/shard_map/ppermute | solution.py:490

commit v2 on v0

v2 whole, which is shorter than its diff:
```python
import functools
import math

import jax
import jax.numpy as jnp
from jax import lax
from jax.experimental import pallas as pl
from jax.experimental.pallas import tpu as pltpu
from jax.sharding import PartitionSpec as P

HDIM = 64
LANES = 128
ROWS = 256
EPSILON = 1e-06
FAR = 1e30
VMEM_BYTES = 58 * 1024 * 1024

f32 = jnp.float32
bf16 = jnp.bfloat16

ANYWHERE = pl.BlockSpec(memory_space=pl.ANY)
SCALARS = pl.BlockSpec(memory_space=pltpu.SMEM)


def normalise(values, gain_row):
    average = jnp.mean(values, axis=-1, keepdims=True)
    centred = values - average
    second = jnp.mean(centred * centred, axis=-1, keepdims=True)
    return (centred * lax.rsqrt(second + EPSILON) * gain_row).astype(bf16)


def dot(left, right):
    return jnp.dot(left, right, preferred_element_type=f32)


def split(number, size):
    if size & (size - 1) == 0:
        return number >> (size.bit_length() - 1), number & (size - 1)
    return number // size, number % size


def slots(rank, length, shards):
    cell = length // shards
    owner, within = split(rank, length)
    return owner * cell + within - lax.axis_index("space") * cell


def one_hot(rows_at, columns_at):
    if columns_at.shape[1] <= 1 << 15:
        rows_at, columns_at = rows_at.astype(jnp.int16), columns_at.astype(jnp.int16)
    one, nil = jnp.ones((), bf16), jnp.zeros((), bf16)
    return jnp.concatenate(
        [
            jnp.where(rows_at == columns_at[:, k : k + LANES], one, nil)
            for k in range(0, columns_at.shape[1], LANES)
        ],
        axis=1,
    )


def blocks_of(length, rows=ROWS):
    return [slice(i * rows, (i + 1) * rows) for i in range(length // rows)]


def params():
    return pltpu.CompilerParams(vmem_limit_bytes=VMEM_BYTES)


def send_kernel(shards, rank_hbm, gain_hbm, points_hbm, out_ref, rank_ref, gain_ref, points_ref, half_ref, small, large):
    length, features = points_ref.shape
    half = features // 2
    core = lax.axis_index("mp")
    gain_copy = pltpu.make_async_copy(gain_hbm, gain_ref, small.at[0])
    rank_copy = pltpu.make_async_copy(rank_hbm, rank_ref, small.at[1])
    rows_of = blocks_of(length)
    copies = [
        pltpu.make_async_copy(points_hbm.at[rows], points_ref.at[rows], large.at[i])
        for i, rows in enumerate(rows_of)
    ]
    gain_copy.start()
    for copy in copies:
        copy.start()
    rank_copy.start()
    gain_copy.wait()
    for copy, rows in zip(copies, rows_of):
        copy.wait()
        normed = normalise(points_ref[rows, :].astype(f32), gain_ref[...])
        half_ref[rows, :] = jnp.where(core == 0, normed[:, :half], normed[:, half:])
    rank_copy.wait()
    slot = slots(rank_ref[...], length, shards)

    def order_block(i, carry):
        start = pl.multiple_of(i * ROWS, ROWS)
        place = lax.broadcasted_iota(jnp.int32, (ROWS, LANES), 0) + start
        out_ref[pl.ds(start, ROWS), :] = dot(one_hot(place, slot), half_ref[...]).astype(bf16)
        return carry

    lax.fori_loop(0, length // ROWS, order_block, 0)


def order_for_owners(shards, rank_row, gain_row, points):
    length, features = points.shape
    return pl.pallas_call(
        functools.partial(send_kernel, shards),
        out_shape=jax.ShapeDtypeStruct((length, features // 2), bf16),
        in_specs=[ANYWHERE] * 3,
        out_specs=pl.BlockSpec(memory_space=pltpu.VMEM),
        scratch_shapes=[
            pltpu.VMEM((1, length), jnp.int32),
            pltpu.VMEM((1, features), f32),
            pltpu.VMEM((length, features), bf16),
            pltpu.VMEM((length, features // 2), bf16),
            pltpu.SemaphoreType.DMA((2,)),
            pltpu.SemaphoreType.DMA((length // ROWS,)),
        ],
        compiler_params=params(),
        cost_estimate=pl.CostEstimate(
            flops=length * length * features, bytes_accessed=4 * length * features, transcendentals=0
        ),
    )(rank_row, gain_row, points)


def attend_kernel(
    pair,
    counts_ref,
    own_hbm,
    other_hbm,
    weight_hbm,
    out_hbm,
    x_ref,
    raw_ref,
    w_ref,
    q_ref,
    k_ref,
    v_ref,
    out_ref,
    x_sems,
    w_sems,
    out_sems,
):
    length, features = x_ref.shape
    half = features // 2
    tiles = counts_ref.shape[1]
    core = lax.axis_index("mp")
    scale = math.log2(math.e) / math.sqrt(HDIM)
    pair_columns = slice(pair * LANES, (pair + 1) * LANES)

    w_copies = [
        pltpu.make_async_copy(
            weight_hbm.at[:, pl.ds(pl.multiple_of(at * half, half), half), pair_columns],
            raw_ref.at[:, k * half : (k + 1) * half],
            w_sems.at[k],
        )
        for k, at in enumerate((core, 1 - core))
    ]
    x_copies = [
        [
            pltpu.make_async_copy(
                source.at[rows], x_ref.at[rows, k * half : (k + 1) * half], x_sems.at[2 * i + k]
            )
            for k, source in enumerate((own_hbm, other_hbm))
        ]
        for i, rows in enumerate(blocks_of(length, 2 * ROWS))
    ]
    for copy in w_copies + sum(x_copies, []):
        copy.start()

    starts = [jnp.int32(0)]
    for t in range(tiles):
        starts.append(starts[-1] + counts_ref[0, t])
    lane = lax.broadcasted_iota(jnp.int32, (1, LANES), 1)
    first = jnp.full((1, LANES), length, jnp.int32)
    last = jnp.zeros((1, LANES), jnp.int32)
    for t in range(tiles):
        first = jnp.where(lane == HDIM + t, starts[t], first)
        last = jnp.where(lane == HDIM + t, starts[t + 1], last)
    flags = jnp.logical_and(lane >= HDIM, lane < HDIM + tiles)
    low_lanes = lane < HDIM

    for copy in w_copies:
        copy.wait()
    for j in range(3):
        both = raw_ref[j].astype(f32)
        at = 2 * j * LANES
        w_ref[:, at : at + LANES] = jnp.where(low_lanes, both, 0.0).astype(bf16)
        odd = jnp.where(low_lanes, pltpu.roll(both, HDIM, 1), 0.0) if j < 2 else jnp.where(low_lanes, 0.0, both)
        w_ref[:, at + LANES : at + 2 * LANES] = odd.astype(bf16)

    def project(i, carry):
        rows = pl.ds(pl.multiple_of(i * ROWS, ROWS), ROWS)
        block = x_ref[rows, :]
        place = lax.broadcasted_iota(jnp.int32, (ROWS, LANES), 0) + i * ROWS
        inside = jnp.logical_and(place >= first, place < last)
        q_flag = jnp.where(inside, 1.0, 0.0)
        k_flag = jnp.where(jnp.logical_and(flags, jnp.logical_not(inside)), -FAR, 0.0)
        spread = dot(block, w_ref[...])
        for h in range(2):
            q, k, v = (spread[:, (2 * j + h) * LANES : (2 * j + h + 1) * LANES] for j in range(3))
            q_ref[h, rows, :] = (q * scale + q_flag).astype(bf16)
            k_ref[h, rows, :] = (k + k_flag).astype(bf16)
            ones = jnp.logical_not(low_lanes) if h == 0 else low_lanes
            v_ref[h, rows, :] = (v + jnp.where(ones, 1.0, 0.0)).astype(bf16)
        return carry

    for i, copies in enumerate(x_copies):
        for copy in copies:
            copy.wait()
        lax.fori_loop(2 * i, 2 * i + 2, project, 0)

    def raise_scores(scores):
        return jnp.exp2(scores - jnp.max(scores, axis=1, keepdims=True)).astype(bf16)

    def send_out(i):
        rows = pl.ds(pl.multiple_of(i * ROWS, ROWS), ROWS)
        return pltpu.make_async_copy(out_ref.at[rows], out_hbm.at[rows], out_sems.at[i])

    def query_block(i, carry):
        begin = i * ROWS
        rows = pl.ds(pl.multiple_of(begin, ROWS), ROWS)
        low, high = jnp.int32(0), jnp.int32(length)
        for t in range(tiles):
            low = jnp.where(starts[t] <= begin, starts[t], low)
            end = starts[tiles - t]
            high = jnp.where(end >= begin + ROWS, end, high)
        low = (low // 16) * 16
        blocks = (high - low + ROWS - 1) // ROWS
        for n in range(1, length // ROWS + 1):

            @pl.when(blocks == n)
            def _(n=n):
                start = jnp.minimum(low, length - n * ROWS)
                keys = pl.ds(pl.multiple_of(start, 16), n * ROWS)
                scores = [
                    lax.dot_general(
                        q_ref[h, rows, :],
                        k_ref[h, keys, :],
                        (((1,), (1,)), ((), ())),
                        preferred_element_type=f32,
                    )
                    for h in range(2)
                ]
                even = dot(raise_scores(scores[0]), v_ref[0, keys, :])
                odd = dot(raise_scores(scores[1]), v_ref[1, keys, :])
                total = pltpu.roll(jnp.where(low_lanes, odd, even), HDIM, 1)
                out_ref[rows, :] = (jnp.where(low_lanes, even, odd) / total).astype(bf16)

        send_out(i).start()
        return carry

    lax.fori_loop(0, length // ROWS, query_block, 0)
    for i in range(length // ROWS):
        send_out(i).wait()


def attend(pair, counts, own, other, w_qkv):
    length, half = own.shape
    features = 2 * half
    return pl.pallas_call(
        functools.partial(attend_kernel, pair),
        out_shape=jax.ShapeDtypeStruct((length, LANES), bf16),
        in_specs=[SCALARS] + [ANYWHERE] * 3,
        out_specs=ANYWHERE,
        scratch_shapes=[
            pltpu.VMEM((length, features), bf16),
            pltpu.VMEM((3, features, LANES), bf16),
            pltpu.VMEM((features, 6 * LANES), bf16),
            pltpu.VMEM((2, length, LANES), bf16),
            pltpu.VMEM((2, length, LANES), bf16),
            pltpu.VMEM((2, length, LANES), bf16),
            pltpu.VMEM((length, LANES), bf16),
            pltpu.SemaphoreType.DMA((length // ROWS,)),
            pltpu.SemaphoreType.DMA((2,)),
            pltpu.SemaphoreType.DMA((length // ROWS,)),
        ],
        compiler_params=params(),
        cost_estimate=pl.CostEstimate(
            flops=32 * length * length * HDIM, bytes_accessed=8 * length * half, transcendentals=2 * length * length
        ),
    )(counts, own, other, w_qkv)


def gelu_of_half(h):
    inner = 2 * math.sqrt(2 / math.pi)
    return h + h * jnp.tanh(h * (inner + (4 * 0.044715 * inner) * (h * h)))


def finish_kernel(
    shards,
    rank_hbm,
    gain_hbm,
    points_hbm,
    own_a_hbm,
    other_a_hbm,
    own_b_hbm,
    other_b_hbm,
    out_own_hbm,
    out_other_hbm,
    fc1_own_hbm,
    fc1_other_hbm,
    fc2_own_hbm,
    fc2_other_hbm,
    done_ref,
    whole_hbm,
    rank_ref,
    gain_ref,
    points_ref,
    context_ref,
    out_ref,
    fc1_ref,
    fc2_ref,
    middle_ref,
    normed_ref,
    in_sems,
    sems,
):
    length = context_ref.shape[0]
    half_rows = done_ref.shape[0]
    base = pl.multiple_of(lax.axis_index("mp") * half_rows, half_rows)
    half = out_own_hbm.shape[0]
    hidden_half = fc2_own_hbm.shape[0]
    early = [
        (rank_hbm, rank_ref),
        (own_a_hbm, context_ref.at[:, :LANES]),
        (own_b_hbm, context_ref.at[:, LANES : 2 * LANES]),
        (other_a_hbm, context_ref.at[:, 2 * LANES : 3 * LANES]),
        (other_b_hbm, context_ref.at[:, 3 * LANES :]),
    ]
    later = [
        (out_own_hbm, out_ref.at[:half]),
        (out_other_hbm, out_ref.at[half:]),
        (gain_hbm, gain_ref),
        (points_hbm.at[pl.ds(base, half_rows)], points_ref),
    ]
    last = [
        (fc1_own_hbm, fc1_ref.at[:, :hidden_half]),
        (fc1_other_hbm, fc1_ref.at[:, hidden_half:]),
        (fc2_own_hbm, fc2_ref.at[:hidden_half]),
        (fc2_other_hbm, fc2_ref.at[hidden_half:]),
    ]
    copies = [pltpu.make_async_copy(*ends, in_sems.at[k]) for k, ends in enumerate(early + later + last)]
    early, later, last = copies[:5], copies[5:9], copies[9:]
    for copy in copies:
        copy.start()

    def here(i):
        return pl.ds(pl.multiple_of(i * ROWS, ROWS), ROWS)

    def attend_out(i):
        start = pl.multiple_of(base + i * ROWS, ROWS)
        slot = slots(rank_ref[:, pl.ds(start, ROWS)], length, shards)
        slot = jnp.transpose(jnp.broadcast_to(slot, (LANES, ROWS)))
        place = lax.broadcasted_iota(jnp.int32, (1, length), 1)
        context = dot(one_hot(slot, place), context_ref[...]).astype(bf16)
        return context

    def residual(i, context):
        attn_out = dot(context, out_ref[...]).astype(bf16).astype(f32)
        middle = (points_ref[here(i), :].astype(f32) + attn_out).astype(bf16)
        middle_ref[here(i), :] = middle
        normed_ref[here(i), :] = normalise(middle.astype(f32), gain_ref[...]) * 0.5

    for copy in early:
        copy.wait()
    context = attend_out(0)
    for copy in later:
        copy.wait()
    residual(0, context)

    def rest(i, carry):
        residual(i, attend_out(i))
        return carry

    lax.fori_loop(1, half_rows // ROWS, rest, 0)
    for copy in last:
        copy.wait()

    def away(i):
        there = pl.multiple_of(base + i * ROWS, ROWS)
        return pltpu.make_async_copy(done_ref.at[here(i)], whole_hbm.at[pl.ds(there, ROWS)], sems.at[i])

    chunks = blocks_of(2 * hidden_half, 2 * ROWS)

    def mlp(i, carry):
        normed = normed_ref[here(i), :]
        total = middle_ref[here(i), :].astype(f32)
        half_hidden = dot(normed, fc1_ref[:, chunks[0]])
        for k, chunk in enumerate(chunks):
            ahead = dot(normed, fc1_ref[:, chunks[k + 1]]) if k + 1 < len(chunks) else None
            total = total + dot(gelu_of_half(half_hidden).astype(bf16), fc2_ref[chunk, :])
            half_hidden = ahead
        done_ref[here(i), :] = total.astype(bf16)
        away(i).start()
        return carry

    lax.fori_loop(0, half_rows // ROWS, mlp, 0)
    for i in range(half_rows // ROWS):
        away(i).wait()


def finish(shards, rank_row, gain_row, points, *arrays):
    length, features = points.shape
    half_rows = length // 2
    hidden = 2 * arrays[-1].shape[0]
    return pl.pallas_call(
        functools.partial(finish_kernel, shards),
        out_shape=(
            jax.ShapeDtypeStruct((half_rows, features), bf16),
            jax.ShapeDtypeStruct((length, features), bf16),
        ),
        in_specs=[ANYWHERE] * 13,
        out_specs=(pl.BlockSpec(memory_space=pltpu.VMEM), ANYWHERE),
        scratch_shapes=[
            pltpu.VMEM((1, length), jnp.int32),
            pltpu.VMEM((1, features), f32),
            pltpu.VMEM((half_rows, features), bf16),
            pltpu.VMEM((length, features), bf16),
            pltpu.VMEM((features, features), bf16),
            pltpu.VMEM((features, hidden), bf16),
            pltpu.VMEM((hidden, features), bf16),
            pltpu.VMEM((half_rows, features), bf16),
            pltpu.VMEM((half_rows, features), bf16),
            pltpu.SemaphoreType.DMA((13,)),
            pltpu.SemaphoreType.DMA((half_rows // ROWS,)),
        ],
        compiler_params=params(),
        cost_estimate=pl.CostEstimate(
            flops=2 * half_rows * features * (length + 9 * features),
            bytes_accessed=16 * length * features,
            transcendentals=half_rows * 4 * features,
        ),
    )(rank_row, gain_row, points, *arrays)


def across(values):
    return lax.ppermute(values, "mp", [(0, 1), (1, 0)])


def exchange(rows, shards):
    length, columns = rows.shape
    cells = rows.reshape(shards, length // shards, columns)
    return lax.all_to_all(cells, "space", split_axis=0, concat_axis=0, tiled=True).reshape(length, columns)


def body(points, curve_rank, patch_counts, norm_gain_attn, w_qkv, w_out, norm_gain_mlp, w_fc1, w_fc2):
    shards = lax.axis_size("space")
    length, features = points.shape
    rank_row = curve_rank.reshape(1, length)
    own = exchange(order_for_owners(shards, rank_row, norm_gain_attn.reshape(1, features), points), shards)
    mlp = w_fc1, across(w_fc1), w_fc2, across(w_fc2)
    other_out = across(w_out)
    other = across(own)
    returned = [exchange(attend(pair, patch_counts, own, other, w_qkv), shards) for pair in range(2)]
    context = [rows for own_rows in returned for rows in (own_rows, across(own_rows))]
    done, whole = finish(
        shards, rank_row, norm_gain_mlp.reshape(1, features), points, *context, w_out, other_out, *mlp
    )
    start = (1 - lax.axis_index("mp")) * (length // 2)
    return lax.dynamic_update_slice(whole, across(done), (start, 0))


def solution(mesh):
    placed = (
        P("space", None),
        P("space"),
        P("space", None),
        P(),
        P(None, None, "mp"),
        P("mp", None),
        P(),
        P(None, "mp"),
        P("mp", None),
    )
    return jax.shard_map(
        body, mesh=mesh, in_specs=placed, out_specs=P("space", None), check_vma=False
    )
```

time: 124 us -> 120 us (0.968)
  local copies, waits for them, and re-layouts: 6.19 us -> 2.89 us
  starting transfers between devices: 11.8 us -> 9.68 us
  Pallas kernels: 48.1 us -> 49.8 us
    unnamed x24 -> x18, local copies, waits for them, and re-layouts: 6.19 us -> 1.85 us
    pallas_call x2, Pallas kernels: 25 us -> 27.9 us  [attend(): pl.pallas_call(functools.partial(attend_kernel, pair), out_shape=jax.Shap...]
    pallas_call x1 -> x0, Pallas kernels: 2.2 us -> none  [join(): pl.pallas_call(join_kernel, out_shape=jax.ShapeDtypeStruct(whole.shape, w...]
    all_to_all x2, starting transfers between devices: 10.5 us -> 8.33 us  [exchange(): lax.all_to_all(cells, 'space', split_axis=0, concat_axis=0, tiled=True)]
  transfers between devices with their start and end apart: 9 -> 9, of which waited for: 5 -> 5; matrix products, arithmetic and copies ran while one was open for 0% -> 0% of each run, Pallas kernels for 10% -> 12%
where the time goes in v2:
time: 120 us
  Pallas kernels  49.8 us (42%)
  blocking collectives  34.7 us (29%)
  waiting for transfers between devices  22.8 us (19%)
  starting transfers between devices  9.68 us (8%)
  local copies, waits for them, and re-layouts  2.89 us (2%)
    all_to_all x1, blocking collectives, exchange(): lax.all_to_all(cells, 'space', split_axis=0, concat_axis=0, tiled=True)  34.7 us
    pallas_call x2, Pallas kernels, attend(): pl.pallas_call(functools.partial(attend_kernel, pair), out_shape=jax.Shap...  27.9 us
    all_to_all x2, waiting for transfers between devices, exchange(): lax.all_to_all(cells, 'space', split_axis=0, concat_axis=0, tiled=True)  15.6 us
    pallas_call x1, Pallas kernels, finish(): pl.pallas_call(functools.partial(finish_kernel, shards), out_shape=(jax.S...  14.2 us
    all_to_all x2, starting transfers between devices, exchange(): lax.all_to_all(cells, 'space', split_axis=0, concat_axis=0, tiled=True)  8.33 us
    pallas_call x1, Pallas kernels, order_for_owners(): pl.pallas_call(functools.partial(send_kernel, shards), out_shape=jax.Shap...  7.74 us
    ppermute x7, waiting for transfers between devices, across(): return lax.ppermute(values, 'mp', [(0, 1), (1, 0)])  7.18 us
  transfers between devices with their start and end apart: 9, of which 5 were waited for; matrix products, arithmetic and copies ran while one was open for 0% of the time, Pallas kernels for 12%

profile of v2, /device:TPU:0, one launch (start us, length us, event | category | flops | bytes accessed | tf_op | source)
XLA Modules:
  0.0 120.1 jit_solution(15159210385660517075)
XLA Ops:
  0.0 7.7 %shard_map.91 = bf16[2048,256]{1,0:T(8,128)(2,1)} custom-call(s32[1,2048]{1,0:T(1,128)} %bitcast.19, f32[1,512]{1,0:T(1,128)} %bitcast.21, bf16[2048,512]{1,0:T(8,128)(2,1)} %points_hbm.3), custom_call_target="tpu_custom_call" | custom-call | flops 2147483648 | bytes 4194304 | tf_op jit(solution)/shard_map/pallas_call | solution.py:103
  7.7 34.7 %all_to_all.15 = bf16[16,128,256]{2,1,0:T(8,128)(2,1)S(1)} all-to-all(bf16[16,128,256]{2,1,0:T(8,128)(2,1)} %bitcast.12), channel_id=1, replica_groups=mesh['space'=16,'mp'=2] {'space'}, dimensions={0} | all-to-all | bytes 2097152 | tf_op jit(solution)/shard_map/all_to_all | solution.py:441
  42.5 2.7 %collective-permute-done.other_hbm = bf16[2048,256]{1,0:T(8,128)(2,1)S(1)} collective-permute-done((bf16[2048,256]{1,0:T(8,128)(2,1)S(1)}, bf16[2048,256]{1,0:T(8,128)(2,1)S(1)}, u32[]{:S(2)}, u32[]{:S(2)}) %collective-permute-start) | collective-permute-done | bytes 1048608 | tf_op jit(solution)/shard_map/ppermute | solution.py:435
  45.1 1.0 copy-done.5
  46.1 13.9 %shard_map.93 = bf16[2048,128]{1,0:T(8,128)(2,1)} custom-call(s32[1,4]{1,0:T(1,128)} %counts_ref.3, bf16[2048,256]{1,0:T(8,128)(2,1)} %bitcast.10, bf16[2048,256]{1,0:T(8,128)(2,1)} %copy-done.5, bf16[3,512,256]{2,1,0:T(8,128)(2,1)} %weight_hbm.3), custom_call_target="tpu_custom_call" | custom-call | flops 8589934592 | bytes 4194304 | tf_op jit(solution)/shard_map/pallas_call | solution.py:258
  60.0 3.8 %all-to-all-start.2 = ((bf16[16,128,128]{2,1,0:T(8,128)(2,1)}), bf16[16,128,128]{2,1,0:T(8,128)(2,1)S(1)}, u32[]{:S(2)}, u32[]{:S(2)}) async-start(bf16[16,128,128]{2,1,0:T(8,128)(2,1)} %bitcast.18), calls=%async_computation.2 | async-start | bytes 1048576 | tf_op jit(solution)/shard_map/all_to_all | solution.py:441
  63.8 0.0 copy-start.3
  63.8 0.0 copy-start.4
  63.8 0.0 copy-start.7
  63.8 14.0 %shard_map.92 = bf16[2048,128]{1,0:T(8,128)(2,1)} custom-call(s32[1,4]{1,0:T(1,128)} %counts_ref.3, bf16[2048,256]{1,0:T(8,128)(2,1)} %bitcast.11, bf16[2048,256]{1,0:T(8,128)(2,1)} %copy-done.5, bf16[3,512,256]{2,1,0:T(8,128)(2,1)} %weight_hbm.3), custom_call_target="tpu_custom_call" | custom-call | flops 8589934592 | bytes 4194304 | tf_op jit(solution)/shard_map/pallas_call | solution.py:258
  77.8 1.2 all-to-all-done.2
  79.0 4.6 %all-to-all-start.1 = ((bf16[16,128,128]{2,1,0:T(8,128)(2,1)}), bf16[16,128,128]{2,1,0:T(8,128)(2,1)S(1)}, u32[]{:S(2)}, u32[]{:S(2)}) async-start(bf16[16,128,128]{2,1,0:T(8,128)(2,1)} %bitcast.17), calls=%async_computation.1 | async-start | bytes 1048576 | tf_op jit(solution)/shard_map/all_to_all | solution.py:441
  83.6 0.1 collective-permute-start.4
  83.7 0.5 collective-permute-start.5
  84.2 0.1 collective-permute-start.2
  84.3 14.5 %all-to-all-done.1 = bf16[16,128,128]{2,1,0:T(8,128)(2,1)S(1)} async-done(((bf16[16,128,128]{2,1,0:T(8,128)(2,1)}), bf16[16,128,128]{2,1,0:T(8,128)(2,1)S(1)}, u32[]{:S(2)}, u32[]{:S(2)}) %all-to-all-start.1) | async-done | bytes 524320 | tf_op jit(solution)/shard_map/all_to_all | solution.py:441
  98.8 0.5 collective-permute-start.3
  99.3 1.8 %collective-permute-done.3.out_other_hbm = bf16[256,512]{1,0:T(8,128)(2,1)S(1)} collective-permute-done((bf16[256,512]{1,0:T(8,128)(2,1)S(1)}, bf16[256,512]{1,0:T(8,128)(2,1)S(1)}, u32[]{:S(2)}, u32[]{:S(2)}) %collective-permute-start.3) | collective-permute-done | bytes 262176 | tf_op jit(solution)/shard_map/ppermute | solution.py:435
  101.1 0.6 copy-done.8
  101.7 0.2 copy-done.6
  101.9 14.2 %shard_map.94 = (bf16[1024,512]{1,0:T(8,128)(2,1)}, bf16[2048,512]{1,0:T(8,128)(2,1)}) custom-call(s32[1,2048]{1,0:T(1,128)} %bitcast.20, f32[1,512]{1,0:T(1,128)} %bitcast.22, bf16[2048,512]{1,0:T(8,128)(2,1)} %points_hbm.3, bf16[2048,128]{1,0:T(8,128)(2,1)} %bitcast.16, bf16[2048,128]{1,0:T(8,128)(2,1)} %copy-done.6, bf16[2048,128]{1,0:T(8,128)(2,1)} %bitcast.14, ...), custom_call_target="tpu_custom_call" | custom-call | flops 6979321856 | bytes 16777216 | tf_op jit(solution)/shard_map/pallas_call | solution.py:404
  116.1 0.2 collective-permute-start.6
  116.3 2.7 %collective-permute-done.6 = bf16[1024,512]{1,0:T(8,128)(2,1)S(1)} collective-permute-done((bf16[1024,512]{1,0:T(8,128)(2,1)}, bf16[1024,512]{1,0:T(8,128)(2,1)S(1)}, u32[]{:S(2)}, u32[]{:S(2)}) %collective-permute-start.6) | collective-permute-done | bytes 1048608 | tf_op jit(solution)/shard_map/ppermute | solution.py:435
  119.1 1.0 constant_dynamic-update-slice_fusion
  (18 shorter events, 0.0 us)
Async XLA Ops:
  42.4 2.7 %copy-start = (bf16[16,128,256]{2,1,0:T(8,128)(2,1)}, bf16[16,128,256]{2,1,0:T(8,128)(2,1)S(1)}, u32[]{:S(2)}) copy-start(bf16[16,128,256]{2,1,0:T(8,128)(2,1)S(1)} %all_to_all.15) | copy-start | bytes 3145732
  42.4 2.7 %collective-permute-start = (bf16[2048,256]{1,0:T(8,128)(2,1)S(1)}, bf16[2048,256]{1,0:T(8,128)(2,1)S(1)}, u32[]{:S(2)}, u32[]{:S(2)}) collective-permute-start(bf16[2048,256]{1,0:T(8,128)(2,1)S(1)} %bitcast.9), channel_id=1, source_target_pairs={{0,1},{1,0},{2,3},{3,2},{4,5},{5,4},{6,7},{7,6},{8,9},{9,8},{10,11... | collective-permute-start | bytes 3145736 | tf_op jit(solution)/shard_map/ppermute | solution.py:435
  45.1 1.0 copy-start.5
  60.0 19.0 %all-to-all-start.2 = ((bf16[16,128,128]{2,1,0:T(8,128)(2,1)}), bf16[16,128,128]{2,1,0:T(8,128)(2,1)S(1)}, u32[]{:S(2)}, u32[]{:S(2)}) async-start(bf16[16,128,128]{2,1,0:T(8,128)(2,1)} %bitcast.18), calls=%async_computation.2 | async-start | bytes 1048576 | tf_op jit(solution)/shard_map/all_to_all | solution.py:441
  63.8 19.8 %copy-start.3 = (bf16[512,1024]{1,0:T(8,128)(2,1)S(1)}, bf16[512,1024]{1,0:T(8,128)(2,1)}, u32[]{:S(2)}) copy-start(bf16[512,1024]{1,0:T(8,128)(2,1)} %fc1_own_hbm.1) | copy-start | bytes 3145732
  63.8 19.9 %copy-start.4 = (bf16[1024,512]{1,0:T(8,128)(2,1)S(1)}, bf16[1024,512]{1,0:T(8,128)(2,1)}, u32[]{:S(2)}) copy-start(bf16[1024,512]{1,0:T(8,128)(2,1)} %fc2_own_hbm.1) | copy-start | bytes 3145732
  63.8 35.0 %copy-start.7 = (bf16[256,512]{1,0:T(8,128)(2,1)S(1)}, bf16[256,512]{1,0:T(8,128)(2,1)}, u32[]{:S(2)}) copy-start(bf16[256,512]{1,0:T(8,128)(2,1)} %out_own_hbm.1) | copy-start | bytes 786436
  79.0 22.1 %copy-start.1 = (bf16[16,128,128]{2,1,0:T(8,128)(2,1)}, bf16[16,128,128]{2,1,0:T(8,128)(2,1)S(1)}, u32[]{:S(2)}) copy-start(bf16[16,128,128]{2,1,0:T(8,128)(2,1)S(1)} %all-to-all-done.2) | copy-start | bytes 1572868
  79.0 19.7 %all-to-all-start.1 = ((bf16[16,128,128]{2,1,0:T(8,128)(2,1)}), bf16[16,128,128]{2,1,0:T(8,128)(2,1)S(1)}, u32[]{:S(2)}, u32[]{:S(2)}) async-start(bf16[16,128,128]{2,1,0:T(8,128)(2,1)} %bitcast.17), calls=%async_computation.1 | async-start | bytes 1048576 | tf_op jit(solution)/shard_map/all_to_all | solution.py:441
  83.6 17.4 %collective-permute-start.4 = (bf16[512,1024]{1,0:T(8,128)(2,1)S(1)}, bf16[512,1024]{1,0:T(8,128)(2,1)}, u32[]{:S(2)}, u32[]{:S(2)}) collective-permute-start(bf16[512,1024]{1,0:T(8,128)(2,1)S(1)} %copy-done.3), channel_id=1, source_target_pairs={{0,1},{1,0},{2,3},{3,2},{4,5},{5,4},{6,7},{7,6},{8,9},{9,8},{10,11... | collective-permute-start | bytes 3145736 | tf_op jit(solution)/shard_map/ppermute | solution.py:435
  83.7 17.4 %collective-permute-start.5 = (bf16[1024,512]{1,0:T(8,128)(2,1)S(1)}, bf16[1024,512]{1,0:T(8,128)(2,1)}, u32[]{:S(2)}, u32[]{:S(2)}) collective-permute-start(bf16[1024,512]{1,0:T(8,128)(2,1)S(1)} %copy-done.4), channel_id=1, source_target_pairs={{0,1},{1,0},{2,3},{3,2},{4,5},{5,4},{6,7},{7,6},{8,9},{9,8},{10,11... | collective-permute-start | bytes 3145736 | tf_op jit(solution)/shard_map/ppermute | solution.py:435
  84.2 16.9 %collective-permute-start.2 = (bf16[2048,128]{1,0:T(8,128)(2,1)S(1)}, bf16[2048,128]{1,0:T(8,128)(2,1)}, u32[]{:S(2)}, u32[]{:S(2)}) collective-permute-start(bf16[2048,128]{1,0:T(8,128)(2,1)S(1)} %bitcast.13), channel_id=1, source_target_pairs={{0,1},{1,0},{2,3},{3,2},{4,5},{5,4},{6,7},{7,6},{8,9},{9,8},{10,11... | collective-permute-start | bytes 1572872 | tf_op jit(solution)/shard_map/ppermute | solution.py:435
  98.7 2.3 %copy-start.2 = (bf16[16,128,128]{2,1,0:T(8,128)(2,1)}, bf16[16,128,128]{2,1,0:T(8,128)(2,1)S(1)}, u32[]{:S(2)}) copy-start(bf16[16,128,128]{2,1,0:T(8,128)(2,1)S(1)} %all-to-all-done.1) | copy-start | bytes 1572868
  98.7 2.3 %collective-permute-start.1 = (bf16[2048,128]{1,0:T(8,128)(2,1)S(1)}, bf16[2048,128]{1,0:T(8,128)(2,1)S(1)}, u32[]{:S(2)}, u32[]{:S(2)}) collective-permute-start(bf16[2048,128]{1,0:T(8,128)(2,1)S(1)} %bitcast.15), channel_id=1, source_target_pairs={{0,1},{1,0},{2,3},{3,2},{4,5},{5,4},{6,7},{7,6},{8,9},{9,8},{10,11... | collective-permute-start | bytes 1572872 | tf_op jit(solution)/shard_map/ppermute | solution.py:435
  98.8 2.3 %collective-permute-start.3 = (bf16[256,512]{1,0:T(8,128)(2,1)S(1)}, bf16[256,512]{1,0:T(8,128)(2,1)S(1)}, u32[]{:S(2)}, u32[]{:S(2)}) collective-permute-start(bf16[256,512]{1,0:T(8,128)(2,1)S(1)} %copy-done.7), channel_id=1, source_target_pairs={{0,1},{1,0},{2,3},{3,2},{4,5},{5,4},{6,7},{7,6},{8,9},{9,8},{10,11... | collective-permute-start | bytes 786440 | tf_op jit(solution)/shard_map/ppermute | solution.py:435
  101.0 0.7 copy-start.8
  101.1 0.9 copy-start.6
  116.1 2.9 %collective-permute-start.6 = (bf16[1024,512]{1,0:T(8,128)(2,1)}, bf16[1024,512]{1,0:T(8,128)(2,1)S(1)}, u32[]{:S(2)}, u32[]{:S(2)}) collective-permute-start(bf16[1024,512]{1,0:T(8,128)(2,1)} %get-tuple-element.8), channel_id=1, source_target_pairs={{0,1},{1,0},{2,3},{3,2},{4,5},{5,4},{6,7},{7,6},{8,9},{9,8},{10,11... | collective-permute-start | bytes 3145736 | tf_op jit(solution)/shard_map/ppermute | solution.py:435

commit v3 on v2

v3 whole, which is shorter than its diff:
```python
import functools
import math

import jax
import jax.numpy as jnp
from jax import lax
from jax.experimental import pallas as pl
from jax.experimental.pallas import tpu as pltpu
from jax.sharding import PartitionSpec as P

HDIM = 64
LANES = 128
ROWS = 256
TALL = 512
KEYS = 256
EPSILON = 1e-06
FAR = 1e30
VMEM_BYTES = 58 * 1024 * 1024
SMALL_BYTES = 30 * 1024 * 1024

f32 = jnp.float32
bf16 = jnp.bfloat16

ANYWHERE = pl.BlockSpec(memory_space=pl.ANY)
SCALARS = pl.BlockSpec(memory_space=pltpu.SMEM)


def normalise(values, gain_row):
    average = jnp.mean(values, axis=-1, keepdims=True)
    centred = values - average
    second = jnp.mean(centred * centred, axis=-1, keepdims=True)
    return (centred * lax.rsqrt(second + EPSILON) * gain_row).astype(bf16)


def dot(left, right):
    return jnp.dot(left, right, preferred_element_type=f32)


def split(number, size):
    if size & (size - 1) == 0:
        return number >> (size.bit_length() - 1), number & (size - 1)
    return number // size, number % size


def slots(rank, length, shards):
    cell = length // shards
    owner, within = split(rank, length)
    return owner * cell + within - lax.axis_index("space") * cell


def one_hot(rows_at, columns_at):
    if columns_at.shape[1] <= 1 << 15:
        rows_at, columns_at = rows_at.astype(jnp.int16), columns_at.astype(jnp.int16)
    one, nil = jnp.ones((), bf16), jnp.zeros((), bf16)
    return jnp.concatenate(
        [
            jnp.where(rows_at == columns_at[:, k : k + LANES], one, nil)
            for k in range(0, columns_at.shape[1], LANES)
        ],
        axis=1,
    )


def blocks_of(length, rows=ROWS):
    return [slice(i * rows, (i + 1) * rows) for i in range(length // rows)]


def params(limit=VMEM_BYTES):
    return pltpu.CompilerParams(vmem_limit_bytes=limit)


def send_kernel(shards, rank_hbm, gain_hbm, points_hbm, out_ref, rank_ref, gain_ref, points_ref, half_ref, small, large):
    length, features = points_ref.shape
    half = features // 2
    core = lax.axis_index("mp")
    gain_copy = pltpu.make_async_copy(gain_hbm, gain_ref, small.at[0])
    rank_copy = pltpu.make_async_copy(rank_hbm, rank_ref, small.at[1])
    rows_of = blocks_of(length)
    copies = [
        pltpu.make_async_copy(points_hbm.at[rows], points_ref.at[rows], large.at[i])
        for i, rows in enumerate(rows_of)
    ]
    gain_copy.start()
    for copy in copies:
        copy.start()
    rank_copy.start()
    gain_copy.wait()
    for copy, rows in zip(copies, rows_of):
        copy.wait()
        normed = normalise(points_ref[rows, :].astype(f32), gain_ref[...])
        half_ref[rows, :] = jnp.where(core == 0, normed[:, :half], normed[:, half:])
    rank_copy.wait()
    slot = slots(rank_ref[...], length, shards)

    place = lax.broadcasted_iota(jnp.int32, (TALL, LANES), 0)
    for i, rows in enumerate(blocks_of(length, TALL)):
        out_ref[rows, :] = dot(one_hot(place + i * TALL, slot), half_ref[...]).astype(bf16)


def order_for_owners(shards, rank_row, gain_row, points):
    length, features = points.shape
    return pl.pallas_call(
        functools.partial(send_kernel, shards),
        out_shape=jax.ShapeDtypeStruct((length, features // 2), bf16),
        in_specs=[ANYWHERE] * 3,
        out_specs=pl.BlockSpec(memory_space=pltpu.VMEM),
        scratch_shapes=[
            pltpu.VMEM((1, length), jnp.int32),
            pltpu.VMEM((1, features), f32),
            pltpu.VMEM((length, features), bf16),
            pltpu.VMEM((length, features // 2), bf16),
            pltpu.SemaphoreType.DMA((2,)),
            pltpu.SemaphoreType.DMA((length // ROWS,)),
        ],
        compiler_params=params(),
        cost_estimate=pl.CostEstimate(
            flops=length * length * features, bytes_accessed=4 * length * features, transcendentals=0
        ),
    )(rank_row, gain_row, points)


def attend_kernel(
    pair,
    staged,
    counts_ref,
    own,
    other,
    weight_hbm,
    out_hbm,
    w_ref,
    q_ref,
    k_ref,
    v_ref,
    out_ref,
    w_sems,
    out_sems,
    x_ref=None,
    x_sems=None,
):
    length = out_ref.shape[0]
    features = w_ref.shape[0]
    half = features // 2
    tiles = counts_ref.shape[1]
    core = lax.axis_index("mp")
    scale = math.log2(math.e) / math.sqrt(HDIM)

    copies = [
        pltpu.make_async_copy(
            weight_hbm.at[
                j, pl.ds(pl.multiple_of(at * half, half), half), pair * LANES : (pair + 1) * LANES
            ],
            w_ref.at[k * half : (k + 1) * half, j * LANES : (j + 1) * LANES],
            w_sems.at[2 * j + k],
        )
        for j in range(3)
        for k, at in enumerate((core, 1 - core))
    ]
    if not staged:
        copies += [
            pltpu.make_async_copy(source, x_ref.at[:, k * half : (k + 1) * half], x_sems.at[k])
            for k, source in enumerate((own, other))
        ]
    for copy in copies:
        copy.start()

    starts = [jnp.int32(0)]
    for t in range(tiles):
        starts.append(starts[-1] + counts_ref[0, t])
    lane = lax.broadcasted_iota(jnp.int32, (1, LANES), 1)
    first = jnp.full((1, LANES), length, jnp.int32)
    last = jnp.zeros((1, LANES), jnp.int32)
    for t in range(tiles):
        first = jnp.where(lane == HDIM + t, starts[t], first)
        last = jnp.where(lane == HDIM + t, starts[t + 1], last)
    flags = jnp.logical_and(lane >= HDIM, lane < HDIM + tiles)
    low_lanes = lane < HDIM

    for copy in copies:
        copy.wait()

    def project(i, carry):
        rows = pl.ds(pl.multiple_of(i * TALL, TALL), TALL)
        if staged:
            spread = dot(own[rows, :], w_ref[:half, :]) + dot(other[rows, :], w_ref[half:, :])
        else:
            spread = dot(x_ref[rows, :], w_ref[...])
        q, k, v = (spread[:, j * LANES : (j + 1) * LANES] for j in range(3))
        q = q * scale
        place = lax.broadcasted_iota(jnp.int32, (TALL, LANES), 0) + i * TALL
        inside = jnp.logical_and(place >= first, place < last)
        q_flag = jnp.where(inside, 1.0, 0.0)
        k_flag = jnp.where(jnp.logical_and(flags, jnp.logical_not(inside)), -FAR, 0.0)
        q_ref[0, rows, :] = jnp.where(low_lanes, q, q_flag).astype(bf16)
        q_ref[1, rows, :] = jnp.where(low_lanes, pltpu.roll(q, HDIM, 1), q_flag).astype(bf16)
        k_ref[0, rows, :] = jnp.where(low_lanes, k, k_flag).astype(bf16)
        k_ref[1, rows, :] = jnp.where(low_lanes, pltpu.roll(k, HDIM, 1), k_flag).astype(bf16)
        v_ref[0, rows, :] = jnp.where(low_lanes, v, 1.0).astype(bf16)
        v_ref[1, rows, :] = jnp.where(low_lanes, 1.0, v).astype(bf16)
        return carry

    lax.fori_loop(0, length // TALL, project, 0)

    def raise_scores(scores):
        return jnp.exp2(scores - jnp.max(scores, axis=1, keepdims=True)).astype(bf16)

    def send_out(i):
        rows = pl.ds(pl.multiple_of(i * TALL, TALL), TALL)
        return pltpu.make_async_copy(out_ref.at[rows], out_hbm.at[rows], out_sems.at[i])

    def query_block(i, carry):
        begin = i * TALL
        rows = pl.ds(pl.multiple_of(begin, TALL), TALL)
        low, high = jnp.int32(0), jnp.int32(length)
        for t in range(tiles):
            low = jnp.where(starts[t] <= begin, starts[t], low)
            end = starts[tiles - t]
            high = jnp.where(end >= begin + TALL, end, high)
        low = (low // 16) * 16
        blocks = (high - low + KEYS - 1) // KEYS
        for n in range(TALL // KEYS, length // KEYS + 1):

            @pl.when(blocks == n)
            def _(n=n):
                start = jnp.minimum(low, length - n * KEYS)
                keys = pl.ds(pl.multiple_of(start, 16), n * KEYS)
                scores = [
                    lax.dot_general(
                        q_ref[h, rows, :],
                        k_ref[h, keys, :],
                        (((1,), (1,)), ((), ())),
                        preferred_element_type=f32,
                    )
                    for h in range(2)
                ]
                even = dot(raise_scores(scores[0]), v_ref[0, keys, :])
                odd = dot(raise_scores(scores[1]), v_ref[1, keys, :])
                total = pltpu.roll(jnp.where(low_lanes, odd, even), HDIM, 1)
                out_ref[rows, :] = (jnp.where(low_lanes, even, odd) / total).astype(bf16)

        send_out(i).start()
        return carry

    lax.fori_loop(0, length // TALL, query_block, 0)
    for i in range(length // TALL):
        send_out(i).wait()


def attend(pair, staged, counts, own, other, w_qkv):
    length, half = own.shape
    features = 2 * half
    held = pl.BlockSpec(memory_space=pltpu.VMEM) if staged else ANYWHERE
    scratch = [
        pltpu.VMEM((features, 3 * LANES), bf16),
        pltpu.VMEM((2, length, LANES), bf16),
        pltpu.VMEM((2, length, LANES), bf16),
        pltpu.VMEM((2, length, LANES), bf16),
        pltpu.VMEM((length, LANES), bf16),
        pltpu.SemaphoreType.DMA((6,)),
        pltpu.SemaphoreType.DMA((length // TALL,)),
    ]
    if not staged:
        scratch += [pltpu.VMEM((length, features), bf16), pltpu.SemaphoreType.DMA((2,))]
    return pl.pallas_call(
        functools.partial(attend_kernel, pair, staged),
        out_shape=jax.ShapeDtypeStruct((length, LANES), bf16),
        in_specs=[SCALARS, held, held, ANYWHERE],
        out_specs=ANYWHERE,
        scratch_shapes=scratch,
        compiler_params=params(SMALL_BYTES if staged else VMEM_BYTES),
        cost_estimate=pl.CostEstimate(
            flops=32 * length * length * HDIM, bytes_accessed=8 * length * half, transcendentals=2 * length * length
        ),
    )(counts, own, other, w_qkv)


def unorder(rank_ref, start, rows, length, shards, context_ref):
    slot = slots(rank_ref[:, pl.ds(start, rows)], length, shards)
    slot = jnp.transpose(jnp.broadcast_to(slot, (LANES, rows)))
    place = lax.broadcasted_iota(jnp.int32, (1, length), 1)
    return dot(one_hot(slot, place), context_ref[...]).astype(bf16)


def unorder_kernel(shards, rank_hbm, own_hbm, other_hbm, out_ref, rank_ref, context_ref, sems):
    length = context_ref.shape[0]
    half_rows = out_ref.shape[0]
    base = lax.axis_index("mp") * half_rows
    copies = [
        pltpu.make_async_copy(rank_hbm, rank_ref, sems.at[0]),
        pltpu.make_async_copy(own_hbm, context_ref.at[:, :LANES], sems.at[1]),
        pltpu.make_async_copy(other_hbm, context_ref.at[:, LANES:], sems.at[2]),
    ]
    for copy in copies:
        copy.start()
    for copy in copies:
        copy.wait()
    for i, rows in enumerate(blocks_of(half_rows, TALL)):
        start = pl.multiple_of(base + i * TALL, TALL)
        out_ref[rows, :] = unorder(rank_ref, start, TALL, length, shards, context_ref)


def unorder_pair(shards, rank_row, own, other):
    length = own.shape[0]
    half_rows = length // 2
    return pl.pallas_call(
        functools.partial(unorder_kernel, shards),
        out_shape=jax.ShapeDtypeStruct((half_rows, 2 * LANES), bf16),
        in_specs=[ANYWHERE] * 3,
        out_specs=pl.BlockSpec(memory_space=pltpu.VMEM),
        scratch_shapes=[
            pltpu.VMEM((1, length), jnp.int32),
            pltpu.VMEM((length, 2 * LANES), bf16),
            pltpu.SemaphoreType.DMA((3,)),
        ],
        compiler_params=params(),
        cost_estimate=pl.CostEstimate(
            flops=4 * half_rows * length * LANES, bytes_accessed=8 * length * LANES, transcendentals=0
        ),
    )(rank_row, own, other)


def gelu_of_half(h):
    inner = 2 * math.sqrt(2 / math.pi)
    return h + h * jnp.tanh(h * (inner + (4 * 0.044715 * inner) * (h * h)))


def finish_kernel(
    shards,
    rank_hbm,
    gain_hbm,
    points_hbm,
    first_hbm,
    own_hbm,
    other_hbm,
    out_own_hbm,
    out_other_hbm,
    fc1_own_hbm,
    fc1_other_hbm,
    fc2_own_hbm,
    fc2_other_hbm,
    done_ref,
    whole_hbm,
    rank_ref,
    gain_ref,
    points_ref,
    first_ref,
    context_ref,
    out_ref,
    fc1_ref,
    fc2_ref,
    middle_ref,
    normed_ref,
    in_sems,
    sems,
):
    length = context_ref.shape[0]
    half_rows = done_ref.shape[0]
    base = pl.multiple_of(lax.axis_index("mp") * half_rows, half_rows)
    hidden_half = fc2_own_hbm.shape[0]
    early = [
        (rank_hbm, rank_ref),
        (own_hbm, context_ref.at[:, :LANES]),
        (other_hbm, context_ref.at[:, LANES:]),
    ]
    later = [(first_hbm, first_ref), (gain_hbm, gain_ref), (points_hbm.at[pl.ds(base, half_rows)], points_ref)]
    later += [
        (ref.at[pair * LANES : (pair + 1) * LANES], out_ref.at[(2 * pair + k) * LANES : (2 * pair + k + 1) * LANES])
        for pair in range(2)
        for k, ref in enumerate((out_own_hbm, out_other_hbm))
    ]
    last = [
        (fc1_own_hbm, fc1_ref.at[:, :hidden_half]),
        (fc1_other_hbm, fc1_ref.at[:, hidden_half:]),
        (fc2_own_hbm, fc2_ref.at[:hidden_half]),
        (fc2_other_hbm, fc2_ref.at[hidden_half:]),
    ]
    copies = [pltpu.make_async_copy(*ends, in_sems.at[k]) for k, ends in enumerate(early + later + last)]
    early, later, last = copies[:3], copies[3:10], copies[10:]
    for copy in copies:
        copy.start()

    blocks = blocks_of(half_rows, TALL)
    for copy in early:
        copy.wait()
    for i, rows in enumerate(blocks):
        start = pl.multiple_of(base + i * TALL, TALL)
        second = unorder(rank_ref, start, TALL, length, shards, context_ref)
        if i == 0:
            for copy in later:
                copy.wait()
        split_at = 2 * LANES
        attn_out = dot(first_ref[rows, :], out_ref[:split_at, :]) + dot(second, out_ref[split_at:, :])
        middle = (points_ref[rows, :].astype(f32) + attn_out.astype(bf16).astype(f32)).astype(bf16)
        middle_ref[rows, :] = middle
        normed_ref[rows, :] = normalise(middle.astype(f32), gain_ref[...]) * 0.5
    for copy in last:
        copy.wait()

    def away(i):
        here = pl.ds(pl.multiple_of(i * TALL, TALL), TALL)
        there = pl.ds(pl.multiple_of(base + i * TALL, TALL), TALL)
        return pltpu.make_async_copy(done_ref.at[here], whole_hbm.at[there], sems.at[i])

    chunks = blocks_of(2 * hidden_half, TALL)

    def mlp(i, carry):
        here = pl.ds(pl.multiple_of(i * TALL, TALL), TALL)
        normed = normed_ref[here, :]
        total = middle_ref[here, :].astype(f32)
        half_hidden = dot(normed, fc1_ref[:, chunks[0]])
        for k, chunk in enumerate(chunks):
            ahead = dot(normed, fc1_ref[:, chunks[k + 1]]) if k + 1 < len(chunks) else None
            total = total + dot(gelu_of_half(half_hidden).astype(bf16), fc2_ref[chunk, :])
            half_hidden = ahead
        done_ref[here, :] = total.astype(bf16)
        away(i).start()
        return carry

    lax.fori_loop(0, half_rows // TALL, mlp, 0)
    for i in range(half_rows // TALL):
        away(i).wait()


def finish(shards, rank_row, gain_row, points, *arrays):
    length, features = points.shape
    half_rows = length // 2
    hidden = 2 * arrays[-1].shape[0]
    return pl.pallas_call(
        functools.partial(finish_kernel, shards),
        out_shape=(
            jax.ShapeDtypeStruct((half_rows, features), bf16),
            jax.ShapeDtypeStruct((length, features), bf16),
        ),
        in_specs=[ANYWHERE] * 12,
        out_specs=(pl.BlockSpec(memory_space=pltpu.VMEM), ANYWHERE),
        scratch_shapes=[
            pltpu.VMEM((1, length), jnp.int32),
            pltpu.VMEM((1, features), f32),
            pltpu.VMEM((half_rows, features), bf16),
            pltpu.VMEM((half_rows, 2 * LANES), bf16),
            pltpu.VMEM((length, 2 * LANES), bf16),
            pltpu.VMEM((features, features), bf16),
            pltpu.VMEM((features, hidden), bf16),
            pltpu.VMEM((hidden, features), bf16),
            pltpu.VMEM((half_rows, features), bf16),
            pltpu.VMEM((half_rows, features), bf16),
            pltpu.SemaphoreType.DMA((14,)),
            pltpu.SemaphoreType.DMA((half_rows // TALL,)),
        ],
        compiler_params=params(),
        cost_estimate=pl.CostEstimate(
            flops=2 * half_rows * features * (length + 9 * features),
            bytes_accessed=16 * length * features,
            transcendentals=half_rows * 4 * features,
        ),
    )(rank_row, gain_row, points, *arrays)


def across(values):
    return lax.ppermute(values, "mp", [(0, 1), (1, 0)])


def exchange(rows, shards):
    length, columns = rows.shape
    cells = rows.reshape(shards, length // shards, columns)
    return lax.all_to_all(cells, "space", split_axis=0, concat_axis=0, tiled=True).reshape(length, columns)


def body(points, curve_rank, patch_counts, norm_gain_attn, w_qkv, w_out, norm_gain_mlp, w_fc1, w_fc2):
    shards = lax.axis_size("space")
    length, features = points.shape
    rank_row = curve_rank.reshape(1, length)
    own = exchange(order_for_owners(shards, rank_row, norm_gain_attn.reshape(1, features), points), shards)
    swapped = across(w_fc1), across(w_fc2), across(w_out)
    other = across(own)
    first_own = exchange(attend(0, True, patch_counts, own, other, w_qkv), shards)
    counts, (other_fc1, other_fc2, other_out) = lax.optimization_barrier((patch_counts, swapped))
    second_own = exchange(attend(1, False, counts, own, other, w_qkv), shards)
    first = unorder_pair(shards, rank_row, first_own, across(first_own))
    second_own, first = lax.optimization_barrier((second_own, first))
    done, whole = finish(
        shards,
        rank_row,
        norm_gain_mlp.reshape(1, features),
        points,
        first,
        second_own,
        across(second_own),
        w_out,
        other_out,
        w_fc1,
        other_fc1,
        w_fc2,
        other_fc2,
    )
    start = (1 - lax.axis_index("mp")) * (length // 2)
    return lax.dynamic_update_slice(whole, across(done), (start, 0))


def solution(mesh):
    placed = (
        P("space", None),
        P("space"),
        P("space", None),
        P(),
        P(None, None, "mp"),
        P("mp", None),
        P(),
        P(None, "mp"),
        P("mp", None),
    )
    return jax.shard_map(
        body, mesh=mesh, in_specs=placed, out_specs=P("space", None), check_vma=False
    )
```

time: 120 us -> 113 us (0.942); the launches traced: 120 us -> 112 us
  Pallas kernels: 49.8 us -> 43.8 us
  waiting for transfers between devices: 22.8 us -> 20.9 us
    all_to_all x2, waiting for transfers between devices: 15.6 us -> 11.9 us  [exchange(): lax.all_to_all(cells, 'space', split_axis=0, concat_axis=0, tiled=True)]
    pallas_call x2 -> x3, Pallas kernels: 27.9 us -> 25.2 us  [the longest x2 21.8 us: attend(): pl.pallas_call(functools.partial(attend_kernel, pair, staged), out_shape=...]
    pallas_call x1, Pallas kernels: 14.2 us -> 12 us  [finish(): pl.pallas_call(functools.partial(finish_kernel, shards), out_shape=(jax.S...]
    ppermute x7, waiting for transfers between devices: 7.18 us -> 8.94 us  [across(): return lax.ppermute(values, 'mp', [(0, 1), (1, 0)])]
  transfers between devices with their start and end apart: 9 -> 9, of which waited for: 5 -> 6; matrix products, arithmetic and copies ran while one was open for 0% -> 0% of each run, Pallas kernels for 12% -> 23%
where the time goes in v3:
time: 113 us; the launch traced here: 112 us
  Pallas kernels  43.8 us (39%)
  blocking collectives  34.8 us (31%)
  waiting for transfers between devices  20.9 us (18%)
  starting transfers between devices  9.45 us (8%)
  local copies, waits for them, and re-layouts  2.67 us (2%)
    all_to_all x1, blocking collectives, exchange(): lax.all_to_all(cells, 'space', split_axis=0, concat_axis=0, tiled=True)  34.8 us
    pallas_call x2, Pallas kernels, attend(): pl.pallas_call(functools.partial(attend_kernel, pair, staged), out_shape=...  21.8 us
    pallas_call x1, Pallas kernels, finish(): pl.pallas_call(functools.partial(finish_kernel, shards), out_shape=(jax.S...  12 us
    all_to_all x2, waiting for transfers between devices, exchange(): lax.all_to_all(cells, 'space', split_axis=0, concat_axis=0, tiled=True)  11.9 us
    ppermute x7, waiting for transfers between devices, across(): return lax.ppermute(values, 'mp', [(0, 1), (1, 0)])  8.94 us
    all_to_all x2, starting transfers between devices, exchange(): lax.all_to_all(cells, 'space', split_axis=0, concat_axis=0, tiled=True)  8.16 us
    pallas_call x1, Pallas kernels, order_for_owners(): pl.pallas_call(functools.partial(send_kernel, shards), out_shape=jax.Shap...  6.59 us
    pallas_call x1, Pallas kernels, unorder_pair(): pl.pallas_call(functools.partial(unorder_kernel, shards), out_shape=jax.S...  3.33 us
  transfers between devices with their start and end apart: 9, of which 6 were waited for; matrix products, arithmetic and copies ran while one was open for 0% of the time, Pallas kernels for 23%

profile of v3, /device:TPU:0, one launch (start us, length us, event | category | flops | bytes accessed | tf_op | source)
XLA Modules:
  0.0 111.8 jit_solution(17123645430543007110)
XLA Ops:
  0.0 6.6 %shard_map.91 = bf16[2048,256]{1,0:T(8,128)(2,1)} custom-call(s32[1,2048]{1,0:T(1,128)} %bitcast.18, f32[1,512]{1,0:T(1,128)} %bitcast.21, bf16[2048,512]{1,0:T(8,128)(2,1)} %points_hbm.3), custom_call_target="tpu_custom_call" | custom-call | flops 2147483648 | bytes 4194304 | tf_op jit(solution)/shard_map/pallas_call | solution.py:102
  6.6 0.0 copy-start.2
  6.6 0.0 copy-start.3
  6.7 34.8 %all_to_all.15 = bf16[16,128,256]{2,1,0:T(8,128)(2,1)S(1)} all-to-all(bf16[16,128,256]{2,1,0:T(8,128)(2,1)} %bitcast.12), channel_id=1, replica_groups=mesh['space'=16,'mp'=2] {'space'}, dimensions={0} | all-to-all | bytes 2097152 | tf_op jit(solution)/shard_map/all_to_all | solution.py:465
  41.5 0.5 collective-permute-start
  42.0 0.1 collective-permute-start.1
  42.1 0.4 collective-permute-start.2
  42.5 2.4 %collective-permute-done.3.other = bf16[2048,256]{1,0:T(8,128)(2,1)S(1)} collective-permute-done((bf16[2048,256]{1,0:T(8,128)(2,1)S(1)}, bf16[2048,256]{1,0:T(8,128)(2,1)S(1)}, u32[]{:S(2)}, u32[]{:S(2)}) %collective-permute-start.3) | collective-permute-done | bytes 1048608 | tf_op jit(solution)/shard_map/ppermute | solution.py:459
  44.9 10.1 %shard_map.93 = bf16[2048,128]{1,0:T(8,128)(2,1)} custom-call(s32[1,4]{1,0:T(1,128)S(1)} %copy-done.3, bf16[2048,256]{1,0:T(8,128)(2,1)S(1)} %bitcast.10, bf16[2048,256]{1,0:T(8,128)(2,1)S(1)} %collective-permute-done.3.other, bf16[3,512,256]{2,1,0:T(8,128)(2,1)S(1)} %copy-done.2), custom_call_target="tpu_custom_call" | custom-call | flops 8589934592 | bytes 4194304 | tf_op jit(solution)/shard_map/pallas_call | solution.py:263
  55.0 4.2 %all-to-all-start.2 = ((bf16[16,128,128]{2,1,0:T(8,128)(2,1)}), bf16[16,128,128]{2,1,0:T(8,128)(2,1)S(1)}, u32[]{:S(2)}, u32[]{:S(2)}) async-start(bf16[16,128,128]{2,1,0:T(8,128)(2,1)} %bitcast.7), calls=%async_computation.2 | async-start | bytes 1048576 | tf_op jit(solution)/shard_map/all_to_all | solution.py:465
  59.3 11.7 %shard_map.92 = bf16[2048,128]{1,0:T(8,128)(2,1)} custom-call(s32[1,4]{1,0:T(1,128)} %counts_ref.2, bf16[2048,256]{1,0:T(8,128)(2,1)} %bitcast.11, bf16[2048,256]{1,0:T(8,128)(2,1)} %copy-done.1, bf16[3,512,256]{2,1,0:T(8,128)(2,1)} %weight_hbm.3), custom_call_target="tpu_custom_call" | custom-call | flops 8589934592 | bytes 4194304 | tf_op jit(solution)/shard_map/pallas_call | solution.py:263
  71.1 3.6 %all-to-all-done.2 = bf16[16,128,128]{2,1,0:T(8,128)(2,1)S(1)} async-done(((bf16[16,128,128]{2,1,0:T(8,128)(2,1)}), bf16[16,128,128]{2,1,0:T(8,128)(2,1)S(1)}, u32[]{:S(2)}, u32[]{:S(2)}) %all-to-all-start.2) | async-done | bytes 524320 | tf_op jit(solution)/shard_map/all_to_all | solution.py:465
  74.7 3.9 %all-to-all-start.1 = ((bf16[16,128,128]{2,1,0:T(8,128)(2,1)}), bf16[16,128,128]{2,1,0:T(8,128)(2,1)S(1)}, u32[]{:S(2)}, u32[]{:S(2)}) async-start(bf16[16,128,128]{2,1,0:T(8,128)(2,1)} %bitcast.17), calls=%async_computation.1 | async-start | bytes 1048576 | tf_op jit(solution)/shard_map/all_to_all | solution.py:465
  78.6 0.1 collective-permute-start.4
  78.7 1.9 %collective-permute-done.4.other_hbm = bf16[2048,128]{1,0:T(8,128)(2,1)S(1)} collective-permute-done((bf16[2048,128]{1,0:T(8,128)(2,1)S(1)}, bf16[2048,128]{1,0:T(8,128)(2,1)S(1)}, u32[]{:S(2)}, u32[]{:S(2)}) %collective-permute-start.4) | collective-permute-done | bytes 524320 | tf_op jit(solution)/shard_map/ppermute | solution.py:459
  80.6 0.8 copy-done.9
  81.4 3.3 %shard_map.94.first_hbm = bf16[1024,256]{1,0:T(8,128)(2,1)} custom-call(s32[1,2048]{1,0:T(1,128)} %bitcast.19, bf16[2048,128]{1,0:T(8,128)(2,1)} %bitcast.14, bf16[2048,128]{1,0:T(8,128)(2,1)} %copy-done.9), custom_call_target="tpu_custom_call" | custom-call | flops 1073741824 | bytes 2097152 | tf_op jit(solution)/shard_map/pallas_call | solution.py:304
  84.7 8.3 %all-to-all-done.1 = bf16[16,128,128]{2,1,0:T(8,128)(2,1)S(1)} async-done(((bf16[16,128,128]{2,1,0:T(8,128)(2,1)}), bf16[16,128,128]{2,1,0:T(8,128)(2,1)S(1)}, u32[]{:S(2)}, u32[]{:S(2)}) %all-to-all-start.1) | async-done | bytes 524320 | tf_op jit(solution)/shard_map/all_to_all | solution.py:465
  93.1 1.9 %collective-permute-done.5.other_hbm = bf16[2048,128]{1,0:T(8,128)(2,1)S(1)} collective-permute-done((bf16[2048,128]{1,0:T(8,128)(2,1)S(1)}, bf16[2048,128]{1,0:T(8,128)(2,1)S(1)}, u32[]{:S(2)}, u32[]{:S(2)}) %collective-permute-start.5) | collective-permute-done | bytes 524320 | tf_op jit(solution)/shard_map/ppermute | solution.py:459
  95.0 0.8 copy-done.8
  95.8 12.0 %shard_map.95 = (bf16[1024,512]{1,0:T(8,128)(2,1)}, bf16[2048,512]{1,0:T(8,128)(2,1)}) custom-call(s32[1,2048]{1,0:T(1,128)} %bitcast.20, f32[1,512]{1,0:T(1,128)} %bitcast.22, bf16[2048,512]{1,0:T(8,128)(2,1)} %points_hbm.3, bf16[1024,256]{1,0:T(8,128)(2,1)} %shard_map.94.first_hbm, bf16[2048,128]{1,0:T(8,128)(2,1)} %bitcast.16, ...), custom_call_target="tpu_custom_call" | custom-call | flops 6979321856 | bytes 16777216 | tf_op jit(solution)/shard_map/pallas_call | solution.py:427
  107.8 0.2 collective-permute-start.6
  108.0 2.7 %collective-permute-done.6 = bf16[1024,512]{1,0:T(8,128)(2,1)S(1)} collective-permute-done((bf16[1024,512]{1,0:T(8,128)(2,1)}, bf16[1024,512]{1,0:T(8,128)(2,1)S(1)}, u32[]{:S(2)}, u32[]{:S(2)}) %collective-permute-start.6) | collective-permute-done | bytes 1048608 | tf_op jit(solution)/shard_map/ppermute | solution.py:459
  110.7 1.0 constant_dynamic-update-slice_fusion
  (25 shorter events, 0.1 us)
Async XLA Ops:
  0.0 42.0 %copy-start.7 = (bf16[1024,512]{1,0:T(8,128)(2,1)S(1)}, bf16[1024,512]{1,0:T(8,128)(2,1)}, u32[]{:S(2)}) copy-start(bf16[1024,512]{1,0:T(8,128)(2,1)} %fc2_own_hbm.1) | copy-start | bytes 3145732
  6.6 34.9 %copy-start.6 = (bf16[512,1024]{1,0:T(8,128)(2,1)S(1)}, bf16[512,1024]{1,0:T(8,128)(2,1)}, u32[]{:S(2)}) copy-start(bf16[512,1024]{1,0:T(8,128)(2,1)} %fc1_own_hbm.1) | copy-start | bytes 3145732
  6.6 35.5 %copy-start.10 = (bf16[256,512]{1,0:T(8,128)(2,1)S(1)}, bf16[256,512]{1,0:T(8,128)(2,1)}, u32[]{:S(2)}) copy-start(bf16[256,512]{1,0:T(8,128)(2,1)} %out_own_hbm.1) | copy-start | bytes 786436
  6.6 38.3 %copy-start.2 = (bf16[3,512,256]{2,1,0:T(8,128)(2,1)S(1)}, bf16[3,512,256]{2,1,0:T(8,128)(2,1)}, u32[]{:S(2)}) copy-start(bf16[3,512,256]{2,1,0:T(8,128)(2,1)} %weight_hbm.3) | copy-start | bytes 2359300
  6.6 38.3 %copy-start.3 = (s32[1,4]{1,0:T(1,128)S(1)}, s32[1,4]{1,0:T(1,128)}, u32[]{:S(2)}) copy-start(s32[1,4]{1,0:T(1,128)} %counts_ref.2) | copy-start | bytes 52
  41.5 13.6 %copy-start = (bf16[16,128,256]{2,1,0:T(8,128)(2,1)}, bf16[16,128,256]{2,1,0:T(8,128)(2,1)S(1)}, u32[]{:S(2)}) copy-start(bf16[16,128,256]{2,1,0:T(8,128)(2,1)S(1)} %all_to_all.15) | copy-start | bytes 3145732
  41.5 3.4 %collective-permute-start.3 = (bf16[2048,256]{1,0:T(8,128)(2,1)S(1)}, bf16[2048,256]{1,0:T(8,128)(2,1)S(1)}, u32[]{:S(2)}, u32[]{:S(2)}) collective-permute-start(bf16[2048,256]{1,0:T(8,128)(2,1)S(1)} %bitcast.9), channel_id=1, source_target_pairs={{0,1},{1,0},{2,3},{3,2},{4,5},{5,4},{6,7},{7,6},{8,9},{9,8},{10,11... | collective-permute-start | bytes 3145736 | tf_op jit(solution)/shard_map/ppermute | solution.py:459
  41.5 17.8 %collective-permute-start = (bf16[512,1024]{1,0:T(8,128)(2,1)S(1)}, bf16[512,1024]{1,0:T(8,128)(2,1)}, u32[]{:S(2)}, u32[]{:S(2)}) collective-permute-start(bf16[512,1024]{1,0:T(8,128)(2,1)S(1)} %copy-done.6), channel_id=1, source_target_pairs={{0,1},{1,0},{2,3},{3,2},{4,5},{5,4},{6,7},{7,6},{8,9},{9,8},{10,11... | collective-permute-start | bytes 3145736 | tf_op jit(solution)/shard_map/ppermute | solution.py:459
  42.0 17.3 %collective-permute-start.1 = (bf16[1024,512]{1,0:T(8,128)(2,1)S(1)}, bf16[1024,512]{1,0:T(8,128)(2,1)}, u32[]{:S(2)}, u32[]{:S(2)}) collective-permute-start(bf16[1024,512]{1,0:T(8,128)(2,1)S(1)} %copy-done.7), channel_id=1, source_target_pairs={{0,1},{1,0},{2,3},{3,2},{4,5},{5,4},{6,7},{7,6},{8,9},{9,8},{10,11... | collective-permute-start | bytes 3145736 | tf_op jit(solution)/shard_map/ppermute | solution.py:459
  42.1 17.2 %collective-permute-start.2 = (bf16[256,512]{1,0:T(8,128)(2,1)S(1)}, bf16[256,512]{1,0:T(8,128)(2,1)S(1)}, u32[]{:S(2)}, u32[]{:S(2)}) collective-permute-start(bf16[256,512]{1,0:T(8,128)(2,1)S(1)} %copy-done.10), channel_id=1, source_target_pairs={{0,1},{1,0},{2,3},{3,2},{4,5},{5,4},{6,7},{7,6},{8,9},{9,8},{10,11... | collective-permute-start | bytes 786440 | tf_op jit(solution)/shard_map/ppermute | solution.py:459
  44.9 10.1 %copy-start.1 = (bf16[2048,256]{1,0:T(8,128)(2,1)}, bf16[2048,256]{1,0:T(8,128)(2,1)S(1)}, u32[]{:S(2)}) copy-start(bf16[2048,256]{1,0:T(8,128)(2,1)S(1)} %collective-permute-done.3.other) | copy-start | bytes 3145732
  55.0 19.6 %all-to-all-start.2 = ((bf16[16,128,128]{2,1,0:T(8,128)(2,1)}), bf16[16,128,128]{2,1,0:T(8,128)(2,1)S(1)}, u32[]{:S(2)}, u32[]{:S(2)}) async-start(bf16[16,128,128]{2,1,0:T(8,128)(2,1)} %bitcast.7), calls=%async_computation.2 | async-start | bytes 1048576 | tf_op jit(solution)/shard_map/all_to_all | solution.py:465
  59.3 11.8 %copy-start.11 = (bf16[256,512]{1,0:T(8,128)(2,1)}, bf16[256,512]{1,0:T(8,128)(2,1)S(1)}, u32[]{:S(2)}) copy-start(bf16[256,512]{1,0:T(8,128)(2,1)S(1)} %collective-permute-done.2.out_other_hbm) | copy-start | bytes 786436
  74.7 5.9 %copy-start.4 = (bf16[16,128,128]{2,1,0:T(8,128)(2,1)}, bf16[16,128,128]{2,1,0:T(8,128)(2,1)S(1)}, u32[]{:S(2)}) copy-start(bf16[16,128,128]{2,1,0:T(8,128)(2,1)S(1)} %all-to-all-done.2) | copy-start | bytes 1572868
  74.7 18.4 %all-to-all-start.1 = ((bf16[16,128,128]{2,1,0:T(8,128)(2,1)}), bf16[16,128,128]{2,1,0:T(8,128)(2,1)S(1)}, u32[]{:S(2)}, u32[]{:S(2)}) async-start(bf16[16,128,128]{2,1,0:T(8,128)(2,1)} %bitcast.17), calls=%async_computation.1 | async-start | bytes 1048576 | tf_op jit(solution)/shard_map/all_to_all | solution.py:465
  78.6 2.0 %collective-permute-start.4 = (bf16[2048,128]{1,0:T(8,128)(2,1)S(1)}, bf16[2048,128]{1,0:T(8,128)(2,1)S(1)}, u32[]{:S(2)}, u32[]{:S(2)}) collective-permute-start(bf16[2048,128]{1,0:T(8,128)(2,1)S(1)} %bitcast.13), channel_id=1, source_target_pairs={{0,1},{1,0},{2,3},{3,2},{4,5},{5,4},{6,7},{7,6},{8,9},{9,8},{10,11... | collective-permute-start | bytes 1572872 | tf_op jit(solution)/shard_map/ppermute | solution.py:459
  80.6 0.8 copy-start.9
  93.1 1.9 %copy-start.5 = (bf16[16,128,128]{2,1,0:T(8,128)(2,1)}, bf16[16,128,128]{2,1,0:T(8,128)(2,1)S(1)}, u32[]{:S(2)}) copy-start(bf16[16,128,128]{2,1,0:T(8,128)(2,1)S(1)} %all-to-all-done.1) | copy-start | bytes 1572868
  93.1 1.9 %collective-permute-start.5 = (bf16[2048,128]{1,0:T(8,128)(2,1)S(1)}, bf16[2048,128]{1,0:T(8,128)(2,1)S(1)}, u32[]{:S(2)}, u32[]{:S(2)}) collective-permute-start(bf16[2048,128]{1,0:T(8,128)(2,1)S(1)} %bitcast.15), channel_id=1, source_target_pairs={{0,1},{1,0},{2,3},{3,2},{4,5},{5,4},{6,7},{7,6},{8,9},{9,8},{10,11... | collective-permute-start | bytes 1572872 | tf_op jit(solution)/shard_map/ppermute | solution.py:459
  95.0 0.8 copy-start.8
  107.8 2.9 %collective-permute-start.6 = (bf16[1024,512]{1,0:T(8,128)(2,1)}, bf16[1024,512]{1,0:T(8,128)(2,1)S(1)}, u32[]{:S(2)}, u32[]{:S(2)}) collective-permute-start(bf16[1024,512]{1,0:T(8,128)(2,1)} %get-tuple-element.20), channel_id=1, source_target_pairs={{0,1},{1,0},{2,3},{3,2},{4,5},{5,4},{6,7},{7,6},{8,9},{9,8},{10,11... | collective-permute-start | bytes 3145736 | tf_op jit(solution)/shard_map/ppermute | solution.py:459

commit v4 on v3

--- a/solution.py
+++ b/solution.py
@@ -13,6 +13,7 @@
 ROWS = 256
 TALL = 512
 KEYS = 256
+PADDED = HDIM + 16
 EPSILON = 1e-06
 FAR = 1e30
 VMEM_BYTES = 58 * 1024 * 1024
@@ -120,46 +121,23 @@
 
 
 def attend_kernel(
-    pair,
-    staged,
-    counts_ref,
-    own,
-    other,
-    weight_hbm,
-    out_hbm,
-    w_ref,
-    q_ref,
-    k_ref,
-    v_ref,
-    out_ref,
-    w_sems,
-    out_sems,
-    x_ref=None,
-    x_sems=None,
+    counts_ref, own_ref, other_ref, weight_hbm, out_hbm, w_ref, q_ref, k_ref, v_ref, out_ref, w_sems, out_sems
 ):
-    length = out_ref.shape[0]
-    features = w_ref.shape[0]
-    half = features // 2
+    length, half = own_ref.shape
     tiles = counts_ref.shape[1]
+    pairs = out_ref.shape[0]
     core = lax.axis_index("mp")
     scale = math.log2(math.e) / math.sqrt(HDIM)
 
     copies = [
         pltpu.make_async_copy(
-            weight_hbm.at[
-                j, pl.ds(pl.multiple_of(at * half, half), half), pair * LANES : (pair + 1) * LANES
-            ],
-            w_ref.at[k * half : (k + 1) * half, j * LANES : (j + 1) * LANES],
+            weight_hbm.at[j, pl.ds(pl.multiple_of(at * half, half), half)],
+            w_ref.at[k * half : (k + 1) * half, j * pairs * LANES : (j + 1) * pairs * LANES],
             w_sems.at[2 * j + k],
         )
         for j in range(3)
         for k, at in enumerate((core, 1 - core))
     ]
-    if not staged:
-        copies += [
-            pltpu.make_async_copy(source, x_ref.at[:, k * half : (k + 1) * half], x_sems.at[k])
-            for k, source in enumerate((own, other))
-        ]
     for copy in copies:
         copy.start()
 
@@ -174,38 +152,35 @@
         last = jnp.where(lane == HDIM + t, starts[t + 1], last)
     flags = jnp.logical_and(lane >= HDIM, lane < HDIM + tiles)
     low_lanes = lane < HDIM
-
+    v_ref[:, HDIM:, :] = jnp.ones((2 * pairs, PADDED - HDIM, length), bf16)
     for copy in copies:
         copy.wait()
 
-    def project(i, carry):
-        rows = pl.ds(pl.multiple_of(i * TALL, TALL), TALL)
-        if staged:
-            spread = dot(own[rows, :], w_ref[:half, :]) + dot(other[rows, :], w_ref[half:, :])
-        else:
-            spread = dot(x_ref[rows, :], w_ref[...])
-        q, k, v = (spread[:, j * LANES : (j + 1) * LANES] for j in range(3))
-        q = q * scale
+    for i, rows in enumerate(blocks_of(length, TALL)):
+        spread = dot(own_ref[rows, :], w_ref[:half, :]) + dot(other_ref[rows, :], w_ref[half:, :])
         place = lax.broadcasted_iota(jnp.int32, (TALL, LANES), 0) + i * TALL
         inside = jnp.logical_and(place >= first, place < last)
         q_flag = jnp.where(inside, 1.0, 0.0)
         k_flag = jnp.where(jnp.logical_and(flags, jnp.logical_not(inside)), -FAR, 0.0)
-        q_ref[0, rows, :] = jnp.where(low_lanes, q, q_flag).astype(bf16)
-        q_ref[1, rows, :] = jnp.where(low_lanes, pltpu.roll(q, HDIM, 1), q_flag).astype(bf16)
-        k_ref[0, rows, :] = jnp.where(low_lanes, k, k_flag).astype(bf16)
-        k_ref[1, rows, :] = jnp.where(low_lanes, pltpu.roll(k, HDIM, 1), k_flag).astype(bf16)
-        v_ref[0, rows, :] = jnp.where(low_lanes, v, 1.0).astype(bf16)
-        v_ref[1, rows, :] = jnp.where(low_lanes, 1.0, v).astype(bf16)
-        return carry
-
-    lax.fori_loop(0, length // TALL, project, 0)
-
-    def raise_scores(scores):
-        return jnp.exp2(scores - jnp.max(scores, axis=1, keepdims=True)).astype(bf16)
-
-    def send_out(i):
+        for pair in range(pairs):
+            q, k, v = (spread[:, (j * pairs + pair) * LANES : (j * pairs + pair + 1) * LANES] for j in range(3))
+            q = q * scale
+            q_ref[2 * pair, rows, :] = jnp.where(low_lanes, q, q_flag).astype(bf16)
+            q_ref[2 * pair + 1, rows, :] = jnp.where(low_lanes, pltpu.roll(q, HDIM, 1), q_flag).astype(bf16)
+            k_ref[2 * pair, rows, :] = jnp.where(low_lanes, k, k_flag).astype(bf16)
+            k_ref[2 * pair + 1, rows, :] = jnp.where(low_lanes, pltpu.roll(k, HDIM, 1), k_flag).astype(bf16)
+            v = jnp.transpose(v).astype(bf16)
+            v_ref[2 * pair, :HDIM, rows] = v[:HDIM]
+            v_ref[2 * pair + 1, :HDIM, rows] = v[HDIM:]
+
+    def weigh(scores):
+        return jnp.exp2(scores - jnp.max(scores, axis=0, keepdims=True)).astype(bf16)
+
+    def send_out(i, pair):
         rows = pl.ds(pl.multiple_of(i * TALL, TALL), TALL)
-        return pltpu.make_async_copy(out_ref.at[rows], out_hbm.at[rows], out_sems.at[i])
+        return pltpu.make_async_copy(
+            out_ref.at[pair, rows], out_hbm.at[rows, pair * LANES : (pair + 1) * LANES], out_sems.at[i, pair]
+        )
 
     def query_block(i, carry):
         begin = i * TALL
@@ -215,60 +190,64 @@
             low = jnp.where(starts[t] <= begin, starts[t], low)
             end = starts[tiles - t]
             high = jnp.where(end >= begin + TALL, end, high)
-        low = (low // 16) * 16
+        low = (low // LANES) * LANES
         blocks = (high - low + KEYS - 1) // KEYS
         for n in range(TALL // KEYS, length // KEYS + 1):
 
             @pl.when(blocks == n)
             def _(n=n):
-                start = jnp.minimum(low, length - n * KEYS)
-                keys = pl.ds(pl.multiple_of(start, 16), n * KEYS)
-                scores = [
-                    lax.dot_general(
-                        q_ref[h, rows, :],
-                        k_ref[h, keys, :],
-                        (((1,), (1,)), ((), ())),
-                        preferred_element_type=f32,
-                    )
-                    for h in range(2)
-                ]
-                even = dot(raise_scores(scores[0]), v_ref[0, keys, :])
-                odd = dot(raise_scores(scores[1]), v_ref[1, keys, :])
-                total = pltpu.roll(jnp.where(low_lanes, odd, even), HDIM, 1)
-                out_ref[rows, :] = (jnp.where(low_lanes, even, odd) / total).astype(bf16)
-
-        send_out(i).start()
+                start = pl.multiple_of(jnp.minimum(low, length - n * KEYS), LANES)
+                keys = pl.ds(start, n * KEYS)
+
+                def one_pair(pair, carry):
+                    scores = [
+                        lax.dot_general(
+                            k_ref[2 * pair + h, keys, :],
+                            q_ref[2 * pair + h, rows, :],
+                            (((1,), (1,)), ((), ())),
+                            preferred_element_type=f32,
+                        )
+                        for h in range(2)
+                    ]
+                    sums = [dot(v_ref[2 * pair + h, :, keys], weigh(scores[h])) for h in range(2)]
+                    value = jnp.concatenate([both[:HDIM] / both[HDIM : HDIM + 1] for both in sums], axis=0)
+                    out_ref[pair, rows, :] = jnp.transpose(value).astype(bf16)
+                    return carry
+
+                lax.fori_loop(0, pairs, one_pair, 0)
+
+        for pair in range(pairs):
+            send_out(i, pair).start()
         return carry
 
     lax.fori_loop(0, length // TALL, query_block, 0)
     for i in range(length // TALL):
-        send_out(i).wait()
-
-
-def attend(pair, staged, counts, own, other, w_qkv):
+        for pair in range(pairs):
+            send_out(i, pair).wait()
+
+
+def attend(counts, own, other, w_qkv):
     length, half = own.shape
-    features = 2 * half
-    held = pl.BlockSpec(memory_space=pltpu.VMEM) if staged else ANYWHERE
-    scratch = [
-        pltpu.VMEM((features, 3 * LANES), bf16),
-        pltpu.VMEM((2, length, LANES), bf16),
-        pltpu.VMEM((2, length, LANES), bf16),
-        pltpu.VMEM((2, length, LANES), bf16),
-        pltpu.VMEM((length, LANES), bf16),
-        pltpu.SemaphoreType.DMA((6,)),
-        pltpu.SemaphoreType.DMA((length // TALL,)),
-    ]
-    if not staged:
-        scratch += [pltpu.VMEM((length, features), bf16), pltpu.SemaphoreType.DMA((2,))]
+    features, columns = w_qkv.shape[1:]
+    heads = columns // HDIM
+    held = pl.BlockSpec(memory_space=pltpu.VMEM)
     return pl.pallas_call(
-        functools.partial(attend_kernel, pair, staged),
-        out_shape=jax.ShapeDtypeStruct((length, LANES), bf16),
+        attend_kernel,
+        out_shape=jax.ShapeDtypeStruct((length, columns), bf16),
         in_specs=[SCALARS, held, held, ANYWHERE],
         out_specs=ANYWHERE,
-        scratch_shapes=scratch,
-        compiler_params=params(SMALL_BYTES if staged else VMEM_BYTES),
+        scratch_shapes=[
+            pltpu.VMEM((features, 3 * columns), bf16),
+            pltpu.VMEM((heads, length, LANES), bf16),
+            pltpu.VMEM((heads, length, LANES), bf16),
+            pltpu.VMEM((heads, PADDED, length), bf16),
+            pltpu.VMEM((heads // 2, length, LANES), bf16),
+            pltpu.SemaphoreType.DMA((6,)),
+            pltpu.SemaphoreType.DMA((length // TALL, heads // 2)),
+        ],
+        compiler_params=params(SMALL_BYTES),
         cost_estimate=pl.CostEstimate(
-            flops=32 * length * length * HDIM, bytes_accessed=8 * length * half, transcendentals=2 * length * length
+            flops=64 * length * length * HDIM, bytes_accessed=8 * length * half, transcendentals=4 * length * length
         ),
     )(counts, own, other, w_qkv)
 
@@ -280,44 +259,6 @@
     return dot(one_hot(slot, place), context_ref[...]).astype(bf16)
 
 
-def unorder_kernel(shards, rank_hbm, own_hbm, other_hbm, out_ref, rank_ref, context_ref, sems):
-    length = context_ref.shape[0]
-    half_rows = out_ref.shape[0]
-    base = lax.axis_index("mp") * half_rows
-    copies = [
-        pltpu.make_async_copy(rank_hbm, rank_ref, sems.at[0]),
-        pltpu.make_async_copy(own_hbm, context_ref.at[:, :LANES], sems.at[1]),
-        pltpu.make_async_copy(other_hbm, context_ref.at[:, LANES:], sems.at[2]),
-    ]
-    for copy in copies:
-        copy.start()
-    for copy in copies:
-        copy.wait()
-    for i, rows in enumerate(blocks_of(half_rows, TALL)):
-        start = pl.multiple_of(base + i * TALL, TALL)
-        out_ref[rows, :] = unorder(rank_ref, start, TALL, length, shards, context_ref)
-
-
-def unorder_pair(shards, rank_row, own, other):
-    length = own.shape[0]
-    half_rows = length // 2
-    return pl.pallas_call(
-        functools.partial(unorder_kernel, shards),
-        out_shape=jax.ShapeDtypeStruct((half_rows, 2 * LANES), bf16),
-        in_specs=[ANYWHERE] * 3,
-        out_specs=pl.BlockSpec(memory_space=pltpu.VMEM),
-        scratch_shapes=[
-            pltpu.VMEM((1, length), jnp.int32),
-            pltpu.VMEM((length, 2 * LANES), bf16),
-            pltpu.SemaphoreType.DMA((3,)),
-        ],
-        compiler_params=params(),
-        cost_estimate=pl.CostEstimate(
-            flops=4 * half_rows * length * LANES, bytes_accessed=8 * length * LANES, transcendentals=0
-        ),
-    )(rank_row, own, other)
-
-
 def gelu_of_half(h):
     inner = 2 * math.sqrt(2 / math.pi)
     return h + h * jnp.tanh(h * (inner + (4 * 0.044715 * inner) * (h * h)))
@@ -328,7 +269,6 @@
     rank_hbm,
     gain_hbm,
     points_hbm,
-    first_hbm,
     own_hbm,
     other_hbm,
     out_own_hbm,
@@ -342,7 +282,6 @@
     rank_ref,
     gain_ref,
     points_ref,
-    first_ref,
     context_ref,
     out_ref,
     fc1_ref,
@@ -356,16 +295,13 @@
     half_rows = done_ref.shape[0]
     base = pl.multiple_of(lax.axis_index("mp") * half_rows, half_rows)
     hidden_half = fc2_own_hbm.shape[0]
-    early = [
-        (rank_hbm, rank_ref),
-        (own_hbm, context_ref.at[:, :LANES]),
-        (other_hbm, context_ref.at[:, LANES:]),
-    ]
-    later = [(first_hbm, first_ref), (gain_hbm, gain_ref), (points_hbm.at[pl.ds(base, half_rows)], points_ref)]
-    later += [
-        (ref.at[pair * LANES : (pair + 1) * LANES], out_ref.at[(2 * pair + k) * LANES : (2 * pair + k + 1) * LANES])
-        for pair in range(2)
-        for k, ref in enumerate((out_own_hbm, out_other_hbm))
+    half = out_own_hbm.shape[0]
+    early = [(rank_hbm, rank_ref), (own_hbm, context_ref.at[:, :half]), (other_hbm, context_ref.at[:, half:])]
+    later = [
+        (gain_hbm, gain_ref),
+        (points_hbm.at[pl.ds(base, half_rows)], points_ref),
+        (out_own_hbm, out_ref.at[:half]),
+        (out_other_hbm, out_ref.at[half:]),
     ]
     last = [
         (fc1_own_hbm, fc1_ref.at[:, :hidden_half]),
@@ -374,7 +310,7 @@
         (fc2_other_hbm, fc2_ref.at[hidden_half:]),
     ]
     copies = [pltpu.make_async_copy(*ends, in_sems.at[k]) for k, ends in enumerate(early + later + last)]
-    early, later, last = copies[:3], copies[3:10], copies[10:]
+    early, later, last = copies[:3], copies[3:7], copies[7:]
     for copy in copies:
         copy.start()
 
@@ -383,12 +319,11 @@
         copy.wait()
     for i, rows in enumerate(blocks):
         start = pl.multiple_of(base + i * TALL, TALL)
-        second = unorder(rank_ref, start, TALL, length, shards, context_ref)
+        context = unorder(rank_ref, start, TALL, length, shards, context_ref)
         if i == 0:
             for copy in later:
                 copy.wait()
-        split_at = 2 * LANES
-        attn_out = dot(first_ref[rows, :], out_ref[:split_at, :]) + dot(second, out_ref[split_at:, :])
+        attn_out = dot(context, out_ref[...])
         middle = (points_ref[rows, :].astype(f32) + attn_out.astype(bf16).astype(f32)).astype(bf16)
         middle_ref[rows, :] = middle
         normed_ref[rows, :] = normalise(middle.astype(f32), gain_ref[...]) * 0.5
@@ -430,20 +365,19 @@
             jax.ShapeDtypeStruct((half_rows, features), bf16),
             jax.ShapeDtypeStruct((length, features), bf16),
         ),
-        in_specs=[ANYWHERE] * 12,
+        in_specs=[ANYWHERE] * 11,
         out_specs=(pl.BlockSpec(memory_space=pltpu.VMEM), ANYWHERE),
         scratch_shapes=[
             pltpu.VMEM((1, length), jnp.int32),
             pltpu.VMEM((1, features), f32),
             pltpu.VMEM((half_rows, features), bf16),
-            pltpu.VMEM((half_rows, 2 * LANES), bf16),
-            pltpu.VMEM((length, 2 * LANES), bf16),
+            pltpu.VMEM((length, features), bf16),
             pltpu.VMEM((features, features), bf16),
             pltpu.VMEM((features, hidden), bf16),
             pltpu.VMEM((hidden, features), bf16),
             pltpu.VMEM((half_rows, features), bf16),
             pltpu.VMEM((half_rows, features), bf16),
-            pltpu.SemaphoreType.DMA((14,)),
+            pltpu.SemaphoreType.DMA((11,)),
             pltpu.SemaphoreType.DMA((half_rows // TALL,)),
         ],
         compiler_params=params(),
@@ -472,19 +406,16 @@
     own = exchange(order_for_owners(shards, rank_row, norm_gain_attn.reshape(1, features), points), shards)
     swapped = across(w_fc1), across(w_fc2), across(w_out)
     other = across(own)
-    first_own = exchange(attend(0, True, patch_counts, own, other, w_qkv), shards)
-    counts, (other_fc1, other_fc2, other_out) = lax.optimization_barrier((patch_counts, swapped))
-    second_own = exchange(attend(1, False, counts, own, other, w_qkv), shards)
-    first = unorder_pair(shards, rank_row, first_own, across(first_own))
-    second_own, first = lax.optimization_barrier((second_own, first))
+    context = attend(patch_counts, own, other, w_qkv)
+    context, (other_fc1, other_fc2, other_out) = lax.optimization_barrier((context, swapped))
+    returned = exchange(context, shards)
     done, whole = finish(
         shards,
         rank_row,
         norm_gain_mlp.reshape(1, features),
         points,
-        first,
-        second_own,
-        across(second_own),
+        returned,
+        across(returned),
         w_out,
         other_out,
         w_fc1,

time: 113 us -> 115 us (1.018)
  blocking collectives: 34.8 us -> 64.4 us
  waiting for transfers between devices: 20.9 us -> 7.03 us
  starting transfers between devices: 9.45 us -> 1.23 us
  Pallas kernels: 43.8 us -> 39.6 us
    all_to_all x1 -> x2, blocking collectives: 34.8 us -> 64.4 us  [exchange(): lax.all_to_all(cells, 'space', split_axis=0, concat_axis=0, tiled=True)]
    all_to_all x2 -> x0, waiting for transfers between devices: 11.9 us -> none  [exchange(): lax.all_to_all(cells, 'space', split_axis=0, concat_axis=0, tiled=True)]
    all_to_all x2 -> x0, starting transfers between devices: 8.16 us -> none  [exchange(): lax.all_to_all(cells, 'space', split_axis=0, concat_axis=0, tiled=True)]
    pallas_call x3 -> x1, Pallas kernels: 25.2 us -> 21 us  [attend(): pl.pallas_call(attend_kernel, out_shape=jax.ShapeDtypeStruct((length, col...]
    ppermute x7 -> x6, waiting for transfers between devices: 8.94 us -> 7.03 us  [across(): return lax.ppermute(values, 'mp', [(0, 1), (1, 0)])]
  transfers between devices with their start and end apart: 9 -> 6, of which waited for: 6 -> 3; matrix products, arithmetic and copies ran while one was open for 0% -> 0% of each run, Pallas kernels for 23% -> 18%
where the time goes in v4:
time: 115 us
  blocking collectives  64.4 us (56%)
  Pallas kernels  39.6 us (34%)
  waiting for transfers between devices  7.03 us (6%)
  local copies, waits for them, and re-layouts  2.05 us (2%)
  starting transfers between devices  1.23 us (1%)
    all_to_all x2, blocking collectives, exchange(): lax.all_to_all(cells, 'space', split_axis=0, concat_axis=0, tiled=True)  64.4 us
    pallas_call x1, Pallas kernels, attend(): pl.pallas_call(attend_kernel, out_shape=jax.ShapeDtypeStruct((length, col...  21 us
    pallas_call x1, Pallas kernels, finish(): pl.pallas_call(functools.partial(finish_kernel, shards), out_shape=(jax.S...  12 us
    ppermute x6, waiting for transfers between devices, across(): return lax.ppermute(values, 'mp', [(0, 1), (1, 0)])  7.03 us
    pallas_call x1, Pallas kernels, order_for_owners(): pl.pallas_call(functools.partial(send_kernel, shards), out_shape=jax.Shap...  6.59 us
  transfers between devices with their start and end apart: 6, of which 3 were waited for; matrix products, arithmetic and copies ran while one was open for 0% of the time, Pallas kernels for 18%

profile of v4, /device:TPU:0, one launch (start us, length us, event | category | flops | bytes accessed | tf_op | source)
XLA Modules:
  0.0 114.5 jit_solution(12190236786128579352)
XLA Ops:
  0.0 6.6 %shard_map.91 = bf16[2048,256]{1,0:T(8,128)(2,1)} custom-call(s32[1,2048]{1,0:T(1,128)} %bitcast.13, f32[1,512]{1,0:T(1,128)} %bitcast.15, bf16[2048,512]{1,0:T(8,128)(2,1)} %points_hbm.3), custom_call_target="tpu_custom_call" | custom-call | flops 2147483648 | bytes 4194304 | tf_op jit(solution)/shard_map/pallas_call | solution.py:103
  6.6 0.0 copy-start.3
  6.6 0.0 copy-start.8
  6.6 0.0 copy-start
  6.6 0.0 copy-start.1
  6.7 34.8 %all_to_all.10 = bf16[16,128,256]{2,1,0:T(8,128)(2,1)S(1)} all-to-all(bf16[16,128,256]{2,1,0:T(8,128)(2,1)} %bitcast.12), channel_id=1, replica_groups=mesh['space'=16,'mp'=2] {'space'}, dimensions={0} | all-to-all | bytes 2097152 | tf_op jit(solution)/shard_map/all_to_all | solution.py:399
  41.5 0.0 collective-permute-start
  41.5 0.0 copy-done.3
  41.5 0.5 collective-permute-start.1
  42.0 0.1 collective-permute-start.2
  42.1 0.4 collective-permute-start.3
  42.5 1.6 %collective-permute-done.other_ref = bf16[2048,256]{1,0:T(8,128)(2,1)S(1)} collective-permute-done((bf16[2048,256]{1,0:T(8,128)(2,1)S(1)}, bf16[2048,256]{1,0:T(8,128)(2,1)S(1)}, u32[]{:S(2)}, u32[]{:S(2)}) %collective-permute-start) | collective-permute-done | bytes 1048608 | tf_op jit(solution)/shard_map/ppermute | solution.py:393
  44.1 21.0 %shard_map.92 = bf16[2048,256]{1,0:T(8,128)(2,1)S(1)} custom-call(s32[1,4]{1,0:T(1,128)S(1)} %copy-done.1, bf16[2048,256]{1,0:T(8,128)(2,1)S(1)} %bitcast.8, bf16[2048,256]{1,0:T(8,128)(2,1)S(1)} %collective-permute-done.other_ref, bf16[3,512,256]{2,1,0:T(8,128)(2,1)S(1)} %copy-done), custom_call_target="tpu_custom_call" | custom-call | flops 17179869184 | bytes 4194304 | tf_op jit(solution)/shard_map/pallas_call | solution.py:234
  65.2 0.0 collective-permute-done.3.out_other_hbm
  65.2 0.0 collective-permute-done.1.fc1_other_hbm
  65.2 0.0 collective-permute-done.2.fc2_other_hbm
  65.2 29.6 %all_to_all.11 = bf16[16,128,256]{2,1,0:T(8,128)(2,1)S(1)} all-to-all(bf16[16,128,256]{2,1,0:T(8,128)(2,1)S(1)} %bitcast.9), channel_id=1, replica_groups=mesh['space'=16,'mp'=2] {'space'}, dimensions={0} | all-to-all | bytes 2097152 | tf_op jit(solution)/shard_map/all_to_all | solution.py:399
  94.9 0.0 collective-permute-start.4
  94.9 2.7 %collective-permute-done.4.other_hbm = bf16[2048,256]{1,0:T(8,128)(2,1)S(1)} collective-permute-done((bf16[2048,256]{1,0:T(8,128)(2,1)S(1)}, bf16[2048,256]{1,0:T(8,128)(2,1)S(1)}, u32[]{:S(2)}, u32[]{:S(2)}) %collective-permute-start.4) | collective-permute-done | bytes 1048608 | tf_op jit(solution)/shard_map/ppermute | solution.py:393
  97.6 1.0 copy-done.7
  98.5 12.0 %shard_map.93 = (bf16[1024,512]{1,0:T(8,128)(2,1)}, bf16[2048,512]{1,0:T(8,128)(2,1)}) custom-call(s32[1,2048]{1,0:T(1,128)} %bitcast.14, f32[1,512]{1,0:T(1,128)} %bitcast.16, bf16[2048,512]{1,0:T(8,128)(2,1)} %points_hbm.3, bf16[2048,256]{1,0:T(8,128)(2,1)} %bitcast.11, bf16[2048,256]{1,0:T(8,128)(2,1)} %copy-done.7, bf16[256,512]{1,0:T(8,128)(2,1)} %out_own_hbm.1, ...), custom_call_target="tpu_custom_call" | custom-call | flops 6979321856 | bytes 16777216 | tf_op jit(solution)/shard_map/pallas_call | solution.py:362
  110.5 0.2 collective-permute-start.5
  110.7 2.7 %collective-permute-done.5 = bf16[1024,512]{1,0:T(8,128)(2,1)S(1)} collective-permute-done((bf16[1024,512]{1,0:T(8,128)(2,1)}, bf16[1024,512]{1,0:T(8,128)(2,1)S(1)}, u32[]{:S(2)}, u32[]{:S(2)}) %collective-permute-start.5) | collective-permute-done | bytes 1048608 | tf_op jit(solution)/shard_map/ppermute | solution.py:393
  113.5 1.0 constant_dynamic-update-slice_fusion
  (14 shorter events, 0.0 us)
Async XLA Ops:
  0.0 42.0 %copy-start.4 = (bf16[1024,512]{1,0:T(8,128)(2,1)S(1)}, bf16[1024,512]{1,0:T(8,128)(2,1)}, u32[]{:S(2)}) copy-start(bf16[1024,512]{1,0:T(8,128)(2,1)} %fc2_own_hbm.1) | copy-start | bytes 3145732
  6.6 34.9 %copy-start.3 = (bf16[512,1024]{1,0:T(8,128)(2,1)S(1)}, bf16[512,1024]{1,0:T(8,128)(2,1)}, u32[]{:S(2)}) copy-start(bf16[512,1024]{1,0:T(8,128)(2,1)} %fc1_own_hbm.1) | copy-start | bytes 3145732
  6.6 35.5 %copy-start.8 = (bf16[256,512]{1,0:T(8,128)(2,1)S(1)}, bf16[256,512]{1,0:T(8,128)(2,1)}, u32[]{:S(2)}) copy-start(bf16[256,512]{1,0:T(8,128)(2,1)} %out_own_hbm.1) | copy-start | bytes 786436
  6.6 37.5 %copy-start = (bf16[3,512,256]{2,1,0:T(8,128)(2,1)S(1)}, bf16[3,512,256]{2,1,0:T(8,128)(2,1)}, u32[]{:S(2)}) copy-start(bf16[3,512,256]{2,1,0:T(8,128)(2,1)} %weight_hbm.1) | copy-start | bytes 2359300
  6.6 37.5 %copy-start.1 = (s32[1,4]{1,0:T(1,128)S(1)}, s32[1,4]{1,0:T(1,128)}, u32[]{:S(2)}) copy-start(s32[1,4]{1,0:T(1,128)} %counts_ref.1) | copy-start | bytes 52
  41.5 2.7 %collective-permute-start = (bf16[2048,256]{1,0:T(8,128)(2,1)S(1)}, bf16[2048,256]{1,0:T(8,128)(2,1)S(1)}, u32[]{:S(2)}, u32[]{:S(2)}) collective-permute-start(bf16[2048,256]{1,0:T(8,128)(2,1)S(1)} %bitcast.7), channel_id=1, source_target_pairs={{0,1},{1,0},{2,3},{3,2},{4,5},{5,4},{6,7},{7,6},{8,9},{9,8},{10,11... | collective-permute-start | bytes 3145736 | tf_op jit(solution)/shard_map/ppermute | solution.py:393
  41.5 23.7 %collective-permute-start.1 = (bf16[512,1024]{1,0:T(8,128)(2,1)S(1)}, bf16[512,1024]{1,0:T(8,128)(2,1)S(1)}, u32[]{:S(2)}, u32[]{:S(2)}) collective-permute-start(bf16[512,1024]{1,0:T(8,128)(2,1)S(1)} %copy-done.3), channel_id=1, source_target_pairs={{0,1},{1,0},{2,3},{3,2},{4,5},{5,4},{6,7},{7,6},{8,9},{9,8},{10,11... | collective-permute-start | bytes 3145736 | tf_op jit(solution)/shard_map/ppermute | solution.py:393
  42.0 23.2 %collective-permute-start.2 = (bf16[1024,512]{1,0:T(8,128)(2,1)S(1)}, bf16[1024,512]{1,0:T(8,128)(2,1)S(1)}, u32[]{:S(2)}, u32[]{:S(2)}) collective-permute-start(bf16[1024,512]{1,0:T(8,128)(2,1)S(1)} %copy-done.4), channel_id=1, source_target_pairs={{0,1},{1,0},{2,3},{3,2},{4,5},{5,4},{6,7},{7,6},{8,9},{9,8},{10,11... | collective-permute-start | bytes 3145736 | tf_op jit(solution)/shard_map/ppermute | solution.py:393
  42.1 23.1 %collective-permute-start.3 = (bf16[256,512]{1,0:T(8,128)(2,1)S(1)}, bf16[256,512]{1,0:T(8,128)(2,1)S(1)}, u32[]{:S(2)}, u32[]{:S(2)}) collective-permute-start(bf16[256,512]{1,0:T(8,128)(2,1)S(1)} %copy-done.8), channel_id=1, source_target_pairs={{0,1},{1,0},{2,3},{3,2},{4,5},{5,4},{6,7},{7,6},{8,9},{9,8},{10,11... | collective-permute-start | bytes 786440 | tf_op jit(solution)/shard_map/ppermute | solution.py:393
  65.2 32.3 %copy-start.9 = (bf16[256,512]{1,0:T(8,128)(2,1)}, bf16[256,512]{1,0:T(8,128)(2,1)S(1)}, u32[]{:S(2)}) copy-start(bf16[256,512]{1,0:T(8,128)(2,1)S(1)} %collective-permute-done.3.out_other_hbm) | copy-start | bytes 786436
  65.2 32.3 %copy-start.5 = (bf16[512,1024]{1,0:T(8,128)(2,1)}, bf16[512,1024]{1,0:T(8,128)(2,1)S(1)}, u32[]{:S(2)}) copy-start(bf16[512,1024]{1,0:T(8,128)(2,1)S(1)} %collective-permute-done.1.fc1_other_hbm) | copy-start | bytes 3145732
  65.2 32.3 %copy-start.6 = (bf16[1024,512]{1,0:T(8,128)(2,1)}, bf16[1024,512]{1,0:T(8,128)(2,1)S(1)}, u32[]{:S(2)}) copy-start(bf16[1024,512]{1,0:T(8,128)(2,1)S(1)} %collective-permute-done.2.fc2_other_hbm) | copy-start | bytes 3145732
  94.9 2.7 %copy-start.2 = (bf16[16,128,256]{2,1,0:T(8,128)(2,1)}, bf16[16,128,256]{2,1,0:T(8,128)(2,1)S(1)}, u32[]{:S(2)}) copy-start(bf16[16,128,256]{2,1,0:T(8,128)(2,1)S(1)} %all_to_all.11) | copy-start | bytes 3145732
  94.9 2.7 %collective-permute-start.4 = (bf16[2048,256]{1,0:T(8,128)(2,1)S(1)}, bf16[2048,256]{1,0:T(8,128)(2,1)S(1)}, u32[]{:S(2)}, u32[]{:S(2)}) collective-permute-start(bf16[2048,256]{1,0:T(8,128)(2,1)S(1)} %bitcast.10), channel_id=1, source_target_pairs={{0,1},{1,0},{2,3},{3,2},{4,5},{5,4},{6,7},{7,6},{8,9},{9,8},{10,11... | collective-permute-start | bytes 3145736 | tf_op jit(solution)/shard_map/ppermute | solution.py:393
  97.5 1.0 copy-start.7
  110.5 2.9 %collective-permute-start.5 = (bf16[1024,512]{1,0:T(8,128)(2,1)}, bf16[1024,512]{1,0:T(8,128)(2,1)S(1)}, u32[]{:S(2)}, u32[]{:S(2)}) collective-permute-start(bf16[1024,512]{1,0:T(8,128)(2,1)} %get-tuple-element.16), channel_id=1, source_target_pairs={{0,1},{1,0},{2,3},{3,2},{4,5},{5,4},{6,7},{7,6},{8,9},{9,8},{10,11... | collective-permute-start | bytes 3145736 | tf_op jit(solution)/shard_map/ppermute | solution.py:393

commit v5 on v4

--- a/solution.py
+++ b/solution.py
@@ -70,7 +70,7 @@
     return pltpu.CompilerParams(vmem_limit_bytes=limit)
 
 
-def send_kernel(shards, rank_hbm, gain_hbm, points_hbm, out_ref, rank_ref, gain_ref, points_ref, half_ref, small, large):
+def send_kernel(shards, by_rows, rank_hbm, gain_hbm, points_hbm, out_ref, rank_ref, gain_ref, points_ref, normed_ref, small, large):
     length, features = points_ref.shape
     half = features // 2
     core = lax.axis_index("mp")
@@ -89,27 +89,35 @@
     for copy, rows in zip(copies, rows_of):
         copy.wait()
         normed = normalise(points_ref[rows, :].astype(f32), gain_ref[...])
-        half_ref[rows, :] = jnp.where(core == 0, normed[:, :half], normed[:, half:])
+        if not by_rows:
+            normed = jnp.where(core == 0, normed[:, :half], normed[:, half:])
+        normed_ref[rows, :] = normed
     rank_copy.wait()
     slot = slots(rank_ref[...], length, shards)
+    if by_rows:
+        half_cell = length // shards // 2
+        piece, row = split(slot, half_cell)
+        owner, which = split(piece, 2)
+        slot = jnp.where(which == core, owner * half_cell + row, length)
 
     place = lax.broadcasted_iota(jnp.int32, (TALL, LANES), 0)
-    for i, rows in enumerate(blocks_of(length, TALL)):
-        out_ref[rows, :] = dot(one_hot(place + i * TALL, slot), half_ref[...]).astype(bf16)
-
-
-def order_for_owners(shards, rank_row, gain_row, points):
+    for i, rows in enumerate(blocks_of(out_ref.shape[0], TALL)):
+        out_ref[rows, :] = dot(one_hot(place + i * TALL, slot), normed_ref[...]).astype(bf16)
+
+
+def order_for_owners(shards, by_rows, rank_row, gain_row, points):
     length, features = points.shape
+    rows, columns = (length // 2, features) if by_rows else (length, features // 2)
     return pl.pallas_call(
-        functools.partial(send_kernel, shards),
-        out_shape=jax.ShapeDtypeStruct((length, features // 2), bf16),
+        functools.partial(send_kernel, shards, by_rows),
+        out_shape=jax.ShapeDtypeStruct((rows, columns), bf16),
         in_specs=[ANYWHERE] * 3,
         out_specs=pl.BlockSpec(memory_space=pltpu.VMEM),
         scratch_shapes=[
             pltpu.VMEM((1, length), jnp.int32),
             pltpu.VMEM((1, features), f32),
             pltpu.VMEM((length, features), bf16),
-            pltpu.VMEM((length, features // 2), bf16),
+            pltpu.VMEM((length, columns), bf16),
             pltpu.SemaphoreType.DMA((2,)),
             pltpu.SemaphoreType.DMA((length // ROWS,)),
         ],
@@ -120,19 +128,31 @@
     )(rank_row, gain_row, points)
 
 
+def interleave(own_ref, other_ref, start, half_cell, core):
+    halves = []
+    for at in range(start, start + TALL // 2, half_cell):
+        mine, theirs = (ref[at : at + half_cell, :] for ref in (own_ref, other_ref))
+        halves += [jnp.where(core == 0, mine, theirs), jnp.where(core == 0, theirs, mine)]
+    return jnp.concatenate(halves, axis=0)
+
+
 def attend_kernel(
-    counts_ref, own_ref, other_ref, weight_hbm, out_hbm, w_ref, q_ref, k_ref, v_ref, out_ref, w_sems, out_sems
+    half_cell, counts_ref, own_ref, other_ref, weight_hbm, out_hbm, w_ref, q_ref, k_ref, v_ref, out_ref, w_sems, out_sems
 ):
-    length, half = own_ref.shape
+    length, features = q_ref.shape[1], w_ref.shape[0]
+    half = features // 2
     tiles = counts_ref.shape[1]
     pairs = out_ref.shape[0]
     core = lax.axis_index("mp")
     scale = math.log2(math.e) / math.sqrt(HDIM)
 
+    def in_rows(k, at):
+        return pl.ds(pl.multiple_of((at if half_cell else k) * half, half), half)
+
     copies = [
         pltpu.make_async_copy(
             weight_hbm.at[j, pl.ds(pl.multiple_of(at * half, half), half)],
-            w_ref.at[k * half : (k + 1) * half, j * pairs * LANES : (j + 1) * pairs * LANES],
+            w_ref.at[in_rows(k, at), j * pairs * LANES : (j + 1) * pairs * LANES],
             w_sems.at[2 * j + k],
         )
         for j in range(3)
@@ -157,7 +177,11 @@
         copy.wait()
 
     for i, rows in enumerate(blocks_of(length, TALL)):
-        spread = dot(own_ref[rows, :], w_ref[:half, :]) + dot(other_ref[rows, :], w_ref[half:, :])
+        if half_cell:
+            block = interleave(own_ref, other_ref, i * TALL // 2, half_cell, core)
+            spread = dot(block, w_ref[...])
+        else:
+            spread = dot(own_ref[rows, :], w_ref[:half, :]) + dot(other_ref[rows, :], w_ref[half:, :])
         place = lax.broadcasted_iota(jnp.int32, (TALL, LANES), 0) + i * TALL
         inside = jnp.logical_and(place >= first, place < last)
         q_flag = jnp.where(inside, 1.0, 0.0)
@@ -174,7 +198,7 @@
             v_ref[2 * pair + 1, :HDIM, rows] = v[HDIM:]
 
     def weigh(scores):
-        return jnp.exp2(scores - jnp.max(scores, axis=0, keepdims=True)).astype(bf16)
+        return jnp.exp2((scores - jnp.max(scores, axis=0, keepdims=True)).astype(bf16))
 
     def send_out(i, pair):
         rows = pl.ds(pl.multiple_of(i * TALL, TALL), TALL)
@@ -226,13 +250,13 @@
             send_out(i, pair).wait()
 
 
-def attend(counts, own, other, w_qkv):
-    length, half = own.shape
+def attend(half_cell, counts, own, other, w_qkv):
     features, columns = w_qkv.shape[1:]
+    length = own.size * 2 // features
     heads = columns // HDIM
     held = pl.BlockSpec(memory_space=pltpu.VMEM)
     return pl.pallas_call(
-        attend_kernel,
+        functools.partial(attend_kernel, half_cell),
         out_shape=jax.ShapeDtypeStruct((length, columns), bf16),
         in_specs=[SCALARS, held, held, ANYWHERE],
         out_specs=ANYWHERE,
@@ -247,7 +271,7 @@
         ],
         compiler_params=params(SMALL_BYTES),
         cost_estimate=pl.CostEstimate(
-            flops=64 * length * length * HDIM, bytes_accessed=8 * length * half, transcendentals=4 * length * length
+            flops=64 * length * length * HDIM, bytes_accessed=4 * length * features, transcendentals=4 * length * length
         ),
     )(counts, own, other, w_qkv)
 
@@ -403,10 +427,12 @@
     shards = lax.axis_size("space")
     length, features = points.shape
     rank_row = curve_rank.reshape(1, length)
-    own = exchange(order_for_owners(shards, rank_row, norm_gain_attn.reshape(1, features), points), shards)
+    half_cell = length // shards // 2
+    half_cell = half_cell if half_cell % 16 == 0 and half_cell <= TALL // 2 else 0
+    own = exchange(order_for_owners(shards, half_cell > 0, rank_row, norm_gain_attn.reshape(1, features), points), shards)
     swapped = across(w_fc1), across(w_fc2), across(w_out)
     other = across(own)
-    context = attend(patch_counts, own, other, w_qkv)
+    context = attend(half_cell, patch_counts, own, other, w_qkv)
     context, (other_fc1, other_fc2, other_out) = lax.optimization_barrier((context, swapped))
     returned = exchange(context, shards)
     done, whole = finish(

time: 115 us -> 117 us (1.017)
  blocking collectives: 64.4 us -> 70.3 us
  Pallas kernels: 39.6 us -> 36.1 us
    all_to_all x2, blocking collectives: 64.4 us -> 70.3 us  [exchange(): lax.all_to_all(cells, 'space', split_axis=0, concat_axis=0, tiled=True)]
    pallas_call x2, Pallas kernels: 27.6 us -> 24.1 us  [the longest x1 17.5 us: attend(): pl.pallas_call(functools.partial(attend_kernel, half_cell), out_shape=jax...]
  transfers between devices with their start and end apart: 6 -> 6, of which waited for: 3 -> 3; matrix products, arithmetic and copies ran while one was open for 0% -> 0% of each run, Pallas kernels for 18% -> 15%
where the time goes in v5:
time: 117 us
  blocking collectives  70.3 us (60%)
  Pallas kernels  36.1 us (31%)
  waiting for transfers between devices  7.03 us (6%)
  local copies, waits for them, and re-layouts  2.05 us (2%)
  starting transfers between devices  1.22 us (1%)
    all_to_all x2, blocking collectives, exchange(): lax.all_to_all(cells, 'space', split_axis=0, concat_axis=0, tiled=True)  70.3 us
    pallas_call x1, Pallas kernels, attend(): pl.pallas_call(functools.partial(attend_kernel, half_cell), out_shape=jax...  17.5 us
    pallas_call x1, Pallas kernels, finish(): pl.pallas_call(functools.partial(finish_kernel, shards), out_shape=(jax.S...  12 us
    ppermute x6, waiting for transfers between devices, across(): return lax.ppermute(values, 'mp', [(0, 1), (1, 0)])  7.03 us
    pallas_call x1, Pallas kernels, order_for_owners(): pl.pallas_call(functools.partial(send_kernel, shards, by_rows), out_shape...  6.55 us
  transfers between devices with their start and end apart: 6, of which 3 were waited for; matrix products, arithmetic and copies ran while one was open for 0% of the time, Pallas kernels for 15%

profile of v5, /device:TPU:0, one launch (start us, length us, event | category | flops | bytes accessed | tf_op | source)
XLA Modules:
  0.0 116.9 jit_solution(1891131575484670153)
XLA Ops:
  0.0 6.6 %shard_map.91 = bf16[1024,512]{1,0:T(8,128)(2,1)} custom-call(s32[1,2048]{1,0:T(1,128)} %bitcast.13, f32[1,512]{1,0:T(1,128)} %bitcast.15, bf16[2048,512]{1,0:T(8,128)(2,1)} %points_hbm.3), custom_call_target="tpu_custom_call" | custom-call | flops 2147483648 | bytes 4194304 | tf_op jit(solution)/shard_map/pallas_call | solution.py:111
  6.6 0.0 copy-start.3
  6.6 0.0 copy-start.8
  6.6 0.0 copy-start
  6.6 0.0 copy-start.1
  6.6 34.8 %all_to_all.10 = bf16[16,64,512]{2,1,0:T(8,128)(2,1)S(1)} all-to-all(bf16[16,64,512]{2,1,0:T(8,128)(2,1)} %bitcast.12), channel_id=1, replica_groups=mesh['space'=16,'mp'=2] {'space'}, dimensions={0} | all-to-all | bytes 2097152 | tf_op jit(solution)/shard_map/all_to_all | solution.py:423
  41.4 0.0 collective-permute-start
  41.4 0.5 collective-permute-start.1
  42.0 0.0 copy-done.4
  42.0 0.1 collective-permute-start.2
  42.0 0.4 collective-permute-start.3
  42.5 1.6 %collective-permute-done.other_ref = bf16[1024,512]{1,0:T(8,128)(2,1)S(1)} collective-permute-done((bf16[1024,512]{1,0:T(8,128)(2,1)S(1)}, bf16[1024,512]{1,0:T(8,128)(2,1)S(1)}, u32[]{:S(2)}, u32[]{:S(2)}) %collective-permute-start) | collective-permute-done | bytes 1048608 | tf_op jit(solution)/shard_map/ppermute | solution.py:417
  44.1 17.5 %shard_map.92 = bf16[2048,256]{1,0:T(8,128)(2,1)S(1)} custom-call(s32[1,4]{1,0:T(1,128)S(1)} %copy-done.1, bf16[1024,512]{1,0:T(8,128)(2,1)S(1)} %bitcast.8, bf16[1024,512]{1,0:T(8,128)(2,1)S(1)} %collective-permute-done.other_ref, bf16[3,512,256]{2,1,0:T(8,128)(2,1)S(1)} %copy-done), custom_call_target="tpu_custom_call" | custom-call | flops 17179869184 | bytes 4194304 | tf_op jit(solution)/shard_map/pallas_call | solution.py:258
  61.6 0.0 collective-permute-done.3.out_other_hbm
  61.7 0.0 collective-permute-done.1.fc1_other_hbm
  61.7 0.0 collective-permute-done.2.fc2_other_hbm
  61.7 35.5 %all_to_all.11 = bf16[16,128,256]{2,1,0:T(8,128)(2,1)S(1)} all-to-all(bf16[16,128,256]{2,1,0:T(8,128)(2,1)S(1)} %bitcast.9), channel_id=1, replica_groups=mesh['space'=16,'mp'=2] {'space'}, dimensions={0} | all-to-all | bytes 2097152 | tf_op jit(solution)/shard_map/all_to_all | solution.py:423
  97.2 0.0 collective-permute-start.4
  97.2 2.7 %collective-permute-done.4.other_hbm = bf16[2048,256]{1,0:T(8,128)(2,1)S(1)} collective-permute-done((bf16[2048,256]{1,0:T(8,128)(2,1)S(1)}, bf16[2048,256]{1,0:T(8,128)(2,1)S(1)}, u32[]{:S(2)}, u32[]{:S(2)}) %collective-permute-start.4) | collective-permute-done | bytes 1048608 | tf_op jit(solution)/shard_map/ppermute | solution.py:417
  99.9 1.0 copy-done.7
  100.9 12.0 %shard_map.93 = (bf16[1024,512]{1,0:T(8,128)(2,1)}, bf16[2048,512]{1,0:T(8,128)(2,1)}) custom-call(s32[1,2048]{1,0:T(1,128)} %bitcast.14, f32[1,512]{1,0:T(1,128)} %bitcast.16, bf16[2048,512]{1,0:T(8,128)(2,1)} %points_hbm.3, bf16[2048,256]{1,0:T(8,128)(2,1)} %bitcast.11, bf16[2048,256]{1,0:T(8,128)(2,1)} %copy-done.7, bf16[256,512]{1,0:T(8,128)(2,1)} %out_own_hbm.1, ...), custom_call_target="tpu_custom_call" | custom-call | flops 6979321856 | bytes 16777216 | tf_op jit(solution)/shard_map/pallas_call | solution.py:386
  112.9 0.2 collective-permute-start.5
  113.1 2.7 %collective-permute-done.5 = bf16[1024,512]{1,0:T(8,128)(2,1)S(1)} collective-permute-done((bf16[1024,512]{1,0:T(8,128)(2,1)}, bf16[1024,512]{1,0:T(8,128)(2,1)S(1)}, u32[]{:S(2)}, u32[]{:S(2)}) %collective-permute-start.5) | collective-permute-done | bytes 1048608 | tf_op jit(solution)/shard_map/ppermute | solution.py:417
  115.8 1.0 constant_dynamic-update-slice_fusion
  (14 shorter events, 0.0 us)
Async XLA Ops:
  0.0 42.0 %copy-start.4 = (bf16[1024,512]{1,0:T(8,128)(2,1)S(1)}, bf16[1024,512]{1,0:T(8,128)(2,1)}, u32[]{:S(2)}) copy-start(bf16[1024,512]{1,0:T(8,128)(2,1)} %fc2_own_hbm.1) | copy-start | bytes 3145732
  6.6 34.9 %copy-start.3 = (bf16[512,1024]{1,0:T(8,128)(2,1)S(1)}, bf16[512,1024]{1,0:T(8,128)(2,1)}, u32[]{:S(2)}) copy-start(bf16[512,1024]{1,0:T(8,128)(2,1)} %fc1_own_hbm.1) | copy-start | bytes 3145732
  6.6 35.5 %copy-start.8 = (bf16[256,512]{1,0:T(8,128)(2,1)S(1)}, bf16[256,512]{1,0:T(8,128)(2,1)}, u32[]{:S(2)}) copy-start(bf16[256,512]{1,0:T(8,128)(2,1)} %out_own_hbm.1) | copy-start | bytes 786436
  6.6 37.5 %copy-start = (bf16[3,512,256]{2,1,0:T(8,128)(2,1)S(1)}, bf16[3,512,256]{2,1,0:T(8,128)(2,1)}, u32[]{:S(2)}) copy-start(bf16[3,512,256]{2,1,0:T(8,128)(2,1)} %weight_hbm.1) | copy-start | bytes 2359300
  6.6 37.5 %copy-start.1 = (s32[1,4]{1,0:T(1,128)S(1)}, s32[1,4]{1,0:T(1,128)}, u32[]{:S(2)}) copy-start(s32[1,4]{1,0:T(1,128)} %counts_ref.1) | copy-start | bytes 52
  41.4 2.7 %collective-permute-start = (bf16[1024,512]{1,0:T(8,128)(2,1)S(1)}, bf16[1024,512]{1,0:T(8,128)(2,1)S(1)}, u32[]{:S(2)}, u32[]{:S(2)}) collective-permute-start(bf16[1024,512]{1,0:T(8,128)(2,1)S(1)} %bitcast.7), channel_id=1, source_target_pairs={{0,1},{1,0},{2,3},{3,2},{4,5},{5,4},{6,7},{7,6},{8,9},{9,8},{10,11... | collective-permute-start | bytes 3145736 | tf_op jit(solution)/shard_map/ppermute | solution.py:417
  41.4 20.2 %collective-permute-start.1 = (bf16[512,1024]{1,0:T(8,128)(2,1)S(1)}, bf16[512,1024]{1,0:T(8,128)(2,1)S(1)}, u32[]{:S(2)}, u32[]{:S(2)}) collective-permute-start(bf16[512,1024]{1,0:T(8,128)(2,1)S(1)} %copy-done.3), channel_id=1, source_target_pairs={{0,1},{1,0},{2,3},{3,2},{4,5},{5,4},{6,7},{7,6},{8,9},{9,8},{10,11... | collective-permute-start | bytes 3145736 | tf_op jit(solution)/shard_map/ppermute | solution.py:417
  42.0 19.7 %collective-permute-start.2 = (bf16[1024,512]{1,0:T(8,128)(2,1)S(1)}, bf16[1024,512]{1,0:T(8,128)(2,1)S(1)}, u32[]{:S(2)}, u32[]{:S(2)}) collective-permute-start(bf16[1024,512]{1,0:T(8,128)(2,1)S(1)} %copy-done.4), channel_id=1, source_target_pairs={{0,1},{1,0},{2,3},{3,2},{4,5},{5,4},{6,7},{7,6},{8,9},{9,8},{10,11... | collective-permute-start | bytes 3145736 | tf_op jit(solution)/shard_map/ppermute | solution.py:417
  42.0 19.6 %collective-permute-start.3 = (bf16[256,512]{1,0:T(8,128)(2,1)S(1)}, bf16[256,512]{1,0:T(8,128)(2,1)S(1)}, u32[]{:S(2)}, u32[]{:S(2)}) collective-permute-start(bf16[256,512]{1,0:T(8,128)(2,1)S(1)} %copy-done.8), channel_id=1, source_target_pairs={{0,1},{1,0},{2,3},{3,2},{4,5},{5,4},{6,7},{7,6},{8,9},{9,8},{10,11... | collective-permute-start | bytes 786440 | tf_op jit(solution)/shard_map/ppermute | solution.py:417
  61.6 38.2 %copy-start.9 = (bf16[256,512]{1,0:T(8,128)(2,1)}, bf16[256,512]{1,0:T(8,128)(2,1)S(1)}, u32[]{:S(2)}) copy-start(bf16[256,512]{1,0:T(8,128)(2,1)S(1)} %collective-permute-done.3.out_other_hbm) | copy-start | bytes 786436
  61.7 38.2 %copy-start.5 = (bf16[512,1024]{1,0:T(8,128)(2,1)}, bf16[512,1024]{1,0:T(8,128)(2,1)S(1)}, u32[]{:S(2)}) copy-start(bf16[512,1024]{1,0:T(8,128)(2,1)S(1)} %collective-permute-done.1.fc1_other_hbm) | copy-start | bytes 3145732
  61.7 38.2 %copy-start.6 = (bf16[1024,512]{1,0:T(8,128)(2,1)}, bf16[1024,512]{1,0:T(8,128)(2,1)S(1)}, u32[]{:S(2)}) copy-start(bf16[1024,512]{1,0:T(8,128)(2,1)S(1)} %collective-permute-done.2.fc2_other_hbm) | copy-start | bytes 3145732
  97.2 2.7 %copy-start.2 = (bf16[16,128,256]{2,1,0:T(8,128)(2,1)}, bf16[16,128,256]{2,1,0:T(8,128)(2,1)S(1)}, u32[]{:S(2)}) copy-start(bf16[16,128,256]{2,1,0:T(8,128)(2,1)S(1)} %all_to_all.11) | copy-start | bytes 3145732
  97.2 2.7 %collective-permute-start.4 = (bf16[2048,256]{1,0:T(8,128)(2,1)S(1)}, bf16[2048,256]{1,0:T(8,128)(2,1)S(1)}, u32[]{:S(2)}, u32[]{:S(2)}) collective-permute-start(bf16[2048,256]{1,0:T(8,128)(2,1)S(1)} %bitcast.10), channel_id=1, source_target_pairs={{0,1},{1,0},{2,3},{3,2},{4,5},{5,4},{6,7},{7,6},{8,9},{9,8},{10,11... | collective-permute-start | bytes 3145736 | tf_op jit(solution)/shard_map/ppermute | solution.py:417
  99.9 1.0 copy-start.7
  112.9 2.9 %collective-permute-start.5 = (bf16[1024,512]{1,0:T(8,128)(2,1)}, bf16[1024,512]{1,0:T(8,128)(2,1)S(1)}, u32[]{:S(2)}, u32[]{:S(2)}) collective-permute-start(bf16[1024,512]{1,0:T(8,128)(2,1)} %get-tuple-element.16), channel_id=1, source_target_pairs={{0,1},{1,0},{2,3},{3,2},{4,5},{5,4},{6,7},{7,6},{8,9},{9,8},{10,11... | collective-permute-start | bytes 3145736 | tf_op jit(solution)/shard_map/ppermute | solution.py:417

commit v6 on v4

--- a/solution.py
+++ b/solution.py
@@ -16,6 +16,7 @@
 PADDED = HDIM + 16
 EPSILON = 1e-06
 FAR = 1e30
+SAFE = 105.0
 VMEM_BYTES = 58 * 1024 * 1024
 SMALL_BYTES = 30 * 1024 * 1024
 
@@ -156,6 +157,11 @@
     for copy in copies:
         copy.wait()
 
+    most = [[jnp.zeros((1, 1), f32)] * 2 for _ in range(pairs)]
+
+    def squares(values):
+        return jnp.max(jnp.sum(values * values, axis=1, keepdims=True), axis=0, keepdims=True)
+
     for i, rows in enumerate(blocks_of(length, TALL)):
         spread = dot(own_ref[rows, :], w_ref[:half, :]) + dot(other_ref[rows, :], w_ref[half:, :])
         place = lax.broadcasted_iota(jnp.int32, (TALL, LANES), 0) + i * TALL
@@ -165,6 +171,7 @@
         for pair in range(pairs):
             q, k, v = (spread[:, (j * pairs + pair) * LANES : (j * pairs + pair + 1) * LANES] for j in range(3))
             q = q * scale
+            most[pair] = [jnp.maximum(old, squares(new)) for old, new in zip(most[pair], (q, k))]
             q_ref[2 * pair, rows, :] = jnp.where(low_lanes, q, q_flag).astype(bf16)
             q_ref[2 * pair + 1, rows, :] = jnp.where(low_lanes, pltpu.roll(q, HDIM, 1), q_flag).astype(bf16)
             k_ref[2 * pair, rows, :] = jnp.where(low_lanes, k, k_flag).astype(bf16)
@@ -173,8 +180,31 @@
             v_ref[2 * pair, :HDIM, rows] = v[:HDIM]
             v_ref[2 * pair + 1, :HDIM, rows] = v[HDIM:]
 
-    def weigh(scores):
-        return jnp.exp2(scores - jnp.max(scores, axis=0, keepdims=True)).astype(bf16)
+    bound = functools.reduce(jnp.maximum, [q_most * k_most for q_most, k_most in most])
+    safe = jnp.max(bound) < SAFE * SAFE
+
+    def attend_pair(pair, rows, keys, shifted):
+        scores = [
+            lax.dot_general(
+                k_ref[2 * pair + h, keys, :],
+                q_ref[2 * pair + h, rows, :],
+                (((1,), (1,)), ((), ())),
+                preferred_element_type=f32,
+            )
+            for h in range(2)
+        ]
+        if shifted:
+            scores = [values - jnp.max(values, axis=0, keepdims=True) for values in scores]
+        sums = [dot(v_ref[2 * pair + h, :, keys], jnp.exp2(scores[h]).astype(bf16)) for h in range(2)]
+        value = jnp.concatenate([both[:HDIM] / both[HDIM : HDIM + 1] for both in sums], axis=0)
+        out_ref[pair, rows, :] = jnp.transpose(value).astype(bf16)
+
+    def attend_rows(rows, keys, shifted):
+        def one_pair(pair, carry):
+            attend_pair(pair, rows, keys, shifted)
+            return carry
+
+        lax.fori_loop(0, pairs, one_pair, 0)
 
     def send_out(i, pair):
         rows = pl.ds(pl.multiple_of(i * TALL, TALL), TALL)
@@ -194,27 +224,14 @@
         blocks = (high - low + KEYS - 1) // KEYS
         for n in range(TALL // KEYS, length // KEYS + 1):
 
-            @pl.when(blocks == n)
+            @pl.when(jnp.logical_and(safe, blocks == n))
             def _(n=n):
                 start = pl.multiple_of(jnp.minimum(low, length - n * KEYS), LANES)
-                keys = pl.ds(start, n * KEYS)
-
-                def one_pair(pair, carry):
-                    scores = [
-                        lax.dot_general(
-                            k_ref[2 * pair + h, keys, :],
-                            q_ref[2 * pair + h, rows, :],
-                            (((1,), (1,)), ((), ())),
-                            preferred_element_type=f32,
-                        )
-                        for h in range(2)
-                    ]
-                    sums = [dot(v_ref[2 * pair + h, :, keys], weigh(scores[h])) for h in range(2)]
-                    value = jnp.concatenate([both[:HDIM] / both[HDIM : HDIM + 1] for both in sums], axis=0)
-                    out_ref[pair, rows, :] = jnp.transpose(value).astype(bf16)
-                    return carry
-
-                lax.fori_loop(0, pairs, one_pair, 0)
+                attend_rows(rows, pl.ds(start, n * KEYS), False)
+
+        @pl.when(jnp.logical_not(safe))
+        def _():
+            attend_rows(rows, slice(None), True)
 
         for pair in range(pairs):
             send_out(i, pair).start()

time: 115 us -> 127 us (1.10)
  Pallas kernels: 39.6 us -> 51.3 us
    pallas_call x1, Pallas kernels: 21 us -> 32.7 us  [attend(): pl.pallas_call(attend_kernel, out_shape=jax.ShapeDtypeStruct((length, col...]
  transfers between devices with their start and end apart: 6 -> 6, of which waited for: 3 -> 3; matrix products, arithmetic and copies ran while one was open for 0% -> 0% of each run, Pallas kernels for 18% -> 26%
where the time goes in v6:
time: 127 us
  blocking collectives  65.2 us (51%)
  Pallas kernels  51.3 us (40%)
  waiting for transfers between devices  7.03 us (6%)
  local copies, waits for them, and re-layouts  2.05 us (2%)
    all_to_all x2, blocking collectives, exchange(): lax.all_to_all(cells, 'space', split_axis=0, concat_axis=0, tiled=True)  65.2 us
    pallas_call x1, Pallas kernels, attend(): pl.pallas_call(attend_kernel, out_shape=jax.ShapeDtypeStruct((length, col...  32.7 us
    pallas_call x1, Pallas kernels, finish(): pl.pallas_call(functools.partial(finish_kernel, shards), out_shape=(jax.S...  12 us
    ppermute x6, waiting for transfers between devices, across(): return lax.ppermute(values, 'mp', [(0, 1), (1, 0)])  7.03 us
    pallas_call x1, Pallas kernels, order_for_owners(): pl.pallas_call(functools.partial(send_kernel, shards), out_shape=jax.Shap...  6.59 us
  transfers between devices with their start and end apart: 6, of which 3 were waited for; matrix products, arithmetic and copies ran while one was open for 0% of the time, Pallas kernels for 26%

profile of v6, /device:TPU:0, one launch (start us, length us, event | category | flops | bytes accessed | tf_op | source)
XLA Modules:
  0.0 126.9 jit_solution(1949534439333109448)
XLA Ops:
  0.0 6.6 %shard_map.91 = bf16[2048,256]{1,0:T(8,128)(2,1)} custom-call(s32[1,2048]{1,0:T(1,128)} %bitcast.13, f32[1,512]{1,0:T(1,128)} %bitcast.15, bf16[2048,512]{1,0:T(8,128)(2,1)} %points_hbm.3), custom_call_target="tpu_custom_call" | custom-call | flops 2147483648 | bytes 4194304 | tf_op jit(solution)/shard_map/pallas_call | solution.py:104
  6.6 0.0 copy-start.3
  6.6 0.0 copy-start.8
  6.6 0.0 copy-start
  6.6 0.0 copy-start.1
  6.7 34.8 %all_to_all.10 = bf16[16,128,256]{2,1,0:T(8,128)(2,1)S(1)} all-to-all(bf16[16,128,256]{2,1,0:T(8,128)(2,1)} %bitcast.12), channel_id=1, replica_groups=mesh['space'=16,'mp'=2] {'space'}, dimensions={0} | all-to-all | bytes 2097152 | tf_op jit(solution)/shard_map/all_to_all | solution.py:416
  41.5 0.0 collective-permute-start
  41.5 0.5 collective-permute-start.1
  42.0 0.1 collective-permute-start.2
  42.1 0.4 collective-permute-start.3
  42.5 1.6 %collective-permute-done.other_ref = bf16[2048,256]{1,0:T(8,128)(2,1)S(1)} collective-permute-done((bf16[2048,256]{1,0:T(8,128)(2,1)S(1)}, bf16[2048,256]{1,0:T(8,128)(2,1)S(1)}, u32[]{:S(2)}, u32[]{:S(2)}) %collective-permute-start) | collective-permute-done | bytes 1048608 | tf_op jit(solution)/shard_map/ppermute | solution.py:410
  44.1 0.0 copy-done
  44.1 32.7 %shard_map.92 = bf16[2048,256]{1,0:T(8,128)(2,1)S(1)} custom-call(s32[1,4]{1,0:T(1,128)S(1)} %copy-done.1, bf16[2048,256]{1,0:T(8,128)(2,1)S(1)} %bitcast.8, bf16[2048,256]{1,0:T(8,128)(2,1)S(1)} %collective-permute-done.other_ref, bf16[3,512,256]{2,1,0:T(8,128)(2,1)S(1)} %copy-done), custom_call_target="tpu_custom_call" | custom-call | flops 17179869184 | bytes 4194304 | tf_op jit(solution)/shard_map/pallas_call | solution.py:251
  76.9 0.0 collective-permute-done.3.out_other_hbm
  76.9 0.0 collective-permute-done.1.fc1_other_hbm
  76.9 0.0 collective-permute-done.2.fc2_other_hbm
  76.9 30.3 %all_to_all.11 = bf16[16,128,256]{2,1,0:T(8,128)(2,1)S(1)} all-to-all(bf16[16,128,256]{2,1,0:T(8,128)(2,1)S(1)} %bitcast.9), channel_id=1, replica_groups=mesh['space'=16,'mp'=2] {'space'}, dimensions={0} | all-to-all | bytes 2097152 | tf_op jit(solution)/shard_map/all_to_all | solution.py:416
  107.2 0.0 collective-permute-start.4
  107.2 2.7 %collective-permute-done.4.other_hbm = bf16[2048,256]{1,0:T(8,128)(2,1)S(1)} collective-permute-done((bf16[2048,256]{1,0:T(8,128)(2,1)S(1)}, bf16[2048,256]{1,0:T(8,128)(2,1)S(1)}, u32[]{:S(2)}, u32[]{:S(2)}) %collective-permute-start.4) | collective-permute-done | bytes 1048608 | tf_op jit(solution)/shard_map/ppermute | solution.py:410
  109.9 1.0 copy-done.7
  110.9 12.0 %shard_map.93 = (bf16[1024,512]{1,0:T(8,128)(2,1)}, bf16[2048,512]{1,0:T(8,128)(2,1)}) custom-call(s32[1,2048]{1,0:T(1,128)} %bitcast.14, f32[1,512]{1,0:T(1,128)} %bitcast.16, bf16[2048,512]{1,0:T(8,128)(2,1)} %points_hbm.3, bf16[2048,256]{1,0:T(8,128)(2,1)} %bitcast.11, bf16[2048,256]{1,0:T(8,128)(2,1)} %copy-done.7, bf16[256,512]{1,0:T(8,128)(2,1)} %out_own_hbm.1, ...), custom_call_target="tpu_custom_call" | custom-call | flops 6979321856 | bytes 16777216 | tf_op jit(solution)/shard_map/pallas_call | solution.py:379
  122.9 0.2 collective-permute-start.5
  123.1 2.7 %collective-permute-done.5 = bf16[1024,512]{1,0:T(8,128)(2,1)S(1)} collective-permute-done((bf16[1024,512]{1,0:T(8,128)(2,1)}, bf16[1024,512]{1,0:T(8,128)(2,1)S(1)}, u32[]{:S(2)}, u32[]{:S(2)}) %collective-permute-start.5) | collective-permute-done | bytes 1048608 | tf_op jit(solution)/shard_map/ppermute | solution.py:410
  125.9 1.0 constant_dynamic-update-slice_fusion
  (14 shorter events, 0.0 us)
Async XLA Ops:
  0.0 42.0 %copy-start.4 = (bf16[1024,512]{1,0:T(8,128)(2,1)S(1)}, bf16[1024,512]{1,0:T(8,128)(2,1)}, u32[]{:S(2)}) copy-start(bf16[1024,512]{1,0:T(8,128)(2,1)} %fc2_own_hbm.1) | copy-start | bytes 3145732
  6.6 34.9 %copy-start.3 = (bf16[512,1024]{1,0:T(8,128)(2,1)S(1)}, bf16[512,1024]{1,0:T(8,128)(2,1)}, u32[]{:S(2)}) copy-start(bf16[512,1024]{1,0:T(8,128)(2,1)} %fc1_own_hbm.1) | copy-start | bytes 3145732
  6.6 35.5 %copy-start.8 = (bf16[256,512]{1,0:T(8,128)(2,1)S(1)}, bf16[256,512]{1,0:T(8,128)(2,1)}, u32[]{:S(2)}) copy-start(bf16[256,512]{1,0:T(8,128)(2,1)} %out_own_hbm.1) | copy-start | bytes 786436
  6.6 37.5 %copy-start = (bf16[3,512,256]{2,1,0:T(8,128)(2,1)S(1)}, bf16[3,512,256]{2,1,0:T(8,128)(2,1)}, u32[]{:S(2)}) copy-start(bf16[3,512,256]{2,1,0:T(8,128)(2,1)} %weight_hbm.1) | copy-start | bytes 2359300
  6.6 37.5 %copy-start.1 = (s32[1,4]{1,0:T(1,128)S(1)}, s32[1,4]{1,0:T(1,128)}, u32[]{:S(2)}) copy-start(s32[1,4]{1,0:T(1,128)} %counts_ref.1) | copy-start | bytes 52
  41.5 2.7 %collective-permute-start = (bf16[2048,256]{1,0:T(8,128)(2,1)S(1)}, bf16[2048,256]{1,0:T(8,128)(2,1)S(1)}, u32[]{:S(2)}, u32[]{:S(2)}) collective-permute-start(bf16[2048,256]{1,0:T(8,128)(2,1)S(1)} %bitcast.7), channel_id=1, source_target_pairs={{0,1},{1,0},{2,3},{3,2},{4,5},{5,4},{6,7},{7,6},{8,9},{9,8},{10,11... | collective-permute-start | bytes 3145736 | tf_op jit(solution)/shard_map/ppermute | solution.py:410
  41.5 35.4 %collective-permute-start.1 = (bf16[512,1024]{1,0:T(8,128)(2,1)S(1)}, bf16[512,1024]{1,0:T(8,128)(2,1)S(1)}, u32[]{:S(2)}, u32[]{:S(2)}) collective-permute-start(bf16[512,1024]{1,0:T(8,128)(2,1)S(1)} %copy-done.3), channel_id=1, source_target_pairs={{0,1},{1,0},{2,3},{3,2},{4,5},{5,4},{6,7},{7,6},{8,9},{9,8},{10,11... | collective-permute-start | bytes 3145736 | tf_op jit(solution)/shard_map/ppermute | solution.py:410
  42.0 34.9 %collective-permute-start.2 = (bf16[1024,512]{1,0:T(8,128)(2,1)S(1)}, bf16[1024,512]{1,0:T(8,128)(2,1)S(1)}, u32[]{:S(2)}, u32[]{:S(2)}) collective-permute-start(bf16[1024,512]{1,0:T(8,128)(2,1)S(1)} %copy-done.4), channel_id=1, source_target_pairs={{0,1},{1,0},{2,3},{3,2},{4,5},{5,4},{6,7},{7,6},{8,9},{9,8},{10,11... | collective-permute-start | bytes 3145736 | tf_op jit(solution)/shard_map/ppermute | solution.py:410
  42.1 34.8 %collective-permute-start.3 = (bf16[256,512]{1,0:T(8,128)(2,1)S(1)}, bf16[256,512]{1,0:T(8,128)(2,1)S(1)}, u32[]{:S(2)}, u32[]{:S(2)}) collective-permute-start(bf16[256,512]{1,0:T(8,128)(2,1)S(1)} %copy-done.8), channel_id=1, source_target_pairs={{0,1},{1,0},{2,3},{3,2},{4,5},{5,4},{6,7},{7,6},{8,9},{9,8},{10,11... | collective-permute-start | bytes 786440 | tf_op jit(solution)/shard_map/ppermute | solution.py:410
  76.9 33.0 %copy-start.9 = (bf16[256,512]{1,0:T(8,128)(2,1)}, bf16[256,512]{1,0:T(8,128)(2,1)S(1)}, u32[]{:S(2)}) copy-start(bf16[256,512]{1,0:T(8,128)(2,1)S(1)} %collective-permute-done.3.out_other_hbm) | copy-start | bytes 786436
  76.9 33.0 %copy-start.5 = (bf16[512,1024]{1,0:T(8,128)(2,1)}, bf16[512,1024]{1,0:T(8,128)(2,1)S(1)}, u32[]{:S(2)}) copy-start(bf16[512,1024]{1,0:T(8,128)(2,1)S(1)} %collective-permute-done.1.fc1_other_hbm) | copy-start | bytes 3145732
  76.9 33.0 %copy-start.6 = (bf16[1024,512]{1,0:T(8,128)(2,1)}, bf16[1024,512]{1,0:T(8,128)(2,1)S(1)}, u32[]{:S(2)}) copy-start(bf16[1024,512]{1,0:T(8,128)(2,1)S(1)} %collective-permute-done.2.fc2_other_hbm) | copy-start | bytes 3145732
  107.2 2.7 %copy-start.2 = (bf16[16,128,256]{2,1,0:T(8,128)(2,1)}, bf16[16,128,256]{2,1,0:T(8,128)(2,1)S(1)}, u32[]{:S(2)}) copy-start(bf16[16,128,256]{2,1,0:T(8,128)(2,1)S(1)} %all_to_all.11) | copy-start | bytes 3145732
  107.2 2.7 %collective-permute-start.4 = (bf16[2048,256]{1,0:T(8,128)(2,1)S(1)}, bf16[2048,256]{1,0:T(8,128)(2,1)S(1)}, u32[]{:S(2)}, u32[]{:S(2)}) collective-permute-start(bf16[2048,256]{1,0:T(8,128)(2,1)S(1)} %bitcast.10), channel_id=1, source_target_pairs={{0,1},{1,0},{2,3},{3,2},{4,5},{5,4},{6,7},{7,6},{8,9},{9,8},{10,11... | collective-permute-start | bytes 3145736 | tf_op jit(solution)/shard_map/ppermute | solution.py:410
  109.9 1.0 copy-start.7
  122.9 2.9 %collective-permute-start.5 = (bf16[1024,512]{1,0:T(8,128)(2,1)}, bf16[1024,512]{1,0:T(8,128)(2,1)S(1)}, u32[]{:S(2)}, u32[]{:S(2)}) collective-permute-start(bf16[1024,512]{1,0:T(8,128)(2,1)} %get-tuple-element.16), channel_id=1, source_target_pairs={{0,1},{1,0},{2,3},{3,2},{4,5},{5,4},{6,7},{7,6},{8,9},{9,8},{10,11... | collective-permute-start | bytes 3145736 | tf_op jit(solution)/shard_map/ppermute | solution.py:410

commit v7 on v6

--- a/solution.py
+++ b/solution.py
@@ -122,7 +122,7 @@
 
 
 def attend_kernel(
-    counts_ref, own_ref, other_ref, weight_hbm, out_hbm, w_ref, q_ref, k_ref, v_ref, out_ref, w_sems, out_sems
+    counts_ref, own_ref, other_ref, weight_hbm, out_hbm, w_ref, q_ref, k_ref, v_ref, out_ref, sum_ref, w_sems, out_sems
 ):
     length, half = own_ref.shape
     tiles = counts_ref.shape[1]
@@ -183,28 +183,22 @@
     bound = functools.reduce(jnp.maximum, [q_most * k_most for q_most, k_most in most])
     safe = jnp.max(bound) < SAFE * SAFE
 
-    def attend_pair(pair, rows, keys, shifted):
-        scores = [
-            lax.dot_general(
-                k_ref[2 * pair + h, keys, :],
-                q_ref[2 * pair + h, rows, :],
-                (((1,), (1,)), ((), ())),
-                preferred_element_type=f32,
-            )
-            for h in range(2)
-        ]
-        if shifted:
-            scores = [values - jnp.max(values, axis=0, keepdims=True) for values in scores]
-        sums = [dot(v_ref[2 * pair + h, :, keys], jnp.exp2(scores[h]).astype(bf16)) for h in range(2)]
-        value = jnp.concatenate([both[:HDIM] / both[HDIM : HDIM + 1] for both in sums], axis=0)
-        out_ref[pair, rows, :] = jnp.transpose(value).astype(bf16)
-
-    def attend_rows(rows, keys, shifted):
-        def one_pair(pair, carry):
-            attend_pair(pair, rows, keys, shifted)
-            return carry
-
-        lax.fori_loop(0, pairs, one_pair, 0)
+    def score(h, rows, keys):
+        return lax.dot_general(
+            k_ref[h, keys, :], q_ref[h, rows, :], (((1,), (1,)), ((), ())), preferred_element_type=f32
+        )
+
+    def add_keys(rows, keys):
+        ahead = score(0, rows, keys)
+        for h in range(2 * pairs):
+            scores = ahead
+            ahead = score(h + 1, rows, keys) if h + 1 < 2 * pairs else None
+            sum_ref[h] += dot(v_ref[h, :, keys], jnp.exp2(scores).astype(bf16))
+
+    def add_shifted(h, rows):
+        scores = score(h, rows, slice(None))
+        scores = scores - jnp.max(scores, axis=0, keepdims=True)
+        sum_ref[h] = dot(v_ref[h], jnp.exp2(scores).astype(bf16))
 
     def send_out(i, pair):
         rows = pl.ds(pl.multiple_of(i * TALL, TALL), TALL)
@@ -222,17 +216,30 @@
             high = jnp.where(end >= begin + TALL, end, high)
         low = (low // LANES) * LANES
         blocks = (high - low + KEYS - 1) // KEYS
-        for n in range(TALL // KEYS, length // KEYS + 1):
-
-            @pl.when(jnp.logical_and(safe, blocks == n))
-            def _(n=n):
-                start = pl.multiple_of(jnp.minimum(low, length - n * KEYS), LANES)
-                attend_rows(rows, pl.ds(start, n * KEYS), False)
+        start = jnp.minimum(low, length - blocks * KEYS)
+
+        @pl.when(safe)
+        def _():
+            sum_ref[...] = jnp.zeros_like(sum_ref)
+
+            def step(j, carry):
+                add_keys(rows, pl.ds(pl.multiple_of(start + j * KEYS, LANES), KEYS))
+                return carry
+
+            lax.fori_loop(0, blocks, step, 0)
 
         @pl.when(jnp.logical_not(safe))
         def _():
-            attend_rows(rows, slice(None), True)
-
+            def step(h, carry):
+                add_shifted(h, rows)
+                return carry
+
+            lax.fori_loop(0, 2 * pairs, step, 0)
+
+        for pair in range(pairs):
+            both = sum_ref[2 * pair], sum_ref[2 * pair + 1]
+            value = jnp.concatenate([head[:HDIM] / head[HDIM : HDIM + 1] for head in both], axis=0)
+            out_ref[pair, rows, :] = jnp.transpose(value).astype(bf16)
         for pair in range(pairs):
             send_out(i, pair).start()
         return carry
@@ -259,6 +266,7 @@
             pltpu.VMEM((heads, length, LANES), bf16),
             pltpu.VMEM((heads, PADDED, length), bf16),
             pltpu.VMEM((heads // 2, length, LANES), bf16),
+            pltpu.VMEM((heads, PADDED, TALL), f32),
             pltpu.SemaphoreType.DMA((6,)),
             pltpu.SemaphoreType.DMA((length // TALL, heads // 2)),
         ],

time: 127 us -> 131 us (1.031)
  Pallas kernels: 51.3 us -> 55.2 us
    pallas_call x1, Pallas kernels: 32.7 us -> 36.6 us  [attend(): pl.pallas_call(attend_kernel, out_shape=jax.ShapeDtypeStruct((length, col...]
  transfers between devices with their start and end apart: 6 -> 6, of which waited for: 3 -> 3; matrix products, arithmetic and copies ran while one was open for 0% -> 0% of each run, Pallas kernels for 26% -> 28%
where the time goes in v7:
time: 131 us
  blocking collectives  65.2 us (50%)
  Pallas kernels  55.2 us (42%)
  waiting for transfers between devices  7.03 us (5%)
  local copies, waits for them, and re-layouts  2.05 us (2%)
    all_to_all x2, blocking collectives, exchange(): lax.all_to_all(cells, 'space', split_axis=0, concat_axis=0, tiled=True)  65.2 us
    pallas_call x1, Pallas kernels, attend(): pl.pallas_call(attend_kernel, out_shape=jax.ShapeDtypeStruct((length, col...  36.6 us
    pallas_call x1, Pallas kernels, finish(): pl.pallas_call(functools.partial(finish_kernel, shards), out_shape=(jax.S...  12 us
    ppermute x6, waiting for transfers between devices, across(): return lax.ppermute(values, 'mp', [(0, 1), (1, 0)])  7.03 us
    pallas_call x1, Pallas kernels, order_for_owners(): pl.pallas_call(functools.partial(send_kernel, shards), out_shape=jax.Shap...  6.59 us
  transfers between devices with their start and end apart: 6, of which 3 were waited for; matrix products, arithmetic and copies ran while one was open for 0% of the time, Pallas kernels for 28%

profile of v7, /device:TPU:0, one launch (start us, length us, event | category | flops | bytes accessed | tf_op | source)
XLA Modules:
  0.0 130.7 jit_solution(4120246535464516734)
XLA Ops:
  0.0 6.6 %shard_map.91 = bf16[2048,256]{1,0:T(8,128)(2,1)} custom-call(s32[1,2048]{1,0:T(1,128)} %bitcast.13, f32[1,512]{1,0:T(1,128)} %bitcast.15, bf16[2048,512]{1,0:T(8,128)(2,1)} %points_hbm.3), custom_call_target="tpu_custom_call" | custom-call | flops 2147483648 | bytes 4194304 | tf_op jit(solution)/shard_map/pallas_call | solution.py:104
  6.6 0.0 copy-start.3
  6.6 0.0 copy-start.8
  6.6 0.0 copy-start
  6.6 0.0 copy-start.1
  6.7 34.8 %all_to_all.10 = bf16[16,128,256]{2,1,0:T(8,128)(2,1)S(1)} all-to-all(bf16[16,128,256]{2,1,0:T(8,128)(2,1)} %bitcast.12), channel_id=1, replica_groups=mesh['space'=16,'mp'=2] {'space'}, dimensions={0} | all-to-all | bytes 2097152 | tf_op jit(solution)/shard_map/all_to_all | solution.py:424
  41.5 0.0 collective-permute-start
  41.5 0.5 collective-permute-start.1
  42.0 0.1 collective-permute-start.2
  42.1 0.4 collective-permute-start.3
  42.5 1.6 %collective-permute-done.other_ref = bf16[2048,256]{1,0:T(8,128)(2,1)S(1)} collective-permute-done((bf16[2048,256]{1,0:T(8,128)(2,1)S(1)}, bf16[2048,256]{1,0:T(8,128)(2,1)S(1)}, u32[]{:S(2)}, u32[]{:S(2)}) %collective-permute-start) | collective-permute-done | bytes 1048608 | tf_op jit(solution)/shard_map/ppermute | solution.py:418
  44.1 36.6 %shard_map.92 = bf16[2048,256]{1,0:T(8,128)(2,1)S(1)} custom-call(s32[1,4]{1,0:T(1,128)S(1)} %copy-done.1, bf16[2048,256]{1,0:T(8,128)(2,1)S(1)} %bitcast.8, bf16[2048,256]{1,0:T(8,128)(2,1)S(1)} %collective-permute-done.other_ref, bf16[3,512,256]{2,1,0:T(8,128)(2,1)S(1)} %copy-done), custom_call_target="tpu_custom_call" | custom-call | flops 17179869184 | bytes 4194304 | tf_op jit(solution)/shard_map/pallas_call | solution.py:258
  80.7 0.0 collective-permute-done.3.out_other_hbm
  80.7 0.0 collective-permute-done.1.fc1_other_hbm
  80.7 0.0 copy-start.5
  80.8 0.0 collective-permute-done.2.fc2_other_hbm
  80.8 30.3 %all_to_all.11 = bf16[16,128,256]{2,1,0:T(8,128)(2,1)S(1)} all-to-all(bf16[16,128,256]{2,1,0:T(8,128)(2,1)S(1)} %bitcast.9), channel_id=1, replica_groups=mesh['space'=16,'mp'=2] {'space'}, dimensions={0} | all-to-all | bytes 2097152 | tf_op jit(solution)/shard_map/all_to_all | solution.py:424
  111.1 0.0 collective-permute-start.4
  111.1 2.7 %collective-permute-done.4.other_hbm = bf16[2048,256]{1,0:T(8,128)(2,1)S(1)} collective-permute-done((bf16[2048,256]{1,0:T(8,128)(2,1)S(1)}, bf16[2048,256]{1,0:T(8,128)(2,1)S(1)}, u32[]{:S(2)}, u32[]{:S(2)}) %collective-permute-start.4) | collective-permute-done | bytes 1048608 | tf_op jit(solution)/shard_map/ppermute | solution.py:418
  113.8 1.0 copy-done.7
  114.8 12.0 %shard_map.93 = (bf16[1024,512]{1,0:T(8,128)(2,1)}, bf16[2048,512]{1,0:T(8,128)(2,1)}) custom-call(s32[1,2048]{1,0:T(1,128)} %bitcast.14, f32[1,512]{1,0:T(1,128)} %bitcast.16, bf16[2048,512]{1,0:T(8,128)(2,1)} %points_hbm.3, bf16[2048,256]{1,0:T(8,128)(2,1)} %bitcast.11, bf16[2048,256]{1,0:T(8,128)(2,1)} %copy-done.7, bf16[256,512]{1,0:T(8,128)(2,1)} %out_own_hbm.1, ...), custom_call_target="tpu_custom_call" | custom-call | flops 6979321856 | bytes 16777216 | tf_op jit(solution)/shard_map/pallas_call | solution.py:387
  126.8 0.2 collective-permute-start.5
  127.0 2.7 %collective-permute-done.5 = bf16[1024,512]{1,0:T(8,128)(2,1)S(1)} collective-permute-done((bf16[1024,512]{1,0:T(8,128)(2,1)}, bf16[1024,512]{1,0:T(8,128)(2,1)S(1)}, u32[]{:S(2)}, u32[]{:S(2)}) %collective-permute-start.5) | collective-permute-done | bytes 1048608 | tf_op jit(solution)/shard_map/ppermute | solution.py:418
  129.7 1.0 constant_dynamic-update-slice_fusion
  (14 shorter events, 0.0 us)
Async XLA Ops:
  0.0 42.0 %copy-start.4 = (bf16[1024,512]{1,0:T(8,128)(2,1)S(1)}, bf16[1024,512]{1,0:T(8,128)(2,1)}, u32[]{:S(2)}) copy-start(bf16[1024,512]{1,0:T(8,128)(2,1)} %fc2_own_hbm.1) | copy-start | bytes 3145732
  6.6 34.9 %copy-start.3 = (bf16[512,1024]{1,0:T(8,128)(2,1)S(1)}, bf16[512,1024]{1,0:T(8,128)(2,1)}, u32[]{:S(2)}) copy-start(bf16[512,1024]{1,0:T(8,128)(2,1)} %fc1_own_hbm.1) | copy-start | bytes 3145732
  6.6 35.5 %copy-start.8 = (bf16[256,512]{1,0:T(8,128)(2,1)S(1)}, bf16[256,512]{1,0:T(8,128)(2,1)}, u32[]{:S(2)}) copy-start(bf16[256,512]{1,0:T(8,128)(2,1)} %out_own_hbm.1) | copy-start | bytes 786436
  6.6 37.5 %copy-start = (bf16[3,512,256]{2,1,0:T(8,128)(2,1)S(1)}, bf16[3,512,256]{2,1,0:T(8,128)(2,1)}, u32[]{:S(2)}) copy-start(bf16[3,512,256]{2,1,0:T(8,128)(2,1)} %weight_hbm.1) | copy-start | bytes 2359300
  6.6 37.5 %copy-start.1 = (s32[1,4]{1,0:T(1,128)S(1)}, s32[1,4]{1,0:T(1,128)}, u32[]{:S(2)}) copy-start(s32[1,4]{1,0:T(1,128)} %counts_ref.1) | copy-start | bytes 52
  41.5 2.7 %collective-permute-start = (bf16[2048,256]{1,0:T(8,128)(2,1)S(1)}, bf16[2048,256]{1,0:T(8,128)(2,1)S(1)}, u32[]{:S(2)}, u32[]{:S(2)}) collective-permute-start(bf16[2048,256]{1,0:T(8,128)(2,1)S(1)} %bitcast.7), channel_id=1, source_target_pairs={{0,1},{1,0},{2,3},{3,2},{4,5},{5,4},{6,7},{7,6},{8,9},{9,8},{10,11... | collective-permute-start | bytes 3145736 | tf_op jit(solution)/shard_map/ppermute | solution.py:418
  41.5 39.3 %collective-permute-start.1 = (bf16[512,1024]{1,0:T(8,128)(2,1)S(1)}, bf16[512,1024]{1,0:T(8,128)(2,1)S(1)}, u32[]{:S(2)}, u32[]{:S(2)}) collective-permute-start(bf16[512,1024]{1,0:T(8,128)(2,1)S(1)} %copy-done.3), channel_id=1, source_target_pairs={{0,1},{1,0},{2,3},{3,2},{4,5},{5,4},{6,7},{7,6},{8,9},{9,8},{10,11... | collective-permute-start | bytes 3145736 | tf_op jit(solution)/shard_map/ppermute | solution.py:418
  42.0 38.8 %collective-permute-start.2 = (bf16[1024,512]{1,0:T(8,128)(2,1)S(1)}, bf16[1024,512]{1,0:T(8,128)(2,1)S(1)}, u32[]{:S(2)}, u32[]{:S(2)}) collective-permute-start(bf16[1024,512]{1,0:T(8,128)(2,1)S(1)} %copy-done.4), channel_id=1, source_target_pairs={{0,1},{1,0},{2,3},{3,2},{4,5},{5,4},{6,7},{7,6},{8,9},{9,8},{10,11... | collective-permute-start | bytes 3145736 | tf_op jit(solution)/shard_map/ppermute | solution.py:418
  42.1 38.6 %collective-permute-start.3 = (bf16[256,512]{1,0:T(8,128)(2,1)S(1)}, bf16[256,512]{1,0:T(8,128)(2,1)S(1)}, u32[]{:S(2)}, u32[]{:S(2)}) collective-permute-start(bf16[256,512]{1,0:T(8,128)(2,1)S(1)} %copy-done.8), channel_id=1, source_target_pairs={{0,1},{1,0},{2,3},{3,2},{4,5},{5,4},{6,7},{7,6},{8,9},{9,8},{10,11... | collective-permute-start | bytes 786440 | tf_op jit(solution)/shard_map/ppermute | solution.py:418
  80.7 33.0 %copy-start.9 = (bf16[256,512]{1,0:T(8,128)(2,1)}, bf16[256,512]{1,0:T(8,128)(2,1)S(1)}, u32[]{:S(2)}) copy-start(bf16[256,512]{1,0:T(8,128)(2,1)S(1)} %collective-permute-done.3.out_other_hbm) | copy-start | bytes 786436
  80.7 33.0 %copy-start.5 = (bf16[512,1024]{1,0:T(8,128)(2,1)}, bf16[512,1024]{1,0:T(8,128)(2,1)S(1)}, u32[]{:S(2)}) copy-start(bf16[512,1024]{1,0:T(8,128)(2,1)S(1)} %collective-permute-done.1.fc1_other_hbm) | copy-start | bytes 3145732
  80.8 33.0 %copy-start.6 = (bf16[1024,512]{1,0:T(8,128)(2,1)}, bf16[1024,512]{1,0:T(8,128)(2,1)S(1)}, u32[]{:S(2)}) copy-start(bf16[1024,512]{1,0:T(8,128)(2,1)S(1)} %collective-permute-done.2.fc2_other_hbm) | copy-start | bytes 3145732
  111.1 2.7 %copy-start.2 = (bf16[16,128,256]{2,1,0:T(8,128)(2,1)}, bf16[16,128,256]{2,1,0:T(8,128)(2,1)S(1)}, u32[]{:S(2)}) copy-start(bf16[16,128,256]{2,1,0:T(8,128)(2,1)S(1)} %all_to_all.11) | copy-start | bytes 3145732
  111.1 2.7 %collective-permute-start.4 = (bf16[2048,256]{1,0:T(8,128)(2,1)S(1)}, bf16[2048,256]{1,0:T(8,128)(2,1)S(1)}, u32[]{:S(2)}, u32[]{:S(2)}) collective-permute-start(bf16[2048,256]{1,0:T(8,128)(2,1)S(1)} %bitcast.10), channel_id=1, source_target_pairs={{0,1},{1,0},{2,3},{3,2},{4,5},{5,4},{6,7},{7,6},{8,9},{9,8},{10,11... | collective-permute-start | bytes 3145736 | tf_op jit(solution)/shard_map/ppermute | solution.py:418
  113.8 1.0 copy-start.7
  126.8 2.9 %collective-permute-start.5 = (bf16[1024,512]{1,0:T(8,128)(2,1)}, bf16[1024,512]{1,0:T(8,128)(2,1)S(1)}, u32[]{:S(2)}, u32[]{:S(2)}) collective-permute-start(bf16[1024,512]{1,0:T(8,128)(2,1)} %get-tuple-element.16), channel_id=1, source_target_pairs={{0,1},{1,0},{2,3},{3,2},{4,5},{5,4},{6,7},{7,6},{8,9},{9,8},{10,11... | collective-permute-start | bytes 3145736 | tf_op jit(solution)/shard_map/ppermute | solution.py:418

commit v8 on v4

--- a/solution.py
+++ b/solution.py
@@ -199,22 +199,21 @@
                 start = pl.multiple_of(jnp.minimum(low, length - n * KEYS), LANES)
                 keys = pl.ds(start, n * KEYS)
 
-                def one_pair(pair, carry):
-                    scores = [
-                        lax.dot_general(
-                            k_ref[2 * pair + h, keys, :],
-                            q_ref[2 * pair + h, rows, :],
-                            (((1,), (1,)), ((), ())),
-                            preferred_element_type=f32,
-                        )
-                        for h in range(2)
-                    ]
-                    sums = [dot(v_ref[2 * pair + h, :, keys], weigh(scores[h])) for h in range(2)]
-                    value = jnp.concatenate([both[:HDIM] / both[HDIM : HDIM + 1] for both in sums], axis=0)
+                def score(h):
+                    return lax.dot_general(
+                        k_ref[h, keys, :], q_ref[h, rows, :], (((1,), (1,)), ((), ())), preferred_element_type=f32
+                    )
+
+                ahead, sums = score(0), []
+                for h in range(2 * pairs):
+                    scores = ahead
+                    ahead = score(h + 1) if h + 1 < 2 * pairs else None
+                    sums.append(dot(v_ref[h, :, keys], weigh(scores)))
+                for pair in range(pairs):
+                    value = jnp.concatenate(
+                        [both[:HDIM] / both[HDIM : HDIM + 1] for both in sums[2 * pair : 2 * pair + 2]], axis=0
+                    )
                     out_ref[pair, rows, :] = jnp.transpose(value).astype(bf16)
-                    return carry
-
-                lax.fori_loop(0, pairs, one_pair, 0)
 
         for pair in range(pairs):
             send_out(i, pair).start()

time: 115 us -> 114 us (level)
  Pallas kernels: 39.6 us -> 33.9 us
  blocking collectives: 64.4 us -> 68.9 us
    pallas_call x1, Pallas kernels: 21 us -> 15.2 us  [attend(): pl.pallas_call(attend_kernel, out_shape=jax.ShapeDtypeStruct((length, col...]
    all_to_all x2, blocking collectives: 64.4 us -> 68.9 us  [exchange(): lax.all_to_all(cells, 'space', split_axis=0, concat_axis=0, tiled=True)]
  transfers between devices with their start and end apart: 6 -> 6, of which waited for: 3 -> 3; matrix products, arithmetic and copies ran while one was open for 0% -> 0% of each run, Pallas kernels for 18% -> 13%
where the time goes in v8:
time: 114 us; the launch traced here: 113 us
  blocking collectives  68.9 us (60%)
  Pallas kernels  33.9 us (30%)
  waiting for transfers between devices  7.03 us (6%)
  local copies, waits for them, and re-layouts  2.05 us (2%)
  starting transfers between devices  1.23 us (1%)
    all_to_all x2, blocking collectives, exchange(): lax.all_to_all(cells, 'space', split_axis=0, concat_axis=0, tiled=True)  68.9 us
    pallas_call x1, Pallas kernels, attend(): pl.pallas_call(attend_kernel, out_shape=jax.ShapeDtypeStruct((length, col...  15.2 us
    pallas_call x1, Pallas kernels, finish(): pl.pallas_call(functools.partial(finish_kernel, shards), out_shape=(jax.S...  12 us
    ppermute x6, waiting for transfers between devices, across(): return lax.ppermute(values, 'mp', [(0, 1), (1, 0)])  7.03 us
    pallas_call x1, Pallas kernels, order_for_owners(): pl.pallas_call(functools.partial(send_kernel, shards), out_shape=jax.Shap...  6.59 us
  transfers between devices with their start and end apart: 6, of which 3 were waited for; matrix products, arithmetic and copies ran while one was open for 0% of the time, Pallas kernels for 13%

profile of v8, /device:TPU:0, one launch (start us, length us, event | category | flops | bytes accessed | tf_op | source)
XLA Modules:
  0.0 113.2 jit_solution(5341961194251898041)
XLA Ops:
  0.0 6.6 %shard_map.91 = bf16[2048,256]{1,0:T(8,128)(2,1)} custom-call(s32[1,2048]{1,0:T(1,128)} %bitcast.13, f32[1,512]{1,0:T(1,128)} %bitcast.15, bf16[2048,512]{1,0:T(8,128)(2,1)} %points_hbm.3), custom_call_target="tpu_custom_call" | custom-call | flops 2147483648 | bytes 4194304 | tf_op jit(solution)/shard_map/pallas_call | solution.py:103
  6.6 0.0 copy-start.3
  6.6 0.0 copy-start.8
  6.6 0.0 copy-start
  6.6 0.0 copy-start.1
  6.7 34.8 %all_to_all.10 = bf16[16,128,256]{2,1,0:T(8,128)(2,1)S(1)} all-to-all(bf16[16,128,256]{2,1,0:T(8,128)(2,1)} %bitcast.12), channel_id=1, replica_groups=mesh['space'=16,'mp'=2] {'space'}, dimensions={0} | all-to-all | bytes 2097152 | tf_op jit(solution)/shard_map/all_to_all | solution.py:398
  41.5 0.0 collective-permute-start
  41.5 0.5 collective-permute-start.1
  42.0 0.0 copy-done.4
  42.0 0.1 collective-permute-start.2
  42.1 0.4 collective-permute-start.3
  42.5 1.6 %collective-permute-done.other_ref = bf16[2048,256]{1,0:T(8,128)(2,1)S(1)} collective-permute-done((bf16[2048,256]{1,0:T(8,128)(2,1)S(1)}, bf16[2048,256]{1,0:T(8,128)(2,1)S(1)}, u32[]{:S(2)}, u32[]{:S(2)}) %collective-permute-start) | collective-permute-done | bytes 1048608 | tf_op jit(solution)/shard_map/ppermute | solution.py:392
  44.1 15.2 %shard_map.92 = bf16[2048,256]{1,0:T(8,128)(2,1)S(1)} custom-call(s32[1,4]{1,0:T(1,128)S(1)} %copy-done.1, bf16[2048,256]{1,0:T(8,128)(2,1)S(1)} %bitcast.8, bf16[2048,256]{1,0:T(8,128)(2,1)S(1)} %collective-permute-done.other_ref, bf16[3,512,256]{2,1,0:T(8,128)(2,1)S(1)} %copy-done), custom_call_target="tpu_custom_call" | custom-call | flops 17179869184 | bytes 4194304 | tf_op jit(solution)/shard_map/pallas_call | solution.py:233
  59.4 0.0 collective-permute-done.3.out_other_hbm
  59.4 0.0 collective-permute-done.1.fc1_other_hbm
  59.4 0.0 collective-permute-done.2.fc2_other_hbm
  59.5 34.1 %all_to_all.11 = bf16[16,128,256]{2,1,0:T(8,128)(2,1)S(1)} all-to-all(bf16[16,128,256]{2,1,0:T(8,128)(2,1)S(1)} %bitcast.9), channel_id=1, replica_groups=mesh['space'=16,'mp'=2] {'space'}, dimensions={0} | all-to-all | bytes 2097152 | tf_op jit(solution)/shard_map/all_to_all | solution.py:398
  93.5 0.0 collective-permute-start.4
  93.5 2.7 %collective-permute-done.4.other_hbm = bf16[2048,256]{1,0:T(8,128)(2,1)S(1)} collective-permute-done((bf16[2048,256]{1,0:T(8,128)(2,1)S(1)}, bf16[2048,256]{1,0:T(8,128)(2,1)S(1)}, u32[]{:S(2)}, u32[]{:S(2)}) %collective-permute-start.4) | collective-permute-done | bytes 1048608 | tf_op jit(solution)/shard_map/ppermute | solution.py:392
  96.2 1.0 copy-done.7
  97.2 12.0 %shard_map.93 = (bf16[1024,512]{1,0:T(8,128)(2,1)}, bf16[2048,512]{1,0:T(8,128)(2,1)}) custom-call(s32[1,2048]{1,0:T(1,128)} %bitcast.14, f32[1,512]{1,0:T(1,128)} %bitcast.16, bf16[2048,512]{1,0:T(8,128)(2,1)} %points_hbm.3, bf16[2048,256]{1,0:T(8,128)(2,1)} %bitcast.11, bf16[2048,256]{1,0:T(8,128)(2,1)} %copy-done.7, bf16[256,512]{1,0:T(8,128)(2,1)} %out_own_hbm.1, ...), custom_call_target="tpu_custom_call" | custom-call | flops 6979321856 | bytes 16777216 | tf_op jit(solution)/shard_map/pallas_call | solution.py:361
  109.2 0.2 collective-permute-start.5
  109.4 2.7 %collective-permute-done.5 = bf16[1024,512]{1,0:T(8,128)(2,1)S(1)} collective-permute-done((bf16[1024,512]{1,0:T(8,128)(2,1)}, bf16[1024,512]{1,0:T(8,128)(2,1)S(1)}, u32[]{:S(2)}, u32[]{:S(2)}) %collective-permute-start.5) | collective-permute-done | bytes 1048608 | tf_op jit(solution)/shard_map/ppermute | solution.py:392
  112.1 1.0 constant_dynamic-update-slice_fusion
  (14 shorter events, 0.0 us)
Async XLA Ops:
  0.0 42.0 %copy-start.4 = (bf16[1024,512]{1,0:T(8,128)(2,1)S(1)}, bf16[1024,512]{1,0:T(8,128)(2,1)}, u32[]{:S(2)}) copy-start(bf16[1024,512]{1,0:T(8,128)(2,1)} %fc2_own_hbm.1) | copy-start | bytes 3145732
  6.6 34.9 %copy-start.3 = (bf16[512,1024]{1,0:T(8,128)(2,1)S(1)}, bf16[512,1024]{1,0:T(8,128)(2,1)}, u32[]{:S(2)}) copy-start(bf16[512,1024]{1,0:T(8,128)(2,1)} %fc1_own_hbm.1) | copy-start | bytes 3145732
  6.6 35.5 %copy-start.8 = (bf16[256,512]{1,0:T(8,128)(2,1)S(1)}, bf16[256,512]{1,0:T(8,128)(2,1)}, u32[]{:S(2)}) copy-start(bf16[256,512]{1,0:T(8,128)(2,1)} %out_own_hbm.1) | copy-start | bytes 786436
  6.6 37.5 %copy-start = (bf16[3,512,256]{2,1,0:T(8,128)(2,1)S(1)}, bf16[3,512,256]{2,1,0:T(8,128)(2,1)}, u32[]{:S(2)}) copy-start(bf16[3,512,256]{2,1,0:T(8,128)(2,1)} %weight_hbm.1) | copy-start | bytes 2359300
  6.6 37.5 %copy-start.1 = (s32[1,4]{1,0:T(1,128)S(1)}, s32[1,4]{1,0:T(1,128)}, u32[]{:S(2)}) copy-start(s32[1,4]{1,0:T(1,128)} %counts_ref.1) | copy-start | bytes 52
  41.5 2.7 %collective-permute-start = (bf16[2048,256]{1,0:T(8,128)(2,1)S(1)}, bf16[2048,256]{1,0:T(8,128)(2,1)S(1)}, u32[]{:S(2)}, u32[]{:S(2)}) collective-permute-start(bf16[2048,256]{1,0:T(8,128)(2,1)S(1)} %bitcast.7), channel_id=1, source_target_pairs={{0,1},{1,0},{2,3},{3,2},{4,5},{5,4},{6,7},{7,6},{8,9},{9,8},{10,11... | collective-permute-start | bytes 3145736 | tf_op jit(solution)/shard_map/ppermute | solution.py:392
  41.5 17.9 %collective-permute-start.1 = (bf16[512,1024]{1,0:T(8,128)(2,1)S(1)}, bf16[512,1024]{1,0:T(8,128)(2,1)S(1)}, u32[]{:S(2)}, u32[]{:S(2)}) collective-permute-start(bf16[512,1024]{1,0:T(8,128)(2,1)S(1)} %copy-done.3), channel_id=1, source_target_pairs={{0,1},{1,0},{2,3},{3,2},{4,5},{5,4},{6,7},{7,6},{8,9},{9,8},{10,11... | collective-permute-start | bytes 3145736 | tf_op jit(solution)/shard_map/ppermute | solution.py:392
  42.0 17.4 %collective-permute-start.2 = (bf16[1024,512]{1,0:T(8,128)(2,1)S(1)}, bf16[1024,512]{1,0:T(8,128)(2,1)S(1)}, u32[]{:S(2)}, u32[]{:S(2)}) collective-permute-start(bf16[1024,512]{1,0:T(8,128)(2,1)S(1)} %copy-done.4), channel_id=1, source_target_pairs={{0,1},{1,0},{2,3},{3,2},{4,5},{5,4},{6,7},{7,6},{8,9},{9,8},{10,11... | collective-permute-start | bytes 3145736 | tf_op jit(solution)/shard_map/ppermute | solution.py:392
  42.1 17.3 %collective-permute-start.3 = (bf16[256,512]{1,0:T(8,128)(2,1)S(1)}, bf16[256,512]{1,0:T(8,128)(2,1)S(1)}, u32[]{:S(2)}, u32[]{:S(2)}) collective-permute-start(bf16[256,512]{1,0:T(8,128)(2,1)S(1)} %copy-done.8), channel_id=1, source_target_pairs={{0,1},{1,0},{2,3},{3,2},{4,5},{5,4},{6,7},{7,6},{8,9},{9,8},{10,11... | collective-permute-start | bytes 786440 | tf_op jit(solution)/shard_map/ppermute | solution.py:392
  59.4 36.8 %copy-start.9 = (bf16[256,512]{1,0:T(8,128)(2,1)}, bf16[256,512]{1,0:T(8,128)(2,1)S(1)}, u32[]{:S(2)}) copy-start(bf16[256,512]{1,0:T(8,128)(2,1)S(1)} %collective-permute-done.3.out_other_hbm) | copy-start | bytes 786436
  59.4 36.8 %copy-start.5 = (bf16[512,1024]{1,0:T(8,128)(2,1)}, bf16[512,1024]{1,0:T(8,128)(2,1)S(1)}, u32[]{:S(2)}) copy-start(bf16[512,1024]{1,0:T(8,128)(2,1)S(1)} %collective-permute-done.1.fc1_other_hbm) | copy-start | bytes 3145732
  59.5 36.7 %copy-start.6 = (bf16[1024,512]{1,0:T(8,128)(2,1)}, bf16[1024,512]{1,0:T(8,128)(2,1)S(1)}, u32[]{:S(2)}) copy-start(bf16[1024,512]{1,0:T(8,128)(2,1)S(1)} %collective-permute-done.2.fc2_other_hbm) | copy-start | bytes 3145732
  93.5 2.7 %copy-start.2 = (bf16[16,128,256]{2,1,0:T(8,128)(2,1)}, bf16[16,128,256]{2,1,0:T(8,128)(2,1)S(1)}, u32[]{:S(2)}) copy-start(bf16[16,128,256]{2,1,0:T(8,128)(2,1)S(1)} %all_to_all.11) | copy-start | bytes 3145732
  93.5 2.7 %collective-permute-start.4 = (bf16[2048,256]{1,0:T(8,128)(2,1)S(1)}, bf16[2048,256]{1,0:T(8,128)(2,1)S(1)}, u32[]{:S(2)}, u32[]{:S(2)}) collective-permute-start(bf16[2048,256]{1,0:T(8,128)(2,1)S(1)} %bitcast.10), channel_id=1, source_target_pairs={{0,1},{1,0},{2,3},{3,2},{4,5},{5,4},{6,7},{7,6},{8,9},{9,8},{10,11... | collective-permute-start | bytes 3145736 | tf_op jit(solution)/shard_map/ppermute | solution.py:392
  96.2 1.0 copy-start.7
  109.2 2.9 %collective-permute-start.5 = (bf16[1024,512]{1,0:T(8,128)(2,1)}, bf16[1024,512]{1,0:T(8,128)(2,1)S(1)}, u32[]{:S(2)}, u32[]{:S(2)}) collective-permute-start(bf16[1024,512]{1,0:T(8,128)(2,1)} %get-tuple-element.16), channel_id=1, source_target_pairs={{0,1},{1,0},{2,3},{3,2},{4,5},{5,4},{6,7},{7,6},{8,9},{9,8},{10,11... | collective-permute-start | bytes 3145736 | tf_op jit(solution)/shard_map/ppermute | solution.py:392
